TPU v7x, 32 devices: a whole 2x2x4 slice. The times are simulated.
32 devices in a mesh: fsdp: 32 (over z, y, x, core).
Axes of the slice: x: 2, y: 2, z: 4, core: 2. Of those that a mesh axis runs over, the one named last changes fastest.
Arguments:
- block_input: bfloat16 [8192, 2048], P('fsdp'), may hold values from -6 to 6
- cotangent: bfloat16 [8192, 2048], P('fsdp'), may hold values from -6 to 6
- inward_weight: float32 [2048, 6144], P('fsdp'), may hold values from -0.125 to 0.125
- inward_first: float32 [2048, 6144], P('fsdp'), may hold values from -80 to 80
- inward_second: float32 [2048, 6144], P('fsdp'), may hold values from 729.088 to 2916.352
- outward_weight: float32 [2048, 2048], P('fsdp'), may hold values from -0.125 to 0.125
- outward_first: float32 [2048, 2048], P('fsdp'), may hold values from -80 to 80
- outward_second: float32 [2048, 2048], P('fsdp'), may hold values from 729.088 to 2916.352
- gate_weight: float32 [2048, 8192], P('fsdp'), may hold values from -0.125 to 0.125
- gate_first: float32 [2048, 8192], P('fsdp'), may hold values from -16 to 16
- gate_second: float32 [2048, 8192], P('fsdp'), may hold values from 38.5024 to 155.648
- up_weight: float32 [2048, 8192], P('fsdp'), may hold values from -0.125 to 0.125
- up_first: float32 [2048, 8192], P('fsdp'), may hold values from -16 to 16
- up_second: float32 [2048, 8192], P('fsdp'), may hold values from 38.5024 to 155.648
- down_weight: float32 [8192, 2048], P('fsdp'), may hold values from -0.0625 to 0.0625
- down_first: float32 [8192, 2048], P('fsdp'), may hold values from -32 to 32
- down_second: float32 [8192, 2048], P('fsdp'), may hold values from 155.648 to 622.592
- norm_gains: float32 [2, 2048], P(None, 'fsdp'), may hold values from 0.5 to 1.5
- gains_first: float32 [2, 2048], P(None, 'fsdp'), may hold values from -80 to 80
- gains_second: float32 [2, 2048], P(None, 'fsdp'), may hold values from 409.6 to 3276.8
- conv_taps: float32 [3, 2048], P(None, 'fsdp'), may hold values from -2.4 to 2.4
- taps_first: float32 [3, 2048], P(None, 'fsdp'), may hold values from -80 to 80
- taps_second: float32 [3, 2048], P(None, 'fsdp'), may hold values from 729.088 to 2916.352
Outputs:
- block_output: bfloat16 [8192, 2048], P('fsdp')
- input_grad: float32 [8192, 2048], P('fsdp')
- inward_momentum: float32 [2048, 6144], P('fsdp')
- inward_variance: float32 [2048, 6144], P('fsdp')
- inward_updated: float32 [2048, 6144], P('fsdp')
- outward_momentum: float32 [2048, 2048], P('fsdp')
- outward_variance: float32 [2048, 2048], P('fsdp')
- outward_updated: float32 [2048, 2048], P('fsdp')
- gate_momentum: float32 [2048, 8192], P('fsdp')
- gate_variance: float32 [2048, 8192], P('fsdp')
- gate_updated: float32 [2048, 8192], P('fsdp')
- up_momentum: float32 [2048, 8192], P('fsdp')
- up_variance: float32 [2048, 8192], P('fsdp')
- up_updated: float32 [2048, 8192], P('fsdp')
- down_momentum: float32 [8192, 2048], P('fsdp')
- down_variance: float32 [8192, 2048], P('fsdp')
- down_updated: float32 [8192, 2048], P('fsdp')
- gains_momentum: float32 [2, 2048], P(None, 'fsdp')
- gains_variance: float32 [2, 2048], P(None, 'fsdp')
- gains_updated: float32 [2, 2048], P(None, 'fsdp')
- taps_momentum: float32 [3, 2048], P(None, 'fsdp')
- taps_variance: float32 [3, 2048], P(None, 'fsdp')
- taps_updated: float32 [3, 2048], P(None, 'fsdp')
All inputs are finite; a program needn't handle non-finite values.
Results may differ from a plain program's by a relative error of at most 0.012.
The roundings to bfloat16 on the way count: a program that leaves them out, or rounds other values in their place, can miss the bound.
Values may be sent and summed in bfloat16 or wider, within the bound.
No kernel may reach another device: no remote copies, remote signals or barrier semaphores. Data moves between devices by JAX's collectives and lax.ppermute only.
A program may use at most 576 MiB of HBM per device.

v0:
```python
import jax
import jax.numpy as jnp
from jax import lax
from jax.sharding import PartitionSpec as P

D = 2048
SEQ_BASE = 8192
STEP = 10


EPS_NORM = 1e-05
BETA_ONE = 0.9
BETA_TWO = 0.95
ADAM_EPS = 1e-08
DECAY_RATE = 0.1
RATE_MATRIX = 0.01
RATE_VECTOR = 0.3


def shifted(block, axis, distance):
    devices = range(lax.axis_size(axis))
    route = [(i - distance, i) for i in devices if i - distance in devices]
    return lax.ppermute(block, axis, route)


def forward_dot(operand, partner):
    return jnp.dot(operand, partner, preferred_element_type=jnp.float32)


def over_tokens(operand, partner):
    return lax.dot_general(
        operand, partner, (((0,), (0,)), ((), ())), preferred_element_type=jnp.float32
    )


def against_rows(operand, partner):
    return lax.dot_general(
        operand, partner, (((1,), (1,)), ((), ())), preferred_element_type=jnp.float32
    )


def rms_parts(values):
    scale = lax.rsqrt(jnp.mean(values * values, axis=-1, keepdims=True) + EPS_NORM)
    return (scale, values * scale)


def norm_back(upstream, normal, scale, gain):
    scaled = upstream * gain
    return scale * (scaled - normal * jnp.mean(scaled * normal, axis=-1, keepdims=True))


def adamw(weight, first, second, grad, rate, decay):
    first_new = BETA_ONE * first + (1.0 - BETA_ONE) * grad
    second_new = BETA_TWO * second + (1.0 - BETA_TWO) * grad * grad
    fix_one = 1.0 - BETA_ONE**STEP
    fix_two = 1.0 - BETA_TWO**STEP
    stepped = first_new / fix_one / (jnp.sqrt(second_new / fix_two) + ADAM_EPS)
    return (first_new, second_new, weight - rate * (stepped + decay * weight))


def on_device(
    block_input,
    cotangent,
    inward_weight,
    inward_first,
    inward_second,
    outward_weight,
    outward_first,
    outward_second,
    gate_weight,
    gate_first,
    gate_second,
    up_weight,
    up_first,
    up_second,
    down_weight,
    down_first,
    down_second,
    norm_gains,
    gains_first,
    gains_second,
    conv_taps,
    taps_first,
    taps_second,
):
    tok_rows = block_input.shape[0]
    seq_len = min(SEQ_BASE, tok_rows * lax.axis_size("fsdp"))
    small_local = jnp.concatenate([norm_gains, conv_taps], axis=0).T.astype(jnp.bfloat16)
    inward_low = inward_weight.astype(jnp.bfloat16)
    outward_low = outward_weight.astype(jnp.bfloat16)
    inward_full, outward_full, small_full = (
        lax.all_gather(inward_low, "fsdp", axis=0, tiled=True),
        lax.all_gather(outward_low, "fsdp", axis=0, tiled=True),
        lax.all_gather(small_local, "fsdp", axis=0, tiled=True),
    )
    small_vals = small_full.astype(jnp.float32)
    gain_one = small_vals[:, 0]
    gain_two = small_vals[:, 1]
    tap_zero = small_vals[:, 2]
    tap_one = small_vals[:, 3]
    tap_two = small_vals[:, 4]
    inputs = block_input.astype(jnp.float32)
    scale_one, normal_one = rms_parts(inputs)
    normed_one = (normal_one * gain_one).astype(jnp.bfloat16)
    mixed = forward_dot(normed_one, inward_full)
    b_part = mixed[:, :D]
    c_part = mixed[:, D : 2 * D]
    x_part = mixed[:, 2 * D :]
    gated = b_part * x_part
    starts_here = lax.axis_index("fsdp") * tok_rows % seq_len == 0
    previous = shifted(gated[tok_rows - 2 :], "fsdp", 1)
    previous = jnp.where(starts_here, 0.0, previous)
    extended = jnp.concatenate([previous, gated], axis=0)
    convolved = (
        tap_zero * extended[:tok_rows]
        + tap_one * extended[1 : tok_rows + 1]
        + tap_two * extended[2:]
    )
    branch_in = (c_part * convolved).astype(jnp.bfloat16)
    middle = inputs + forward_dot(branch_in, outward_full)
    scale_two, normal_two = rms_parts(middle)
    normed_two = (normal_two * gain_two).astype(jnp.bfloat16)
    ffn_local = (
        gate_weight.astype(jnp.bfloat16),
        up_weight.astype(jnp.bfloat16),
        down_weight.astype(jnp.bfloat16),
    )
    gate_full, up_full, down_full = (
        lax.all_gather(ffn_local[0], "fsdp", axis=0, tiled=True),
        lax.all_gather(ffn_local[1], "fsdp", axis=0, tiled=True),
        lax.all_gather(ffn_local[2], "fsdp", axis=0, tiled=True),
    )
    gate_value = forward_dot(normed_two, gate_full)
    up_value = forward_dot(normed_two, up_full)
    sigmoid_gate = jax.nn.sigmoid(gate_value)
    silu_gate = gate_value * sigmoid_gate
    hidden = (silu_gate * up_value).astype(jnp.bfloat16)
    block_output = (middle + forward_dot(hidden, down_full)).astype(jnp.bfloat16)
    gate_back, up_back, down_back = (
        lax.all_gather(ffn_local[0], "fsdp", axis=0, tiled=True),
        lax.all_gather(ffn_local[1], "fsdp", axis=0, tiled=True),
        lax.all_gather(ffn_local[2], "fsdp", axis=0, tiled=True),
    )
    hidden_grad = against_rows(cotangent, down_back)
    down_term = over_tokens(hidden, cotangent)
    gate_grad = (
        hidden_grad * up_value * sigmoid_gate * (1.0 + gate_value * (1.0 - sigmoid_gate))
    ).astype(jnp.bfloat16)
    up_grad = (hidden_grad * silu_gate).astype(jnp.bfloat16)
    normed_two_grad = against_rows(gate_grad, gate_back) + against_rows(up_grad, up_back)
    gate_term = over_tokens(normed_two, gate_grad)
    up_term = over_tokens(normed_two, up_grad)
    gain_two_grad = jnp.sum(normed_two_grad * normal_two, axis=0)
    gate_sum, up_sum, down_sum = (
        lax.psum_scatter(gate_term, "fsdp", scatter_dimension=0, tiled=True),
        lax.psum_scatter(up_term, "fsdp", scatter_dimension=0, tiled=True),
        lax.psum_scatter(down_term, "fsdp", scatter_dimension=0, tiled=True),
    )
    middle_grad = cotangent.astype(jnp.float32) + norm_back(
        normed_two_grad, normal_two, scale_two, gain_two
    )
    branch_grad = middle_grad.astype(jnp.bfloat16)
    inward_back, outward_back = (
        lax.all_gather(inward_low, "fsdp", axis=0, tiled=True),
        lax.all_gather(outward_low, "fsdp", axis=0, tiled=True),
    )
    outward_term = over_tokens(branch_in, branch_grad)
    branch_in_grad = against_rows(branch_grad, outward_back)
    c_grad = branch_in_grad * convolved
    conv_grad = branch_in_grad * c_part
    ext_grad = (
        jnp.pad(tap_zero * conv_grad, ((0, 2), (0, 0)))
        + jnp.pad(tap_one * conv_grad, ((1, 1), (0, 0)))
        + jnp.pad(tap_two * conv_grad, ((2, 0), (0, 0)))
    )
    tap_grads = [
        jnp.sum(conv_grad * extended[offset : offset + tok_rows], axis=0) for offset in range(3)
    ]
    rim_grad = jnp.where(starts_here, 0.0, ext_grad[:2])
    returned = shifted(rim_grad, "fsdp", -1)
    gated_grad = ext_grad[2:] + jnp.pad(returned, ((tok_rows - 2, 0), (0, 0)))
    mixed_grad = jnp.concatenate([gated_grad * x_part, c_grad, gated_grad * b_part], axis=1).astype(
        jnp.bfloat16
    )
    inward_term = over_tokens(normed_one, mixed_grad)
    normed_one_grad = against_rows(mixed_grad, inward_back)
    gain_one_grad = jnp.sum(normed_one_grad * normal_one, axis=0)
    input_grad = middle_grad + norm_back(normed_one_grad, normal_one, scale_one, gain_one)
    small_term = jnp.stack([gain_one_grad, gain_two_grad] + tap_grads, axis=1)
    inward_sum, outward_sum, small_sum = (
        lax.psum_scatter(inward_term, "fsdp", scatter_dimension=0, tiled=True),
        lax.psum_scatter(outward_term, "fsdp", scatter_dimension=0, tiled=True),
        lax.psum_scatter(small_term, "fsdp", scatter_dimension=0, tiled=True),
    )
    gains_grad = small_sum[:, :2].T
    taps_grad = small_sum[:, 2:].T
    inward_new = adamw(
        inward_weight, inward_first, inward_second, inward_sum, RATE_MATRIX, DECAY_RATE
    )
    outward_new = adamw(
        outward_weight, outward_first, outward_second, outward_sum, RATE_MATRIX, DECAY_RATE
    )
    gate_new = adamw(gate_weight, gate_first, gate_second, gate_sum, RATE_MATRIX, DECAY_RATE)
    up_new = adamw(up_weight, up_first, up_second, up_sum, RATE_MATRIX, DECAY_RATE)
    down_new = adamw(down_weight, down_first, down_second, down_sum, RATE_MATRIX, DECAY_RATE)
    gains_new = adamw(norm_gains, gains_first, gains_second, gains_grad, RATE_VECTOR, 0.0)
    taps_new = adamw(conv_taps, taps_first, taps_second, taps_grad, RATE_VECTOR, 0.0)
    return (
        block_output,
        input_grad,
        inward_new[0],
        inward_new[1],
        inward_new[2],
        outward_new[0],
        outward_new[1],
        outward_new[2],
        gate_new[0],
        gate_new[1],
        gate_new[2],
        up_new[0],
        up_new[1],
        up_new[2],
        down_new[0],
        down_new[1],
        down_new[2],
        gains_new[0],
        gains_new[1],
        gains_new[2],
        taps_new[0],
        taps_new[1],
        taps_new[2],
    )


def solution(mesh):
    placed = (
        P("fsdp", None),
        P("fsdp", None),
        P("fsdp", None),
        P("fsdp", None),
        P("fsdp", None),
        P("fsdp", None),
        P("fsdp", None),
        P("fsdp", None),
        P("fsdp", None),
        P("fsdp", None),
        P("fsdp", None),
        P("fsdp", None),
        P("fsdp", None),
        P("fsdp", None),
        P("fsdp", None),
        P("fsdp", None),
        P("fsdp", None),
        P(None, "fsdp"),
        P(None, "fsdp"),
        P(None, "fsdp"),
        P(None, "fsdp"),
        P(None, "fsdp"),
        P(None, "fsdp"),
    )
    return jax.shard_map(
        on_device,
        mesh=mesh,
        in_specs=placed,
        out_specs=(
            P("fsdp", None),
            P("fsdp", None),
            P("fsdp", None),
            P("fsdp", None),
            P("fsdp", None),
            P("fsdp", None),
            P("fsdp", None),
            P("fsdp", None),
            P("fsdp", None),
            P("fsdp", None),
            P("fsdp", None),
            P("fsdp", None),
            P("fsdp", None),
            P("fsdp", None),
            P("fsdp", None),
            P("fsdp", None),
            P("fsdp", None),
            P(None, "fsdp"),
            P(None, "fsdp"),
            P(None, "fsdp"),
            P(None, "fsdp"),
            P(None, "fsdp"),
            P(None, "fsdp"),
        ),
        check_vma=False,
    )
```

profile of v0, /device:TPU:0, one launch (start us, length us, event | category | flops | bytes accessed | tf_op | source)
XLA Modules:
  0.0 3831.2 jit_solution(18185364832895738613)
XLA Ops:
  16.0 44.1 %all-gather = bf16[32,64,5]{1,2,0:T(8,128)(2,1)S(1)} all-gather(bf16[1,64,5]{1,2,0:T(8,128)(2,1)S(1)} %maximum_bitcast_fusion), channel_id=1, replica_groups=mesh['fsdp'=32] {'fsdp'}, dimensions={0}, use_global_device_ids=true | all-gather | bytes 21120 | tf_op jit(solution)/shard_map/all_gather | solution.py:94
  60.6 108.5 %all-gather.7.cloned.1.call-done = bf16[2048,6144]{1,0:T(8,128)(2,1)} async-done(((bf16[64,6144]{1,0:T(8,128)(2,1)}), bf16[2048,6144]{1,0:T(8,128)(2,1)}) %all-gather.7.cloned.1.call-update) | async-done | bytes 25165840 | tf_op jit(solution)/shard_map/all_gather | solution.py:92
  169.1 11.7 fusion.26
  186.4 4.0 multiply_convert_fusion.7
  190.4 57.7 %all-gather.9.cloned.1.call-done = bf16[2048,2048]{1,0:T(8,128)(2,1)} async-done(((bf16[64,2048]{1,0:T(8,128)(2,1)}), bf16[2048,2048]{1,0:T(8,128)(2,1)}) %all-gather.9.cloned.1.call-update) | async-done | bytes 8388624 | tf_op jit(solution)/shard_map/all_gather | solution.py:93
  248.1 6.2 multiply_reduce_fusion.5
  255.9 189.1 %all-gather.13.cloned.1.call-done = bf16[2048,8192]{1,0:T(8,128)(2,1)} async-done(((bf16[64,8192]{1,0:T(8,128)(2,1)}), bf16[2048,8192]{1,0:T(8,128)(2,1)}) %all-gather.13.cloned.1.call-update) | async-done | bytes 33554448 | tf_op jit(solution)/shard_map/all_gather | solution.py:130
  445.0 17.9 fusion.45
  462.9 178.4 %all-gather.11.cloned.1.call-done = bf16[2048,8192]{1,0:T(8,128)(2,1)} async-done(((bf16[64,8192]{1,0:T(8,128)(2,1)}), bf16[2048,8192]{1,0:T(8,128)(2,1)}) %all-gather.11.cloned.1.call-update) | async-done | bytes 33554448 | tf_op jit(solution)/shard_map/all_gather | solution.py:129
  641.3 17.7 fusion.44
  658.9 178.6 %all-gather.15.cloned.1.call-done = bf16[8192,2048]{1,0:T(8,128)(2,1)} async-done(((bf16[256,2048]{1,0:T(8,128)(2,1)}), bf16[8192,2048]{1,0:T(8,128)(2,1)}) %all-gather.15.cloned.1.call-update) | async-done | bytes 33554448 | tf_op jit(solution)/shard_map/all_gather | solution.py:131
  837.5 23.9 multiply_convert_fusion
  861.4 17.3 fusion.46
  878.6 18.8 multiply_reduce_fusion.3
  900.4 6.5 fusion.23
  913.2 14.8 fusion.12
  930.0 9.4 fusion.21
  940.9 20.8 fusion.18
  962.9 25.4 fusion.49
  989.5 25.6 fusion.48
  1015.2 25.4 fusion.47
  1042.2 17.5 fusion.5
  1061.8 4.5 reduce-scatter.19.cloned.1.call-done
  1069.2 178.1 %reduce-scatter.11.cloned.1.call-done = f32[64,2048]{1,0:T(8,128)} async-done(((f32[2048,2048]{1,0:T(8,128)}), f32[64,2048]{1,0:T(8,128)}) %reduce-scatter.11.cloned.1.call-update) | async-done | bytes 524304 | tf_op jit(solution)/shard_map/reduce_scatter | solution.py:192
  1249.8 438.5 %reduce-scatter.9.cloned.1.call-done = f32[64,6144]{1,0:T(8,128)} async-done(((f32[2048,6144]{1,0:T(8,128)}), f32[64,6144]{1,0:T(8,128)}) %reduce-scatter.9.cloned.1.call-update) | async-done | bytes 1572880 | tf_op jit(solution)/shard_map/reduce_scatter | solution.py:191
  1688.3 5.8 multiply_subtract_fusion.3
  1694.1 698.3 %reduce-scatter.17.cloned.1.call-done = f32[256,2048]{1,0:T(8,128)} async-done(((f32[8192,2048]{1,0:T(8,128)}), f32[256,2048]{1,0:T(8,128)}) %reduce-scatter.17.cloned.1.call-update) | async-done | bytes 2097168 | tf_op jit(solution)/shard_map/reduce_scatter | solution.py:157
  2392.3 6.9 multiply_subtract_fusion
  2399.2 705.7 %reduce-scatter.15.cloned.1.call-done = f32[64,8192]{1,0:T(8,128)} async-done(((f32[2048,8192]{1,0:T(8,128)}), f32[64,8192]{1,0:T(8,128)}) %reduce-scatter.15.cloned.1.call-update) | async-done | bytes 2097168 | tf_op jit(solution)/shard_map/reduce_scatter | solution.py:156
  3104.9 7.2 multiply_subtract_fusion.1
  3112.1 705.6 %reduce-scatter.13.cloned.1.call-done = f32[64,8192]{1,0:T(8,128)} async-done(((f32[2048,8192]{1,0:T(8,128)}), f32[64,8192]{1,0:T(8,128)}) %reduce-scatter.13.cloned.1.call-update) | async-done | bytes 2097168 | tf_op jit(solution)/shard_map/reduce_scatter | solution.py:155
  3817.7 6.6 multiply_subtract_fusion.2
  (148 shorter events, 40.3 us)
Async XLA Ops:
  7.2 161.8 %all-gather.7.cloned.1.call-start = ((), (), s32[]{:S(2)}) async-start(), calls=%async_computation.6 | async-start | bytes 25952256 | tf_op jit(solution)/shard_map/all_gather | solution.py:92
  9.8 238.3 %all-gather.9.cloned.1.call-start = ((), (), s32[]{:S(2)}) async-start(), calls=%async_computation.7 | async-start | bytes 8650752 | tf_op jit(solution)/shard_map/all_gather | solution.py:93
  10.6 434.4 %all-gather.13.cloned.1.call-start = ((), (), s32[]{:S(2)}) async-start(), calls=%async_computation.9 | async-start | bytes 34603008 | tf_op jit(solution)/shard_map/all_gather | solution.py:130
  11.8 629.5 %all-gather.11.cloned.1.call-start = ((), (), s32[]{:S(2)}) async-start(), calls=%async_computation.8 | async-start | bytes 34603008 | tf_op jit(solution)/shard_map/all_gather | solution.py:129
  14.7 45.5 %copy-start.6 = (bf16[256,2048]{1,0:T(8,128)(2,1)S(1)}, bf16[256,2048]{1,0:T(8,128)(2,1)}, u32[]{:S(2)}) copy-start(bf16[256,2048]{1,0:T(8,128)(2,1)} %param.23) | copy-start | bytes 3145732
  14.7 822.8 %all-gather.15.cloned.1.call-start = ((), (), s32[]{:S(2)}) async-start(), calls=%async_computation.10 | async-start | bytes 34603008 | tf_op jit(solution)/shard_map/all_gather | solution.py:131
  15.9 1050.3 %reduce-scatter.19.cloned.1.call-start = ((), (), s32[]{:S(2)}) async-start(), calls=%async_computation.16 | async-start | bytes 1081344
  60.5 878.9 %copy-start.30 = (f32[256]{0:T(256)}, f32[256]{0:T(256)S(1)}, u32[]{:S(2)}) copy-start(f32[256]{0:T(256)S(1)} %add_rsqrt_fusion.1) | copy-start | bytes 3076
  60.6 878.9 %copy-start.26 = (f32[2048,1]{0,1:T(1,128)}, f32[2048,1]{0,1:T(1,128)S(1)}, u32[]{:S(2)}) copy-start(f32[2048,1]{0,1:T(1,128)S(1)} %get-tuple-element.67) | copy-start | bytes 24580
  183.4 3.0 collective-permute-start
  255.9 385.4 %copy-start.4 = (bf16[256,2048]{1,0:T(8,128)(2,1)}, bf16[256,2048]{1,0:T(8,128)(2,1)S(1)}, u32[]{:S(2)}) copy-start(bf16[256,2048]{1,0:T(8,128)(2,1)S(1)} %multiply_convert_fusion.6) | copy-start | bytes 3145732
  878.6 18.8 copy-start.16
  897.4 9.6 slice-start
  909.4 3.1 collective-permute-start.1
  913.2 14.8 copy-start.20
  913.2 14.8 copy-start.22
  929.5 317.9 %reduce-scatter.11.cloned.1.call-start = ((), (), s32[]{:S(2)}) async-start(), calls=%async_computation.12 | async-start | bytes 17301504 | tf_op jit(solution)/shard_map/reduce_scatter | solution.py:192
  939.4 748.9 %reduce-scatter.9.cloned.1.call-start = ((), (), s32[]{:S(2)}) async-start(), calls=%async_computation.11 | async-start | bytes 51904512 | tf_op jit(solution)/shard_map/reduce_scatter | solution.py:191
  961.7 1430.6 %reduce-scatter.17.cloned.1.call-start = ((), (), s32[]{:S(2)}) async-start(), calls=%async_computation.15 | async-start | bytes 69206016 | tf_op jit(solution)/shard_map/reduce_scatter | solution.py:157
  988.3 2116.6 %reduce-scatter.15.cloned.1.call-start = ((), (), s32[]{:S(2)}) async-start(), calls=%async_computation.14 | async-start | bytes 69206016 | tf_op jit(solution)/shard_map/reduce_scatter | solution.py:156
  1015.1 2802.5 %reduce-scatter.13.cloned.1.call-start = ((), (), s32[]{:S(2)}) async-start(), calls=%async_computation.13 | async-start | bytes 69206016 | tf_op jit(solution)/shard_map/reduce_scatter | solution.py:155
  1042.2 17.5 copy-start.40
  1042.2 17.6 copy-start.3
  1042.2 17.6 copy-start.8
  1042.2 17.6 copy-start.23
  1042.2 17.6 copy-start.27
  1042.2 17.6 copy-start.31
  1059.9 187.5 %copy-start.25 = (f32[64,2048]{1,0:T(8,128)S(1)}, f32[64,2048]{1,0:T(8,128)}, u32[]{:S(2)}) copy-start(f32[64,2048]{1,0:T(8,128)} %param.28) | copy-start | bytes 1572868
  1059.9 187.5 %copy-start.28 = (f32[64,2048]{1,0:T(8,128)S(1)}, f32[64,2048]{1,0:T(8,128)}, u32[]{:S(2)}) copy-start(f32[64,2048]{1,0:T(8,128)} %param.30) | copy-start | bytes 1572868
  1059.9 187.5 %copy-start.29 = (f32[64,2048]{1,0:T(8,128)S(1)}, f32[64,2048]{1,0:T(8,128)}, u32[]{:S(2)}) copy-start(f32[64,2048]{1,0:T(8,128)} %param.29) | copy-start | bytes 1572868
  1249.8 1142.6 %copy-start.10 = (f32[256,2048]{1,0:T(8,128)S(1)}, f32[256,2048]{1,0:T(8,128)}, u32[]{:S(2)}) copy-start(f32[256,2048]{1,0:T(8,128)} %param.37) | copy-start | bytes 6291460
  2399.2 1418.5 %copy-start.12 = (f32[64,8192]{1,0:T(8,128)S(1)}, f32[64,8192]{1,0:T(8,128)}, u32[]{:S(2)}) copy-start(f32[64,8192]{1,0:T(8,128)} %param.31) | copy-start | bytes 6291460
  (24 other events, 101.7 us)
Sparse Core Ops, SparseCore 0:
  11.5 157.5 all-gather.6
  172.5 75.6 all-gather.8
  251.6 193.3 all-gather.12
  448.3 192.9 all-gather.10
  644.5 192.9 all-gather.14
  929.6 136.6 reduce-scatter.18
  1068.7 178.6 reduce-scatter.10
  1254.9 433.3 reduce-scatter.8
  1690.8 701.5 reduce-scatter.16
  2394.7 710.2 reduce-scatter.14
  3107.4 710.2 reduce-scatter.12
where the time goes:
time: 3840 us; the launch traced here: 3830 us
  waiting for transfers between devices  3440 us (90%)
  matrix products  259 us (7%)
  other arithmetic  51.9 us (1%)
  blocking collectives  44.1 us (1%)
    reduce_scatter x1, waiting for transfers between devices, on_device(): lax.psum_scatter(up_term, 'fsdp', scatter_dimension=0, tiled=True)  706 us
    reduce_scatter x1, waiting for transfers between devices, on_device(): lax.psum_scatter(gate_term, 'fsdp', scatter_dimension=0, tiled=True)  706 us
    reduce_scatter x1, waiting for transfers between devices, on_device(): lax.psum_scatter(down_term, 'fsdp', scatter_dimension=0, tiled=True)  698 us
    reduce_scatter x1, waiting for transfers between devices, on_device(): lax.psum_scatter(inward_term, 'fsdp', scatter_dimension=0, tiled=True)  439 us
    all_gather x1, waiting for transfers between devices, on_device(): lax.all_gather(ffn_local[1], 'fsdp', axis=0, tiled=True)  189 us
    all_gather x1, waiting for transfers between devices, on_device(): lax.all_gather(ffn_local[2], 'fsdp', axis=0, tiled=True)  179 us
    all_gather x1, waiting for transfers between devices, on_device(): lax.all_gather(ffn_local[0], 'fsdp', axis=0, tiled=True)  178 us
    reduce_scatter x1, waiting for transfers between devices, on_device(): lax.psum_scatter(outward_term, 'fsdp', scatter_dimension=0, tiled=True)  178 us
  transfers between devices with their start and end apart: 13, of which 13 were waited for; matrix products, arithmetic and copies ran while one was open for 6% of the time, Pallas kernels for 0%

commit v1 on v0

v1 whole, which is shorter than its diff:
```python
import jax
import jax.numpy as jnp
from jax import lax
from jax.sharding import Mesh
from jax.sharding import PartitionSpec as P

SEQ_BASE = 8192
STEP = 10

EPS_NORM = 1e-05
BETA_ONE = 0.9
BETA_TWO = 0.95
ADAM_EPS = 1e-08
DECAY_RATE = 0.1
RATE_MATRIX = 0.01
RATE_VECTOR = 0.3

AXES = ("p", "y", "x", "c")
PLANE = ("y", "x", "c")
COLUMN = ("p", "c")
CROSS = ("y", "x")
LOW = jnp.bfloat16


def forward_dot(operand, partner):
    return jnp.dot(operand, partner, preferred_element_type=jnp.float32)


def over_tokens(operand, partner):
    return lax.dot_general(
        operand, partner, (((0,), (0,)), ((), ())), preferred_element_type=jnp.float32
    )


def against_rows(operand, partner):
    return lax.dot_general(
        operand, partner, (((1,), (1,)), ((), ())), preferred_element_type=jnp.float32
    )


def rms_parts(values):
    scale = lax.rsqrt(jnp.mean(values * values, axis=-1, keepdims=True) + EPS_NORM)
    return (scale, values * scale)


def norm_back(upstream, normal, scale, gain):
    scaled = upstream * gain
    return scale * (scaled - normal * jnp.mean(scaled * normal, axis=-1, keepdims=True))


def adamw(weight, first, second, grad, rate, decay):
    first_new = BETA_ONE * first + (1.0 - BETA_ONE) * grad
    second_new = BETA_TWO * second + (1.0 - BETA_TWO) * grad * grad
    fix_one = 1.0 - BETA_ONE**STEP
    fix_two = 1.0 - BETA_TWO**STEP
    stepped = first_new / fix_one / (jnp.sqrt(second_new / fix_two) + ADAM_EPS)
    return (first_new, second_new, weight - rate * (stepped + decay * weight))


def gather(block, axes):
    return lax.all_gather(block, axes, axis=0, tiled=True)


def scatter(term, axes):
    return lax.psum_scatter(term, axes, scatter_dimension=0, tiled=True)


def exchange(blocks, axes):
    return lax.all_to_all(blocks, axes, split_axis=0, concat_axis=0, tiled=True)


def along_planes(block, distance):
    count = lax.axis_size("p")
    route = [(i - distance, i) for i in range(count) if 0 <= i - distance < count]
    return lax.ppermute(block, "p", route)


def on_device(
    block_input,
    cotangent,
    inward_weight,
    inward_first,
    inward_second,
    outward_weight,
    outward_first,
    outward_second,
    gate_weight,
    gate_first,
    gate_second,
    up_weight,
    up_first,
    up_second,
    down_weight,
    down_first,
    down_second,
    norm_gains,
    gains_first,
    gains_second,
    conv_taps,
    taps_first,
    taps_second,
):
    planes = lax.axis_size("p")
    tok_rows, d = block_input.shape
    d_rows = inward_weight.shape[0]
    ff = gate_weight.shape[1]
    ff_rows = down_weight.shape[0]
    plane_rows = 8 * tok_rows
    seq_len = min(SEQ_BASE, plane_rows * planes)
    feats = d // 8
    plane = lax.axis_index("p")
    place = lax.axis_index(PLANE)

    small_local = jnp.concatenate([norm_gains, conv_taps], axis=0).T.astype(LOW)
    small_full = gather(small_local, AXES).astype(jnp.float32)
    gain_one = small_full[:, 0]
    gain_two = small_full[:, 1]
    taps_here = lax.dynamic_index_in_dim(
        small_full.reshape(planes, 8, d_rows, 5), place, axis=1, keepdims=False
    ).reshape(feats, 5)
    tap_zero = taps_here[:, 2]
    tap_one = taps_here[:, 3]
    tap_two = taps_here[:, 4]

    inward_low = inward_weight.astype(LOW)
    inward_sent = inward_low.reshape(d_rows, 3, planes, 8, d_rows).transpose(3, 0, 1, 2, 4)
    inward_part = gather(exchange(inward_sent.reshape(8, d_rows, 3 * feats), PLANE), "p")
    inward_part = inward_part.reshape(d, 3 * feats)
    outward_full = gather(gather(outward_weight.astype(LOW), "p"), PLANE)

    gate_low = gate_weight.astype(LOW)
    up_low = up_weight.astype(LOW)

    def ffn_part(low):
        sent = low.reshape(d_rows, planes, 4, 2, ff_rows).transpose(1, 3, 0, 2, 4)
        got = exchange(sent.reshape(2 * planes, d_rows, 4 * ff_rows), COLUMN)
        whole = gather(got[None], CROSS)
        whole = whole.reshape(4, planes, 2, d_rows, 4 * ff_rows).transpose(1, 0, 2, 3, 4)
        return whole.reshape(d, 4 * ff_rows)

    gate_part = ffn_part(gate_low)
    up_part = ffn_part(up_low)
    down_part = gather(down_weight.astype(LOW), CROSS)

    inputs = block_input.astype(jnp.float32)
    scale_one, normal_one = rms_parts(inputs)
    normed_one = gather((normal_one * gain_one).astype(LOW), PLANE)
    mixed = forward_dot(normed_one, inward_part)
    b_part = mixed[:, :feats]
    c_part = mixed[:, feats : 2 * feats]
    x_part = mixed[:, 2 * feats :]
    gated = b_part * x_part
    starts_here = plane * plane_rows % seq_len == 0
    previous = jnp.where(starts_here, 0.0, along_planes(gated[plane_rows - 2 :], 1))
    extended = jnp.concatenate([previous, gated], axis=0)
    convolved = (
        tap_zero * extended[:plane_rows]
        + tap_one * extended[1 : plane_rows + 1]
        + tap_two * extended[2:]
    )
    branch_feats = (c_part * convolved).astype(LOW)
    branch_in = exchange(branch_feats.reshape(8, tok_rows, feats), PLANE)
    branch_in = branch_in.transpose(1, 0, 2).reshape(tok_rows, d)
    middle = inputs + forward_dot(branch_in, outward_full)
    scale_two, normal_two = rms_parts(middle)

    normed_two = gather((normal_two * gain_two).astype(LOW), COLUMN)
    upstream = gather(cotangent, COLUMN)
    gate_value = forward_dot(normed_two, gate_part)
    up_value = forward_dot(normed_two, up_part)
    sigmoid_gate = jax.nn.sigmoid(gate_value)
    silu_gate = gate_value * sigmoid_gate
    hidden = (silu_gate * up_value).astype(LOW)
    hidden_grad = against_rows(upstream, down_part)
    gate_grad = (
        hidden_grad * up_value * sigmoid_gate * (1.0 + gate_value * (1.0 - sigmoid_gate))
    ).astype(LOW)
    up_grad = (hidden_grad * silu_gate).astype(LOW)
    normed_two_grad = against_rows(gate_grad, gate_part) + against_rows(up_grad, up_part)
    normed_two_grad = scatter(normed_two_grad.astype(LOW), COLUMN).astype(jnp.float32)
    result = scatter(forward_dot(hidden, down_part).astype(LOW), COLUMN)
    block_output = (middle + result.astype(jnp.float32)).astype(LOW)

    down_sum = scatter(over_tokens(hidden, upstream).astype(LOW), CROSS).astype(jnp.float32)

    def ffn_sum(grad):
        term = over_tokens(normed_two, grad).astype(LOW)
        term = term.reshape(planes, 4, 2, d_rows, 4 * ff_rows).transpose(1, 0, 2, 3, 4)
        own = scatter(term, CROSS).reshape(2 * planes, d_rows, 4 * ff_rows)
        own = exchange(own, COLUMN).reshape(planes, 2, d_rows, 4, ff_rows)
        return own.transpose(2, 0, 3, 1, 4).reshape(d_rows, ff).astype(jnp.float32)

    gate_sum = ffn_sum(gate_grad)
    up_sum = ffn_sum(up_grad)

    middle_grad = cotangent.astype(jnp.float32) + norm_back(
        normed_two_grad, normal_two, scale_two, gain_two
    )
    branch_grad = middle_grad.astype(LOW)
    outward_sum = scatter(
        scatter(over_tokens(branch_in, branch_grad).astype(LOW), PLANE), "p"
    ).astype(jnp.float32)
    branch_in_grad = against_rows(branch_grad, outward_full).astype(LOW)
    branch_in_grad = branch_in_grad.reshape(tok_rows, 8, feats).transpose(1, 0, 2)
    branch_in_grad = exchange(branch_in_grad, PLANE).reshape(plane_rows, feats)
    branch_in_grad = branch_in_grad.astype(jnp.float32)
    c_grad = branch_in_grad * convolved
    conv_grad = branch_in_grad * c_part
    ext_grad = (
        jnp.pad(tap_zero * conv_grad, ((0, 2), (0, 0)))
        + jnp.pad(tap_one * conv_grad, ((1, 1), (0, 0)))
        + jnp.pad(tap_two * conv_grad, ((2, 0), (0, 0)))
    )
    tap_grads = jnp.stack(
        [
            jnp.sum(conv_grad * extended[offset : offset + plane_rows], axis=0)
            for offset in range(3)
        ],
        axis=1,
    )
    returned = along_planes(jnp.where(starts_here, 0.0, ext_grad[:2]), -1)
    gated_grad = ext_grad[2:] + jnp.pad(returned, ((plane_rows - 2, 0), (0, 0)))
    mixed_grad = jnp.concatenate([gated_grad * x_part, c_grad, gated_grad * b_part], axis=1)
    mixed_grad = mixed_grad.astype(LOW)
    normed_one_grad = against_rows(mixed_grad, inward_part)
    normed_one_grad = scatter(normed_one_grad.astype(LOW), PLANE).astype(jnp.float32)
    input_grad = middle_grad + norm_back(normed_one_grad, normal_one, scale_one, gain_one)

    inward_term = over_tokens(normed_one, mixed_grad).astype(LOW)
    inward_own = scatter(inward_term, "p").reshape(8, d_rows, 3 * feats)
    inward_own = exchange(inward_own, PLANE).reshape(8, d_rows, 3, planes, d_rows)
    inward_sum = inward_own.transpose(1, 2, 3, 0, 4).reshape(d_rows, 3 * d).astype(jnp.float32)

    own_gains = norm_gains.astype(LOW).astype(jnp.float32)
    gain_one_grad = jnp.sum(inward_low.astype(jnp.float32) * inward_sum, axis=1) / own_gains[0]
    gain_two_grad = (
        jnp.sum(gate_low.astype(jnp.float32) * gate_sum, axis=1)
        + jnp.sum(up_low.astype(jnp.float32) * up_sum, axis=1)
    ) / own_gains[1]
    gains_grad = jnp.stack([gain_one_grad, gain_two_grad])
    taps_grad = scatter(tap_grads, "p").T

    inward_new = adamw(
        inward_weight, inward_first, inward_second, inward_sum, RATE_MATRIX, DECAY_RATE
    )
    outward_new = adamw(
        outward_weight, outward_first, outward_second, outward_sum, RATE_MATRIX, DECAY_RATE
    )
    gate_new = adamw(gate_weight, gate_first, gate_second, gate_sum, RATE_MATRIX, DECAY_RATE)
    up_new = adamw(up_weight, up_first, up_second, up_sum, RATE_MATRIX, DECAY_RATE)
    down_new = adamw(down_weight, down_first, down_second, down_sum, RATE_MATRIX, DECAY_RATE)
    gains_new = adamw(norm_gains, gains_first, gains_second, gains_grad, RATE_VECTOR, 0.0)
    taps_new = adamw(conv_taps, taps_first, taps_second, taps_grad, RATE_VECTOR, 0.0)
    return (
        block_output,
        input_grad,
        *inward_new,
        *outward_new,
        *gate_new,
        *up_new,
        *down_new,
        *gains_new,
        *taps_new,
    )


def solution(mesh):
    devices = mesh.devices.reshape(-1, 2, 2, 2)
    rows = P(AXES, None)
    columns = P(None, AXES)
    return jax.shard_map(
        on_device,
        mesh=Mesh(devices, AXES),
        in_specs=(rows,) * 17 + (columns,) * 6,
        out_specs=(rows,) * 17 + (columns,) * 6,
        check_vma=False,
    )
```

time: 3840 us -> 1330 us (0.35)
  waiting for transfers between devices: 3440 us -> 811 us
  blocking collectives: 44.1 us -> 162 us
  matrix products: 259 us -> 183 us
  local copies, waits for them, and re-layouts: 12.9 us -> 74.5 us
    reduce_scatter x5 -> x7, waiting for transfers between devices: 2730 us -> 324 us  [scatter(): return lax.psum_scatter(term, axes, scatter_dimension=0, tiled=True)]
    all_gather x5 -> x9, waiting for transfers between devices: 712 us -> 319 us  [gather(): return lax.all_gather(block, axes, axis=0, tiled=True)]
    all_to_all x0 -> x4, blocking collectives: none -> 121 us  [exchange(): return lax.all_to_all(blocks, axes, split_axis=0, concat_axis=0, tiled=True)]
    unnamed x12 -> x20, waiting for transfers between devices: 4.63 us -> 112 us
    dot_general x5, matrix products: 107 us -> 56.2 us  [over_tokens(): lax.dot_general(operand, partner, (((0,), (0,)), ((), ())), preferred_ele...]
    all_to_all x0 -> x4, waiting for transfers between devices: none -> 50 us  [exchange(): return lax.all_to_all(blocks, axes, split_axis=0, concat_axis=0, tiled=True)]
  transfers between devices with their start and end apart: 13 -> 24, of which waited for: 13 -> 20; matrix products, arithmetic and copies ran while one was open for 6% -> 19% of each run, Pallas kernels for 0% -> 0%
where the time goes in v1:
time: 1330 us
  waiting for transfers between devices  811 us (61%)
  matrix products  183 us (14%)
  blocking collectives  162 us (12%)
  local copies, waits for them, and re-layouts  74.5 us (6%)
  other arithmetic  57.8 us (4%)
  starting transfers between devices  22.2 us (2%)
  between operations  15.3 us (1%)
    reduce_scatter x7, waiting for transfers between devices, scatter(): return lax.psum_scatter(term, axes, scatter_dimension=0, tiled=True)  324 us
    all_gather x9, waiting for transfers between devices, gather(): return lax.all_gather(block, axes, axis=0, tiled=True)  319 us
    all_to_all x4, blocking collectives, exchange(): return lax.all_to_all(blocks, axes, split_axis=0, concat_axis=0, tiled=True)  121 us
    unnamed x20, waiting for transfers between devices  112 us
    dot_general x5, matrix products, against_rows(): lax.dot_general(operand, partner, (((1,), (1,)), ((), ())), preferred_ele...  71.4 us
    dot_general x5, matrix products, over_tokens(): lax.dot_general(operand, partner, (((0,), (0,)), ((), ())), preferred_ele...  56.2 us
    dot_general x5, matrix products, forward_dot(): return jnp.dot(operand, partner, preferred_element_type=jnp.float32)  55.3 us
    all_to_all x4, waiting for transfers between devices, exchange(): return lax.all_to_all(blocks, axes, split_axis=0, concat_axis=0, tiled=True)  50 us
  transfers between devices with their start and end apart: 24, of which 20 were waited for; matrix products, arithmetic and copies ran while one was open for 19% of the time, Pallas kernels for 0%

profile of v1, /device:TPU:0, one launch (start us, length us, event | category | flops | bytes accessed | tf_op | source)
XLA Modules:
  0.0 1325.5 jit_solution(956689595121001530)
XLA Ops:
  14.6 17.8 %all_to_all.40 = bf16[8,64,768]{2,1,0:T(8,128)(2,1)} all-to-all(bf16[8,64,768]{2,1,0:T(8,128)(2,1)} %reshape.174), channel_id=1, replica_groups=mesh['p'=4,'y'=2,'x'=2,'c'=2] {'y','x','c'}, dimensions={0} | all-to-all | bytes 1572864 | tf_op jit(solution)/shard_map/all_to_all | solution.py:69
  33.1 41.2 %all-gather.2 = bf16[32,64,5]{1,2,0:T(8,128)(2,1)S(1)} all-gather(bf16[1,64,5]{1,2,0:T(8,128)(2,1)S(1)} %maximum_bitcast_fusion), channel_id=1, replica_groups=mesh['p'=4,'y'=2,'x'=2,'c'=2] {'p','y','x','c'}, dimensions={0}, use_global_device_ids=true | all-gather | bytes 21120 | tf_op jit(solution)/shard_map/all_gather | solution.py:61
  82.1 45.5 %all_to_all.41 = bf16[8,64,1024]{2,1,0:T(8,128)(2,1)} all-to-all(bf16[8,64,1024]{2,1,0:T(8,128)(2,1)} %reshape.181), channel_id=1, replica_groups=mesh['p'=4,'y'=2,'x'=2,'c'=2] {'p','c'}, dimensions={0} | all-to-all | bytes 2097152 | tf_op jit(solution)/shard_map/all_to_all | solution.py:69
  136.3 26.3 %all-to-all-done.3 = bf16[8,64,1024]{2,1,0:T(8,128)(2,1)S(1)} async-done(((bf16[8,64,1024]{2,1,0:T(8,128)(2,1)}), bf16[8,64,1024]{2,1,0:T(8,128)(2,1)S(1)}, u32[]{:S(2)}, u32[]{:S(2)}) %all-to-all-start.3) | async-done | bytes 1048608 | tf_op jit(solution)/shard_map/all_to_all | solution.py:69
  163.7 18.9 %all-gather.13.cloned.1.call-done = bf16[2048,2048]{1,0:T(8,128)(2,1)} async-done(((bf16[256,2048]{1,0:T(8,128)(2,1)}), bf16[2048,2048]{1,0:T(8,128)(2,1)}) %all-gather.13.cloned.1.call-update) | async-done | bytes 8388624 | tf_op jit(solution)/shard_map/all_gather | solution.py:61
  205.5 27.4 %all_to_all.42 = bf16[8,256,256]{1,2,0:T(8,128)(2,1)S(1)} all-to-all(bf16[8,256,256]{1,2,0:T(8,128)(2,1)S(1)} %copy.83), channel_id=1, replica_groups=mesh['p'=4,'y'=2,'x'=2,'c'=2] {'y','x','c'}, dimensions={0} | all-to-all | bytes 2097152 | tf_op jit(solution)/shard_map/all_to_all | solution.py:69
  232.9 14.5 %all-gather.19.cloned.1.call-done = bf16[2048,2048]{1,0:T(8,128)(2,1)} async-done(((bf16[256,2048]{1,0:T(8,128)(2,1)}), bf16[2048,2048]{1,0:T(8,128)(2,1)}) %all-gather.19.cloned.1.call-update) | async-done | bytes 8388624 | tf_op jit(solution)/shard_map/all_gather | solution.py:61
  258.6 44.1 %all-gather.27.cloned.1.call-done = bf16[32,64,1024]{2,1,0:T(8,128)(2,1)} async-done(((bf16[8,64,1024]{2,1,0:T(8,128)(2,1)}), bf16[32,64,1024]{2,1,0:T(8,128)(2,1)}) %all-gather.27.cloned.1.call-update) | async-done | bytes 4194320 | tf_op jit(solution)/shard_map/all_gather | solution.py:61
  307.7 50.0 %all-gather.29.cloned.1.call-done = bf16[32,64,1024]{2,1,0:T(8,128)(2,1)} async-done(((bf16[8,64,1024]{2,1,0:T(8,128)(2,1)}), bf16[32,64,1024]{2,1,0:T(8,128)(2,1)}) %all-gather.29.cloned.1.call-update) | async-done | bytes 4194320 | tf_op jit(solution)/shard_map/all_gather | solution.py:61
  362.6 79.4 %all-gather.21.cloned.1.call-done = bf16[2048,2048]{1,0:T(8,128)(2,1)} async-done(((bf16[256,2048]{1,0:T(8,128)(2,1)}), bf16[2048,2048]{1,0:T(8,128)(2,1)}) %all-gather.21.cloned.1.call-update) | async-done | bytes 8388624 | tf_op jit(solution)/shard_map/all_gather | solution.py:61
  442.0 14.6 %fusion.41 = f32[2048,1024]{1,0:T(8,128)} fusion(bf16[2048,2048]{1,0:T(8,128)(2,1)} %all-gather.21.cloned.1.call-done, bf16[2048,1024]{1,0:T(8,128)(2,1)} %bitcast.135), kind=kOutput, calls=%fused_computation.116 | convolution fusion | flops 8589934592 | bytes 20971520 | tf_op jit(solution)/shard_map/dot_general | solution.py:26
  467.5 28.1 %all-gather.23.cloned.1.call-done = bf16[1024,2048]{1,0:T(8,128)(2,1)} async-done(((bf16[256,2048]{1,0:T(8,128)(2,1)}), bf16[1024,2048]{1,0:T(8,128)(2,1)}) %all-gather.23.cloned.1.call-update) | async-done | bytes 4194320 | tf_op jit(solution)/shard_map/all_gather | solution.py:61
  495.6 83.7 %all-gather.25.cloned.1.call-done = bf16[2048,2048]{1,0:T(8,128)(2,1)} async-done(((bf16[256,2048]{1,0:T(8,128)(2,1)}), bf16[2048,2048]{1,0:T(8,128)(2,1)}) %all-gather.25.cloned.1.call-update) | async-done | bytes 8388624 | tf_op jit(solution)/shard_map/all_gather | solution.py:61
  579.3 23.8 %multiply_convert_fusion = (bf16[2048,1024]{1,0:T(8,128)(2,1)}, bf16[2048,1024]{1,0:T(8,128)(2,1)}, bf16[2048,1024]{1,0:T(8,128)(2,1)}) fusion(f32[2048,1024]{1,0:T(8,128)} %fusion.40, f32[2048,1024]{1,0:T(8,128)} %fusion.41, bf16[2048,2048]{1,0:T(8,128)(2,1)} %all-gather.25.cloned.1.call-done, bf16[1024,2048]{1,0:T(8,128)(2,1)} %all-gather.23.cloned.1.call-done), kind=kOutput, calls=%fused_computation.1 | convolution fusion | flops 8621391872 | bytes 41943040 | tf_op jit(solution)/shard_map/dot_general | solution.py:36
  603.1 15.4 %fusion.42 = f32[2048,2048]{1,0:T(8,128)} fusion(bf16[2048,1024]{1,0:T(8,128)(2,1)} %get-tuple-element.55, bf16[2048,1024]{1,0:T(8,128)(2,1)} %bitcast.133), kind=kOutput, calls=%fused_computation.117 | convolution fusion | flops 8589934592 | bytes 25165824 | tf_op jit(solution)/shard_map/dot_general | solution.py:36
  618.6 14.3 %add_convert_fusion = bf16[2048,2048]{1,0:T(8,128)(2,1)} fusion(f32[2048,2048]{1,0:T(8,128)} %fusion.42, bf16[2048,1024]{1,0:T(8,128)(2,1)S(1)} %copy-done.51, bf16[2048,1024]{1,0:T(8,128)(2,1)S(1)} %bitcast.136), kind=kOutput, calls=%fused_computation | convolution fusion | flops 8598323200 | bytes 33554432 | tf_op jit(solution)/shard_map/dot_general | solution.py:36
  632.9 13.9 %convolution_convert_fusion.2 = bf16[2048,2048]{1,0:T(8,128)(2,1)} fusion(bf16[2048,1024]{1,0:T(8,128)(2,1)} %get-tuple-element.56, bf16[1024,2048]{1,0:T(8,128)(2,1)} %all-gather.23.cloned.1.call-done), kind=kOutput, calls=%fused_computation.8 | convolution fusion | flops 8594128896 | bytes 16777216 | tf_op jit(solution)/shard_map/dot_general | solution.py:26
  646.9 14.7 %convolution_convert_fusion.4 = bf16[2048,1024]{1,0:T(8,128)(2,1)} fusion(bf16[2048,2048]{1,0:T(8,128)(2,1)} %all-gather.21.cloned.1.call-done, bf16[2048,1024]{1,0:T(8,128)(2,1)} %get-tuple-element.54), kind=kOutput, calls=%fused_computation.10 | convolution fusion | flops 8592031744 | bytes 16777216 | tf_op jit(solution)/shard_map/dot_general | solution.py:30
  661.6 12.9 convolution_convert_fusion.5
  674.6 14.4 %convolution_convert_fusion.3 = bf16[1024,2048]{1,0:T(8,128)(2,1)} fusion(bf16[2048,1024]{1,0:T(8,128)(2,1)} %get-tuple-element.56, bf16[2048,2048]{1,0:T(8,128)(2,1)} %all-gather.25.cloned.1.call-done), kind=kOutput, calls=%fused_computation.9 | convolution fusion | flops 8592031744 | bytes 16777216 | tf_op jit(solution)/shard_map/dot_general | solution.py:30
  689.0 32.1 %reduce-scatter.19.cloned.1.call-done = bf16[256,2048]{1,0:T(8,128)(2,1)} async-done(((bf16[2048,2048]{1,0:T(8,128)(2,1)}), bf16[256,2048]{1,0:T(8,128)(2,1)}) %reduce-scatter.19.cloned.1.call-update) | async-done | bytes 1048592 | tf_op jit(solution)/shard_map/reduce_scatter | solution.py:65
  722.9 88.6 %reduce-scatter.17.cloned.1.call-done = bf16[256,2048]{1,0:T(8,128)(2,1)} async-done(((bf16[2048,2048]{1,0:T(8,128)(2,1)}), bf16[256,2048]{1,0:T(8,128)(2,1)}) %reduce-scatter.17.cloned.1.call-update) | async-done | bytes 1048592 | tf_op jit(solution)/shard_map/reduce_scatter | solution.py:65
  821.8 30.4 %all_to_all.43 = bf16[8,256,256]{2,1,0:T(8,128)(2,1)S(1)} all-to-all(bf16[8,256,256]{2,1,0:T(8,128)(2,1)S(1)} %bitcast.139), channel_id=1, replica_groups=mesh['p'=4,'y'=2,'x'=2,'c'=2] {'y','x','c'}, dimensions={0} | all-to-all | bytes 2097152 | tf_op jit(solution)/shard_map/all_to_all | solution.py:69
  879.3 11.1 convolution_convert_fusion.1
  891.6 105.7 %all-reduce.9.cloned.1.call-done = (bf16[4,4,2,64,1024]{4,3,2,0,1:T(8,128)(2,1)}, bf16[4,4,2,64,1024]{4,3,2,0,1:T(8,128)(2,1)}) async-done(((bf16[4,4,2,64,1024]{4,3,2,0,1:T(8,128)(2,1)}, bf16[4,4,2,64,1024]{4,3,2,0,1:T(8,128)(2,1)}), (bf16[4,4,2,64,1024]{4,3,2,0,1:T(8,128)(2,1)}, bf16[4,4,2,64,1024]{4,3,2,0,1:T(8,128)(2,1)})) %all-reduce.9.cloned.1.call-update) | async-done | bytes 8388624
  1007.7 23.7 %all-to-all-done.7 = bf16[8,64,1024]{2,1,0:T(8,128)(2,1)S(1)} async-done(((bf16[8,64,1024]{2,1,0:T(8,128)(2,1)}), bf16[8,64,1024]{2,1,0:T(8,128)(2,1)S(1)}, u32[]{:S(2)}, u32[]{:S(2)}) %all-to-all-start.7) | async-done | bytes 1048608 | tf_op jit(solution)/shard_map/all_to_all | solution.py:69
  1036.1 17.9 %reduce-scatter.29.cloned.1.call-done = bf16[256,2048]{1,0:T(8,128)(2,1)} async-done(((bf16[1024,2048]{1,0:T(8,128)(2,1)}), bf16[256,2048]{1,0:T(8,128)(2,1)}) %reduce-scatter.29.cloned.1.call-update) | async-done | bytes 1048592 | tf_op jit(solution)/shard_map/reduce_scatter | solution.py:65
  1082.7 33.7 %reduce-scatter.23.cloned.1.call-done = bf16[512,768]{1,0:T(8,128)(2,1)} async-done(((bf16[2048,768]{1,0:T(8,128)(2,1)}), bf16[512,768]{1,0:T(8,128)(2,1)}) %reduce-scatter.23.cloned.1.call-update) | async-done | bytes 786448 | tf_op jit(solution)/shard_map/reduce_scatter | solution.py:65
  1120.2 12.8 multiply_subtract_fusion.1
  1139.2 72.4 %reduce-scatter.25.cloned.1.call-done = bf16[256,2048]{1,0:T(8,128)(2,1)} async-done(((bf16[2048,2048]{1,0:T(8,128)(2,1)}), bf16[256,2048]{1,0:T(8,128)(2,1)}) %reduce-scatter.25.cloned.1.call-update) | async-done | bytes 1048592 | tf_op jit(solution)/shard_map/reduce_scatter | solution.py:65
  1232.3 53.9 %reduce-scatter.21.cloned.1.call-done = bf16[256,2048]{1,0:T(8,128)(2,1)} async-done(((bf16[2048,2048]{1,0:T(8,128)(2,1)}), bf16[256,2048]{1,0:T(8,128)(2,1)}) %reduce-scatter.21.cloned.1.call-update) | async-done | bytes 1048592 | tf_op jit(solution)/shard_map/reduce_scatter | solution.py:65
  1290.0 25.6 %reduce-scatter.27.cloned.1.call-done = bf16[64,2048]{1,0:T(8,128)(2,1)} async-done(((bf16[256,2048]{1,0:T(8,128)(2,1)}), bf16[64,2048]{1,0:T(8,128)(2,1)}) %reduce-scatter.27.cloned.1.call-update) | async-done | bytes 262160 | tf_op jit(solution)/shard_map/reduce_scatter | solution.py:65
  (241 shorter events, 201.4 us)
Async XLA Ops:
  7.2 69.5 %all-gather.17.cloned.1.call-start = ((), (), s32[]{:S(2)}) async-start(), calls=%async_computation.18 | async-start | bytes 1310720 | tf_op jit(solution)/shard_map/all_gather | solution.py:61
  9.0 154.7 %all-gather.15.cloned.1.call-start = ((), (), s32[]{:S(2)}) async-start(), calls=%async_computation.17 | async-start | bytes 3932160 | tf_op jit(solution)/shard_map/all_gather | solution.py:61
  32.4 150.2 %all-gather.13.cloned.1.call-start = ((), (), s32[]{:S(2)}) async-start(), calls=%async_computation.16 | async-start | bytes 9437184 | tf_op jit(solution)/shard_map/all_gather | solution.py:61
  74.7 178.6 %copy-start.26 = (f32[2048,1]{0,1:T(1,128)}, f32[2048,1]{0,1:T(1,128)S(1)}, u32[]{:S(2)}) copy-start(f32[2048,1]{0,1:T(1,128)S(1)} %get-tuple-element.68) | copy-start | bytes 24580
  76.6 170.9 %all-gather.19.cloned.1.call-start = ((), (), s32[]{:S(2)}) async-start(), calls=%async_computation.19 | async-start | bytes 9437184 | tf_op jit(solution)/shard_map/all_gather | solution.py:61
  77.2 225.5 %all-gather.27.cloned.1.call-start = ((), (), s32[]{:S(2)}) async-start(), calls=%async_computation.30 | async-start | bytes 5242880 | tf_op jit(solution)/shard_map/all_gather | solution.py:61
  132.5 30.1 %all-to-all-start.3 = ((bf16[8,64,1024]{2,1,0:T(8,128)(2,1)}), bf16[8,64,1024]{2,1,0:T(8,128)(2,1)S(1)}, u32[]{:S(2)}, u32[]{:S(2)}) async-start(bf16[8,64,1024]{2,1,0:T(8,128)(2,1)} %reshape.185), calls=%async_computation.3 | async-start | bytes 2097152 | tf_op jit(solution)/shard_map/all_to_all | solution.py:69
  136.1 221.6 %all-gather.29.cloned.1.call-start = ((), (), s32[]{:S(2)}) async-start(), calls=%async_computation.31 | async-start | bytes 5242880 | tf_op jit(solution)/shard_map/all_gather | solution.py:61
  163.6 278.3 %all-gather.21.cloned.1.call-start = ((), (), s32[]{:S(2)}) async-start(), calls=%async_computation.20 | async-start | bytes 9437184 | tf_op jit(solution)/shard_map/all_gather | solution.py:61
  195.3 4.7 collective-permute-start
  255.9 239.8 %all-gather.23.cloned.1.call-start = ((), (), s32[]{:S(2)}) async-start(), calls=%async_computation.21 | async-start | bytes 5242880 | tf_op jit(solution)/shard_map/all_gather | solution.py:61
  257.8 321.5 %all-gather.25.cloned.1.call-start = ((), (), s32[]{:S(2)}) async-start(), calls=%async_computation.23 | async-start | bytes 9437184 | tf_op jit(solution)/shard_map/all_gather | solution.py:61
  258.5 462.6 %reduce-scatter.19.cloned.1.call-start = ((), (), s32[]{:S(2)}) async-start(), calls=%async_computation.24 | async-start | bytes 9437184 | tf_op jit(solution)/shard_map/reduce_scatter | solution.py:65
  632.9 178.6 %reduce-scatter.17.cloned.1.call-start = ((), (), s32[]{:S(2)}) async-start(), calls=%async_computation.22 | async-start | bytes 9437184 | tf_op jit(solution)/shard_map/reduce_scatter | solution.py:65
  646.9 350.4 %all-reduce.9.cloned.1.call-start = ((), (), s32[]{:S(2)}) async-start(), calls=%async_computation.33 | async-start | bytes 16777216
  674.5 379.5 %reduce-scatter.29.cloned.1.call-start = ((), (), s32[]{:S(2)}) async-start(), calls=%async_computation.29 | async-start | bytes 5242880 | tf_op jit(solution)/shard_map/reduce_scatter | solution.py:65
  689.0 122.5 %copy-start.19 = (bf16[256,2048]{1,0:T(8,128)(2,1)S(1)}, bf16[256,2048]{1,0:T(8,128)(2,1)}, u32[]{:S(2)}) copy-start(bf16[256,2048]{1,0:T(8,128)(2,1)} %param.24) | copy-start | bytes 3145732
  689.0 427.4 %reduce-scatter.23.cloned.1.call-start = ((), (), s32[]{:S(2)}) async-start(), calls=%async_computation.26 | async-start | bytes 3932160 | tf_op jit(solution)/shard_map/reduce_scatter | solution.py:65
  854.2 5.7 collective-permute-start.1
  870.5 267.9 %reduce-scatter.31.cloned.1.call-start = ((), (), s32[]{:S(2)}) async-start(), calls=%async_computation.32 | async-start | bytes 163840
  871.4 340.2 %reduce-scatter.25.cloned.1.call-start = ((), (), s32[]{:S(2)}) async-start(), calls=%async_computation.27 | async-start | bytes 9437184 | tf_op jit(solution)/shard_map/reduce_scatter | solution.py:65
  878.1 408.1 %reduce-scatter.21.cloned.1.call-start = ((), (), s32[]{:S(2)}) async-start(), calls=%async_computation.25 | async-start | bytes 9437184 | tf_op jit(solution)/shard_map/reduce_scatter | solution.py:65
  1000.2 31.2 %all-to-all-start.7 = ((bf16[8,64,1024]{2,1,0:T(8,128)(2,1)}), bf16[8,64,1024]{2,1,0:T(8,128)(2,1)S(1)}, u32[]{:S(2)}, u32[]{:S(2)}) async-start(bf16[8,64,1024]{2,1,0:T(8,128)(2,1)} %bitcast.128), calls=%async_computation.13 | async-start | bytes 2097152 | tf_op jit(solution)/shard_map/all_to_all | solution.py:69
  1031.4 40.0 %all-to-all-start.6 = ((bf16[8,64,1024]{2,1,0:T(8,128)(2,1)}), bf16[8,64,1024]{2,1,0:T(8,128)(2,1)}, u32[]{:S(2)}, u32[]{:S(2)}) async-start(bf16[8,64,1024]{2,1,0:T(8,128)(2,1)} %bitcast.127), calls=%async_computation.12 | async-start | bytes 2097152 | tf_op jit(solution)/shard_map/all_to_all | solution.py:69
  1116.4 95.8 %all-to-all-start.5 = ((bf16[8,64,768]{2,1,0:T(8,128)(2,1)}), bf16[8,64,768]{2,1,0:T(8,128)(2,1)S(1)}, u32[]{:S(2)}, u32[]{:S(2)}) async-start(bf16[8,64,768]{2,1,0:T(8,128)(2,1)} %bitcast.141), calls=%async_computation.9 | async-start | bytes 1572864 | tf_op jit(solution)/shard_map/all_to_all | solution.py:69
  1120.1 91.5 %copy-start.41 = (f32[3,64]{1,0:T(4,128)S(1)}, f32[3,64]{1,0:T(4,128)}, u32[]{:S(2)}) copy-start(f32[3,64]{1,0:T(4,128)} %param.43) | copy-start | bytes 2308
  1120.1 91.5 %copy-start.45 = (f32[3,64]{1,0:T(4,128)S(1)}, f32[3,64]{1,0:T(4,128)}, u32[]{:S(2)}) copy-start(f32[3,64]{1,0:T(4,128)} %param.45) | copy-start | bytes 2308
  1120.1 91.5 %copy-start.46 = (f32[3,64]{1,0:T(4,128)S(1)}, f32[3,64]{1,0:T(4,128)}, u32[]{:S(2)}) copy-start(f32[3,64]{1,0:T(4,128)} %param.44) | copy-start | bytes 2308
  1120.1 195.5 %reduce-scatter.27.cloned.1.call-start = ((), (), s32[]{:S(2)}) async-start(), calls=%async_computation.28 | async-start | bytes 1310720 | tf_op jit(solution)/shard_map/reduce_scatter | solution.py:65
  1223.5 62.7 %copy-start.3 = (bf16[256,2048]{1,0:T(8,128)(2,1)S(1)}, bf16[256,2048]{1,0:T(8,128)(2,1)}, u32[]{:S(2)}) copy-start(bf16[256,2048]{1,0:T(8,128)(2,1)} %param.23) | copy-start | bytes 3145732
  1223.6 62.6 %copy-start.25 = (f32[2048,1]{0,1:T(1,128)S(1)}, f32[2048,1]{0,1:T(1,128)}, u32[]{:S(2)}) copy-start(f32[2048,1]{0,1:T(1,128)} %copy-done.24) | copy-start | bytes 24580
  1223.6 62.6 %copy-start.31 = (f32[256]{0:T(256)S(1)}, f32[256]{0:T(256)}, u32[]{:S(2)}) copy-start(f32[256]{0:T(256)} %copy-done.30) | copy-start | bytes 3076
  (49 other events, 620.6 us)
Sparse Core Ops, SparseCore 0:
  10.2 30.6 all-gather.16
  42.4 82.2 all-gather.14
  127.2 55.3 all-gather.12
  184.3 63.0 all-gather.18
  249.2 53.4 all-gather.26
  305.0 52.6 all-gather.28
  359.9 82.0 all-gather.20
  444.4 51.2 all-gather.22
  497.2 82.0 all-gather.24
  633.0 88.1 reduce-scatter.18
  723.5 87.9 reduce-scatter.16
  815.1 182.1 all-reduce.8
  1000.5 53.3 reduce-scatter.28
  1056.1 60.2 reduce-scatter.22
  1119.1 19.2 reduce-scatter.30
  1142.0 69.4 reduce-scatter.24
  1214.9 71.2 reduce-scatter.20
  1288.4 27.1 reduce-scatter.26

commit v2 on v1

v2 whole, which is shorter than its diff:
```python
import functools

import jax
import jax.numpy as jnp
from jax import lax
from jax.experimental import pallas as pl
from jax.experimental.pallas import tpu as pltpu
from jax.sharding import Mesh
from jax.sharding import PartitionSpec as P

SEQ_BASE = 8192
STEP = 10

EPS_NORM = 1e-05
BETA_ONE = 0.9
BETA_TWO = 0.95
ADAM_EPS = 1e-08
DECAY_RATE = 0.1
RATE_MATRIX = 0.01
RATE_VECTOR = 0.3

AXES = ("h", "l", "y", "x", "c")
GROUP = ("l", "x", "c")
CLASS = ("h", "y")
LOW = jnp.bfloat16
F32 = jnp.float32


def forward_dot(operand, partner):
    return jnp.dot(operand, partner, preferred_element_type=jnp.float32)


def over_tokens(operand, partner):
    return lax.dot_general(
        operand, partner, (((0,), (0,)), ((), ())), preferred_element_type=jnp.float32
    )


def against_rows(operand, partner):
    return lax.dot_general(
        operand, partner, (((1,), (1,)), ((), ())), preferred_element_type=jnp.float32
    )


def rms_parts(values):
    scale = lax.rsqrt(jnp.mean(values * values, axis=-1, keepdims=True) + EPS_NORM)
    return (scale, values * scale)


def norm_back(upstream, normal, scale, gain):
    scaled = upstream * gain
    return scale * (scaled - normal * jnp.mean(scaled * normal, axis=-1, keepdims=True))


def adamw(weight, first, second, grad, rate, decay):
    first_new = BETA_ONE * first + (1.0 - BETA_ONE) * grad
    second_new = BETA_TWO * second + (1.0 - BETA_TWO) * grad * grad
    fix_one = 1.0 - BETA_ONE**STEP
    fix_two = 1.0 - BETA_TWO**STEP
    stepped = first_new / fix_one / (jnp.sqrt(second_new / fix_two) + ADAM_EPS)
    return (first_new, second_new, weight - rate * (stepped + decay * weight))


def after(value, *others):
    return lax.optimization_barrier((value, *others))[0]


def together(*values):
    return lax.optimization_barrier(values)


def swap(block, axis):
    return lax.ppermute(block, axis, [(0, 1), (1, 0)])


def turn(block, distance):
    count = lax.axis_size("h")
    return lax.ppermute(block, "h", [((i + distance) % count, i) for i in range(count)])


def in_order(pieces, axis):
    own, other = pieces
    first = lax.axis_index(axis) == 0
    return jnp.stack([jnp.where(first, own, other), jnp.where(first, other, own)])


def class_small(block):
    if lax.axis_size("h") == 2:
        block = in_order((block, turn(block, 1)), "h")
    else:
        block = lax.all_gather(block, "h", axis=0, tiled=False)
    return in_order((block, swap(block, "y")), "y")


def group_small(block):
    for axis in ("l", "x", "c"):
        block = in_order((block, swap(block, axis)), axis)
    return block.transpose(4, 2, 3, 1, 0, 5, 6)


def turns(block):
    return [turn(block, i) for i in range(1, lax.axis_size("h"))]


def swaps(blocks):
    return [swap(block, "y") for block in blocks]


def class_stack(own, by_h, by_y, by_both):
    count = lax.axis_size("h")
    rows = []
    for first, rest in ((own, by_h), (by_y, by_both)):
        rows += first
        for i in range(count - 1):
            rows += [part[i] for part in rest]
    return jnp.concatenate(rows, axis=0)


def class_lend(term):
    half = term.shape[0] // 2
    return term[:half] + swap(term[half:], "y")


def class_settle(column):
    count = lax.axis_size("h")
    rows = column.shape[0] // count
    total = column[:rows].astype(F32)
    for i in range(1, count):
        total = total + turn(column[i * rows : (i + 1) * rows], -i).astype(F32)
    return total.astype(LOW)


def class_scatter(term):
    return class_settle(class_lend(term))


def group_gather(block):
    return lax.all_gather(block, GROUP, axis=0, tiled=True)


def group_exchange(blocks):
    return lax.all_to_all(blocks, GROUP, split_axis=0, concat_axis=0, tiled=True)


def core_rows(array, own):
    core = lax.axis_index("c") if own else 1 - lax.axis_index("c")
    rows = array.shape[0] // 8
    return jnp.concatenate(
        [lax.dynamic_slice_in_dim(array, (2 * i + core) * rows, rows, axis=0) for i in range(4)],
        axis=0,
    )


def group_lend(near, far):
    quarter = near.shape[0] // 4
    half = quarter // 2
    got = swap(far, "c")
    mine_l, mine_x = lax.axis_index("l"), lax.axis_index("x")

    def block(dl, dx):
        place = (mine_l ^ dl) * 2 + (mine_x ^ dx)
        return tuple(
            lax.dynamic_slice_in_dim(part, place * quarter, quarter, axis=0) for part in (near, got)
        )

    corner = sum(block(1, 1))
    from_l = swap(corner[:half], "l")
    from_x = swap(corner[half:], "x")
    return from_l, from_x, block


def group_settle(from_l, from_x, block):
    near_x, got_x = block(0, 1)
    near_l, got_l = block(1, 0)
    by_x = near_x + got_x + jnp.concatenate([from_l, jnp.zeros_like(from_l)], axis=0)
    by_l = near_l + got_l + jnp.concatenate([jnp.zeros_like(from_x), from_x], axis=0)
    own = sum(block(0, 0))
    return own, swap(by_x, "x"), swap(by_l, "l")


def rearranged(values, to_class):
    count = lax.axis_size("h")
    rest = values.shape[-1] // (4 * count)
    blocks = [values[..., i * rest : (i + 1) * rest] for i in range(4 * count)]
    mine_h, mine_y = lax.axis_index("h"), lax.axis_index("y")
    if to_class:
        lists = [
            [[blocks[((h * 2) + l) * 2 + y] for h in range(count)] for y in range(2)] for l in range(2)
        ]
    else:
        lists = [
            [[blocks[(y * count + h) * 2 + l] for h in range(count)] for y in range(2)] for l in range(2)
        ]

    def pick(l, y, h):
        chosen = None
        for shift in range(count):
            at = (h + shift) % count if to_class else (h - shift) % count
            here = jnp.where(mine_y == 0, lists[l][y][at], lists[l][1 - y][at])
            chosen = here if chosen is None else jnp.where(mine_h == shift, here, chosen)
        return chosen

    if to_class:
        order = [(l, y, h) for y in range(2) for h in range(count) for l in range(2)]
    else:
        order = [(l, y, h) for h in range(count) for l in range(2) for y in range(2)]
    return jnp.concatenate([pick(*place) for place in order], axis=-1)


def class_rows(array):
    count = lax.axis_size("h")
    split = array.reshape(2, count, -1, array.shape[1])
    mine_h, mine_y = lax.axis_index("h"), lax.axis_index("y")
    pieces = []
    for h in range(count):
        for y in range(2):
            at = [mine_y ^ y, (h - mine_h) & (count - 1), 0, 0]
            pieces.append(lax.dynamic_slice(split, at, (1, 1, *split.shape[2:]))[0, 0])
    return jnp.concatenate(pieces, axis=0)


def class_pieces(array):
    count = lax.axis_size("h")
    split = array.reshape(count, 2, -1, array.shape[1])
    mine_h, mine_y = lax.axis_index("h"), lax.axis_index("y")
    pieces = []
    for dy in range(2):
        for dh in range(count):
            at = [(mine_h + dh) & (count - 1), mine_y ^ dy, 0, 0]
            pieces.append(lax.dynamic_slice(split, at, (1, 1, *split.shape[2:]))[0, 0])
    return jnp.concatenate(pieces, axis=0)


def places(count):
    return [(h, l, y, x, c) for h in range(count) for l in (0, 1) for y in (0, 1) for x in (0, 1) for c in (0, 1)]


def pack_body(count, inward_ref, gate_ref, up_ref, inward_out, ffn_out):
    d_rows = inward_ref.shape[1] // (48 * count)
    ff_rows = gate_ref.shape[1] // (16 * count)
    feats, units = 2 * count * d_rows, 2 * count * ff_rows
    for at, (h, l, y, x, c) in enumerate(places(count)):
        to, slot = (l * 2 + x) * 2 + c, h * 2 + y
        for kind, ref in enumerate((gate_ref, up_ref)):
            block = ref[:, at * ff_rows : (at + 1) * ff_rows].astype(LOW)
            ffn_out[to, :, kind * units + slot * ff_rows : kind * units + (slot + 1) * ff_rows] = block
    for part in range(3):
        for to in range(8):
            l, x, c = to // 4, to // 2 % 2, to % 2
            blocks = []
            for h in range(count):
                for y in range(2):
                    at = part * 16 * count + (((h * 2 + l) * 2 + y) * 2 + x) * 2 + c
                    blocks.append(inward_ref[:, at * d_rows : (at + 1) * d_rows])
            block = jnp.concatenate(blocks, axis=1).astype(LOW)
            inward_out[to, :, part * feats : (part + 1) * feats] = block


def packed(inward, gate, up, count):
    d_rows, ff = gate.shape
    feats, units = inward.shape[1] // 24, ff // 8
    if d_rows % 64 or units % (256 * count):
        sent = inward.astype(LOW).reshape(d_rows, 3, count, 2, 2, 2, 2, -1)
        sent = sent.transpose(3, 5, 6, 0, 1, 2, 4, 7).reshape(8, d_rows, 3 * feats)
        both = jnp.stack([gate.astype(LOW), up.astype(LOW)], axis=1)
        both = both.reshape(d_rows, 2, count, 2, 2, 2, 2, -1).transpose(3, 5, 6, 0, 1, 2, 4, 7)
        return sent, both.reshape(8, d_rows, 2 * units)
    rows = 16
    return pl.pallas_call(
        functools.partial(pack_body, count),
        grid=(d_rows // rows,),
        in_specs=[
            pl.BlockSpec((rows, 24 * feats), lambda i: (i, 0)),
            pl.BlockSpec((rows, ff), lambda i: (i, 0)),
            pl.BlockSpec((rows, ff), lambda i: (i, 0)),
        ],
        out_specs=[
            pl.BlockSpec((8, rows, 3 * feats), lambda i: (0, i, 0)),
            pl.BlockSpec((8, rows, 2 * units), lambda i: (0, i, 0)),
        ],
        out_shape=[
            jax.ShapeDtypeStruct((8, d_rows, 3 * feats), LOW),
            jax.ShapeDtypeStruct((8, d_rows, 2 * units), LOW),
        ],
        compiler_params=pltpu.CompilerParams(vmem_limit_bytes=32 * 2**20),
        cost_estimate=pl.CostEstimate(flops=0, transcendentals=0, bytes_accessed=6 * d_rows * (24 * feats + 2 * ff)),
    )(inward, gate, up)


def update_body(pieces, got_ref, weight_ref, first_ref, second_ref, first_out, second_out, weight_out, dot_out):
    width = weight_ref.shape[1] // len(pieces)

    @pl.when(pl.program_id(0) == 0)
    def _():
        dot_out[...] = jnp.zeros_like(dot_out)

    total = jnp.zeros((weight_ref.shape[0], 128), F32)
    for group in range(0, len(pieces), max(1, 128 // width)):
        parts = pieces[group : group + max(1, 128 // width)]
        grad = [got_ref[tuple(at)][:, lane : lane + width].astype(F32) for *at, lane in parts]
        grad = jnp.concatenate(grad, axis=1) if len(grad) > 1 else grad[0]
        here = slice(group * width, group * width + grad.shape[1])
        weight = weight_ref[:, here]
        first, second, updated = adamw(
            weight, first_ref[:, here], second_ref[:, here], grad, RATE_MATRIX, DECAY_RATE
        )
        first_out[:, here] = first
        second_out[:, here] = second
        weight_out[:, here] = updated
        dots = weight.astype(LOW).astype(F32) * grad
        for lane in range(0, grad.shape[1], 128):
            total += dots[:, lane : lane + 128]
    dot_out[...] += total


def updated_columns(got, weight, first, second, count, parts):
    rows, columns = weight.shape
    width = columns // (16 * count * parts)
    if width % (128 if parts == 1 else 64) or rows % 16:
        grad = got.reshape(2, 2, 2, rows, parts, count, 2, width).transpose(3, 4, 5, 0, 6, 1, 2, 7)
        grad = grad.reshape(rows, columns).astype(F32)
        new = adamw(weight, first, second, grad, RATE_MATRIX, DECAY_RATE)
        return new, jnp.sum(weight.astype(LOW).astype(F32) * grad, axis=1)
    if parts == 1:
        grid = (4 * count,)
        got = got.reshape(2, 4, rows, 2 * count * width)
        got_spec = pl.BlockSpec((1, 4, rows, width), lambda k: (k // 2 % 2, 0, 0, k // 4 * 2 + k % 2))
        pieces = [(0, q, 0) for q in range(4)]
        block = 4 * width
    else:
        grid = (parts,)
        got_spec = pl.BlockSpec((8, rows, 2 * count * width), lambda k: (0, 0, k))
        pieces = [((l * 2 + x) * 2 + c, (h * 2 + y) * width) for h, l, y, x, c in places(count)]
        block = 16 * count * width
    spec = pl.BlockSpec((rows, block), lambda k: (0, k))
    shape = jax.ShapeDtypeStruct(weight.shape, F32)
    *new, dots = pl.pallas_call(
        functools.partial(update_body, pieces),
        grid=grid,
        in_specs=[got_spec, spec, spec, spec],
        out_specs=[spec, spec, spec, pl.BlockSpec((rows, 128), lambda k: (0, 0))],
        out_shape=[shape, shape, shape, jax.ShapeDtypeStruct((rows, 128), F32)],
        compiler_params=pltpu.CompilerParams(vmem_limit_bytes=32 * 2**20),
        cost_estimate=pl.CostEstimate(
            flops=20 * rows * columns, transcendentals=2 * rows * columns, bytes_accessed=26 * rows * columns
        ),
    )(got, weight, first, second)
    return tuple(new), jnp.sum(dots, axis=1)


def step_h(block, distance):
    count = lax.axis_size("h")
    route = []
    for i in range(count):
        if 0 <= i - distance < count:
            y_to = 0 if distance == 1 else 1
            route.append((2 * (i - distance) + 1 - y_to, 2 * i + y_to))
    return lax.ppermute(block, CLASS, route)


def on_device(
    block_input,
    cotangent,
    inward_weight,
    inward_first,
    inward_second,
    outward_weight,
    outward_first,
    outward_second,
    gate_weight,
    gate_first,
    gate_second,
    up_weight,
    up_first,
    up_second,
    down_weight,
    down_first,
    down_second,
    norm_gains,
    gains_first,
    gains_second,
    conv_taps,
    taps_first,
    taps_second,
):
    count = lax.axis_size("h")
    tok_rows, d = block_input.shape
    d_rows = inward_weight.shape[0]
    ff = gate_weight.shape[1]
    ff_rows = down_weight.shape[0]
    group_rows = 8 * tok_rows
    near_rows = 4 * tok_rows
    seq_len = min(SEQ_BASE, group_rows * 2 * count)
    feats = d // 8
    units = ff // 8
    mine = {axis: lax.axis_index(axis) for axis in AXES}

    small = class_small(jnp.concatenate([norm_gains, conv_taps], axis=0).astype(LOW))
    outward_low, down_low, small = together(
        outward_weight.astype(LOW), down_weight.astype(LOW), small
    )
    outward_h, outward_y = turns(outward_low), swap(outward_low, "y")
    down_a, down_b = down_low[: ff_rows // 2], down_low[ff_rows // 2 :]
    down_ah, down_ay = turns(down_a), swap(down_a, "y")
    small = group_small(small)
    inward_sent, ffn_sent = packed(inward_weight, gate_weight, up_weight, count)
    inward_got = group_exchange(after(inward_sent, small)).reshape(8 * d_rows, 3 * feats)
    block_here = rearranged(block_input, True)
    inward_got, ffn_sent, outward_h, outward_y, down_ah, down_ay, down_b, small, block_here = together(
        inward_got, ffn_sent, outward_h, outward_y, down_ah, down_ay, down_b, small, block_here
    )

    inward_h, inward_y = turns(inward_got), swap(inward_got, "y")
    ffn_got = group_exchange(ffn_sent).reshape(8 * d_rows, 2 * units)
    inputs_low = group_gather(block_here)
    outward_hy, down_ahy = swaps(outward_h), swaps(down_ah)
    inward_h, inward_y, outward_hy, down_ahy, ffn_got = together(
        inward_h, inward_y, outward_hy, down_ahy, ffn_got
    )
    outward_part = class_stack([outward_low], [outward_h], [outward_y], [outward_hy])
    outward_full = group_gather(class_rows(outward_part))

    half_d = 4 * d_rows
    gate_a, gate_b = ffn_got[:half_d, :units], ffn_got[half_d:, :units]
    up_low = ffn_got[:, units:]
    inward_hy = swaps(inward_h)
    gate_ah, gate_ay = turns(gate_a), swap(gate_a, "y")
    inward_hy, gate_ah, gate_ay, gate_b, up_low, inputs_low = together(
        inward_hy, gate_ah, gate_ay, gate_b, up_low, inputs_low
    )
    inward_part = class_stack([inward_got], [inward_h], [inward_y], [inward_hy])
    gate_bh, gate_by, gate_ahy = turns(gate_b), swap(gate_b, "y"), swaps(gate_ah)
    small = small.astype(F32)

    gain_one = small[..., 0, :].reshape(d)
    gain_two = small[..., 1, :].reshape(d)
    taps_here = lax.dynamic_slice(
        small, (0, mine["l"], 0, mine["x"], mine["c"], 2, 0), (count, 1, 2, 1, 1, 3, d_rows)
    )
    taps_here = taps_here.reshape(2 * count, 3, d_rows).transpose(1, 0, 2).reshape(3, feats)
    tap_zero, tap_one, tap_two = taps_here[0], taps_here[1], taps_here[2]

    _, normed_one = rms_parts(inputs_low.astype(F32))
    normed_one = (normed_one * rearranged(gain_one, True)).astype(LOW)
    mixed = forward_dot(normed_one, inward_part).reshape(2, near_rows, 3 * feats)
    b_part = mixed[..., :feats]
    c_part = mixed[..., feats : 2 * feats]
    x_part = mixed[..., 2 * feats :]
    gated = b_part * x_part
    tails = gated[:, near_rows - 2 :]
    runs = (mine["h"] * 2 + jnp.arange(2)) * 2 + mine["y"]
    starts_here = (runs * near_rows % seq_len == 0).reshape(2, 1, 1)
    beside = swap(tails, "y")
    below = step_h(tails[1], 1)
    before = jnp.where(mine["y"] == 1, beside, jnp.stack([below, beside[0]]))
    before = jnp.where(starts_here, 0.0, before)
    extended = jnp.concatenate([before, gated], axis=1)
    convolved = (
        tap_zero * extended[:, :near_rows]
        + tap_one * extended[:, 1 : near_rows + 1]
        + tap_two * extended[:, 2:]
    )
    branch_feats = (c_part * convolved).astype(LOW).reshape(group_rows, feats)
    branch_feats, gate_bh, gate_by, gate_ahy, up_low = together(
        branch_feats, gate_bh, gate_by, gate_ahy, up_low
    )
    up_h, up_y, gate_bhy = turns(up_low), swap(up_low, "y"), swaps(gate_bh)
    branch_in = group_exchange(branch_feats.reshape(8, tok_rows, feats))
    branch_in = branch_in.transpose(1, 0, 2).reshape(tok_rows, d)
    inputs = block_input.astype(F32)
    middle = inputs + forward_dot(branch_in, outward_full)
    scale_two, normal_two = rms_parts(middle)

    normed_two = rearranged((normal_two * gain_two).astype(LOW), True)
    normed_two, up_h, up_y, gate_bhy, down_b = together(normed_two, up_h, up_y, gate_bhy, down_b)
    upstream = group_gather(after(cotangent, normed_two))
    normed_two = group_gather(normed_two)
    down_bh, down_by, up_hy = turns(down_b), swap(down_b, "y"), swaps(up_h)
    down_bh, down_by, up_hy = together(down_bh, down_by, up_hy)
    down_bhy = swaps(down_bh)
    gate_part = class_stack(
        [gate_a, gate_b], [gate_ah, gate_bh], [gate_ay, gate_by], [gate_ahy, gate_bhy]
    )
    up_part = class_stack([up_low], [up_h], [up_y], [up_hy])
    down_part = class_stack(
        [down_a, down_b], [down_ah, down_bh], [down_ay, down_by], [down_ahy, down_bhy]
    )
    down_part = class_rows(down_part)
    gate_value = forward_dot(normed_two, gate_part)
    up_value = forward_dot(normed_two, up_part)
    sigmoid_gate = jax.nn.sigmoid(gate_value)
    silu_gate = gate_value * sigmoid_gate
    hidden = (silu_gate * up_value).astype(LOW)
    result = forward_dot(hidden, down_part).astype(LOW)
    hidden, result = together(hidden, result)
    result = lax.psum_scatter(result, GROUP, scatter_dimension=0, tiled=True)
    down_term = class_pieces(over_tokens(hidden, upstream).astype(LOW))
    hidden, down_term = together(hidden, down_term)
    down_column = class_lend(down_term)
    hidden_grad = against_rows(upstream, down_part)
    gate_grad = hidden_grad * up_value * sigmoid_gate * (1.0 + gate_value * (1.0 - sigmoid_gate))
    up_grad = hidden_grad * silu_gate
    gate_grad = gate_grad.astype(LOW)
    up_grad = up_grad.astype(LOW)

    def ffn_back(own):
        part = against_rows(core_rows(gate_grad, own), gate_part)
        return (part + against_rows(core_rows(up_grad, own), up_part)).astype(LOW)

    far = ffn_back(False)
    far, down_column = together(far, down_column)
    down_sum = class_settle(down_column)
    near = ffn_back(True)
    gate_term = over_tokens(normed_two, gate_grad).astype(LOW)
    far, near, gate_term = together(far, near, gate_term)
    gate_column = class_lend(gate_term)
    up_term = over_tokens(normed_two, up_grad).astype(LOW)
    from_l, from_x, block = group_lend(near, far)
    from_l, from_x, gate_column, up_term, down_sum = together(
        from_l, from_x, gate_column, up_term, down_sum
    )
    down_sum = down_sum.astype(F32)
    gate_own = class_settle(gate_column)
    up_column = class_lend(up_term)
    *parts, gate_own, up_column, result = together(
        *group_settle(from_l, from_x, block), gate_own, up_column, result
    )
    block_output = (middle + result.astype(F32)).astype(LOW)
    normed_two_grad = rearranged(sum(part.astype(F32) for part in parts), False)

    middle_grad = cotangent.astype(F32) + norm_back(
        normed_two_grad, normal_two, scale_two, gain_two
    )
    branch_grad = middle_grad.astype(LOW)
    branch_in_grad = against_rows(branch_grad, outward_full).astype(LOW)
    branch_in_grad = group_exchange(branch_in_grad.reshape(tok_rows, 8, feats).transpose(1, 0, 2))
    branch_in_grad = branch_in_grad.reshape(2, near_rows, feats).astype(F32)
    branch_grad_full = group_gather(branch_grad)

    c_grad = branch_in_grad * convolved
    conv_grad = branch_in_grad * c_part
    ext_grad = (
        jnp.pad(tap_zero * conv_grad, ((0, 0), (0, 2), (0, 0)))
        + jnp.pad(tap_one * conv_grad, ((0, 0), (1, 1), (0, 0)))
        + jnp.pad(tap_two * conv_grad, ((0, 0), (2, 0), (0, 0)))
    )
    tap_grads = jnp.stack(
        [
            jnp.sum(conv_grad * extended[:, offset : offset + near_rows], axis=(0, 1))
            for offset in range(3)
        ],
        axis=1,
    )
    firsts = jnp.where(starts_here, 0.0, ext_grad[:, :2])
    beside = swap(firsts, "y")
    above = step_h(firsts[0], -1)
    returned = jnp.where(mine["y"] == 0, beside, jnp.stack([beside[1], above]))

    returned, gate_own, up_column = together(returned, gate_own, up_column)
    gate_own = group_exchange(gate_own.reshape(8, d_rows, units))
    up_own = class_settle(up_column)
    gated_grad = ext_grad[:, 2:] + jnp.pad(returned, ((0, 0), (near_rows - 2, 0), (0, 0)))
    mixed_grad = jnp.concatenate([gated_grad * x_part, c_grad, gated_grad * b_part], axis=2)
    mixed_grad = mixed_grad.astype(LOW).reshape(group_rows, 3 * feats)
    far = against_rows(core_rows(mixed_grad, False), inward_part).astype(LOW)
    near = against_rows(core_rows(mixed_grad, True), inward_part).astype(LOW)
    inward_term = over_tokens(normed_one, mixed_grad).astype(LOW)
    far, near, inward_term, branch_grad_full = together(far, near, inward_term, branch_grad_full)
    inward_column = class_lend(inward_term)
    outward_term = class_pieces(over_tokens(branch_feats, branch_grad_full).astype(LOW))
    from_l, from_x, block = group_lend(near, far)
    from_l, from_x, up_own, inward_column, outward_term = together(
        from_l, from_x, up_own, inward_column, outward_term
    )
    up_own = group_exchange(up_own.reshape(8, d_rows, units))
    inward_own = class_settle(inward_column)
    outward_column = class_lend(outward_term)
    *parts, inward_own, outward_column = together(
        *group_settle(from_l, from_x, block), inward_own, outward_column
    )
    outward_sum = class_settle(outward_column).astype(F32)
    normed_one_grad = rearranged(sum(part.astype(F32) for part in parts), False)
    scale_one, normal_one = rms_parts(inputs)
    input_grad = middle_grad + norm_back(normed_one_grad, normal_one, scale_one, gain_one)

    inward_own = group_exchange(inward_own.reshape(8, d_rows, 3 * feats))

    gate_new, gate_dots = updated_columns(gate_own, gate_weight, gate_first, gate_second, count, 1)
    up_new, up_dots = updated_columns(up_own, up_weight, up_first, up_second, count, 1)
    inward_new, inward_dots = updated_columns(
        inward_own, inward_weight, inward_first, inward_second, count, 3
    )
    own_gains = norm_gains.astype(LOW).astype(F32)
    gain_one_grad = inward_dots / own_gains[0]
    gain_two_grad = (gate_dots + up_dots) / own_gains[1]
    gains_grad = jnp.stack([gain_one_grad, gain_two_grad])
    taps_grad = lax.psum_scatter(tap_grads, CLASS, scatter_dimension=0, tiled=True).T

    outward_new = adamw(
        outward_weight, outward_first, outward_second, outward_sum, RATE_MATRIX, DECAY_RATE
    )
    down_new = adamw(down_weight, down_first, down_second, down_sum, RATE_MATRIX, DECAY_RATE)
    gains_new = adamw(norm_gains, gains_first, gains_second, gains_grad, RATE_VECTOR, 0.0)
    taps_new = adamw(conv_taps, taps_first, taps_second, taps_grad, RATE_VECTOR, 0.0)
    return (
        block_output,
        input_grad,
        *inward_new,
        *outward_new,
        *gate_new,
        *up_new,
        *down_new,
        *gains_new,
        *taps_new,
    )


def solution(mesh):
    devices = mesh.devices.reshape(-1, 2, 2, 2, 2)
    rows = P(AXES, None)
    columns = P(None, AXES)
    return jax.shard_map(
        on_device,
        mesh=Mesh(devices, AXES),
        in_specs=(rows,) * 17 + (columns,) * 6,
        out_specs=(rows,) * 17 + (columns,) * 6,
        check_vma=False,
    )
```

time: 1330 us -> 922 us (0.69)
  waiting for transfers between devices: 811 us -> 407 us
  blocking collectives: 162 us -> 28.9 us
  starting transfers between devices: 22.2 us -> 94.1 us
  other arithmetic: 57.8 us -> 90.2 us
  Pallas kernels: 0 us -> 15.7 us
    ppermute x2 -> x50, waiting for transfers between devices: 4.99 us -> 342 us  [the longest x13 242 us: turn(): lax.ppermute(block, 'h', [((i + distance) % count, i) for i in range(coun...]
    reduce_scatter x7 -> x1, waiting for transfers between devices: 324 us -> 0.01 us  [on_device(): result = lax.psum_scatter(result, GROUP, scatter_dimension=0, tiled=True)]
    all_gather x9 -> x5, waiting for transfers between devices: 319 us -> 34.7 us  [group_gather(): return lax.all_gather(block, GROUP, axis=0, tiled=True)]
    unnamed x20 -> x8, waiting for transfers between devices: 112 us -> 0.62 us
    all_to_all x4 -> x1, blocking collectives: 121 us -> 28.9 us  [group_exchange(): lax.all_to_all(blocks, GROUP, split_axis=0, concat_axis=0, tiled=True)]
    ppermute x2 -> x50, starting transfers between devices: 4.93 us -> 69.1 us  [the longest x35 41.6 us: swap(): return lax.ppermute(block, axis, [(0, 1), (1, 0)])]
    all_gather x1 -> x0, blocking collectives: 41.2 us -> none  [gather(): return lax.all_gather(block, axes, axis=0, tiled=True)]
    convert_element_type x11 -> x0, local copies, waits for them, and re-layouts: 33.1 us -> none  [the longest x6 21.7 us: ffn_sum(): return own.transpose(2, 0, 3, 1, 4).reshape(d_rows, ff).astype(jnp.float32)]
  transfers between devices with their start and end apart: 24 -> 63, of which waited for: 20 -> 27; matrix products, arithmetic and copies ran while one was open for 19% -> 30% of each run, Pallas kernels for 0% -> 1%
where the time goes in v2:
time: 922 us; the launch traced here: 917 us
  waiting for transfers between devices  407 us (44%)
  matrix products  190 us (21%)
  starting transfers between devices  94.1 us (10%)
  other arithmetic  90.2 us (10%)
  local copies, waits for them, and re-layouts  75.7 us (8%)
  blocking collectives  28.9 us (3%)
  between operations  16 us (2%)
  Pallas kernels  15.7 us (2%)
    ppermute x13, waiting for transfers between devices, turn(): lax.ppermute(block, 'h', [((i + distance) % count, i) for i in range(coun...  242 us
    ppermute x35, waiting for transfers between devices, swap(): return lax.ppermute(block, axis, [(0, 1), (1, 0)])  100 us
    dot_general x8, matrix products, against_rows(): lax.dot_general(operand, partner, (((1,), (1,)), ((), ())), preferred_ele...  72.2 us
    dot_general x5, matrix products, forward_dot(): return jnp.dot(operand, partner, preferred_element_type=jnp.float32)  65.2 us
    dot_general x5, matrix products, over_tokens(): lax.dot_general(operand, partner, (((0,), (0,)), ((), ())), preferred_ele...  52.4 us
    unnamed x218, local copies, waits for them, and re-layouts  50 us
    ppermute x35, starting transfers between devices, swap(): return lax.ppermute(block, axis, [(0, 1), (1, 0)])  41.6 us
    all_gather x5, waiting for transfers between devices, group_gather(): return lax.all_gather(block, GROUP, axis=0, tiled=True)  34.7 us
  transfers between devices with their start and end apart: 63, of which 27 were waited for; matrix products, arithmetic and copies ran while one was open for 30% of the time, Pallas kernels for 1%

profile of v2, /device:TPU:0, one launch (start us, length us, event | category | flops | bytes accessed | tf_op | source)
XLA Modules:
  0.0 917.4 jit_solution(17640554671385601268)
XLA Ops:
  50.6 30.9 %collective-permute-done.5 = bf16[64,2048]{1,0:T(8,128)(2,1)} collective-permute-done((bf16[64,2048]{1,0:T(8,128)(2,1)S(1)}, bf16[64,2048]{1,0:T(8,128)(2,1)}, u32[]{:S(2)}, u32[]{:S(2)}) %collective-permute-start.5) | collective-permute-done | bytes 262176 | tf_op jit(solution)/shard_map/ppermute | solution.py:78
  90.8 32.4 %collective-permute-done.11 = bf16[64,2048]{1,0:T(8,128)(2,1)} collective-permute-done((bf16[64,2048]{1,0:T(8,128)(2,1)}, bf16[64,2048]{1,0:T(8,128)(2,1)}, u32[]{:S(2)}, u32[]{:S(2)}) %collective-permute-start.11) | collective-permute-done | bytes 262176 | tf_op jit(solution)/shard_map/ppermute | solution.py:73
  123.2 36.9 %collective-permute-done.9 = bf16[512,768]{1,0:T(8,128)(2,1)} collective-permute-done((bf16[512,768]{1,0:T(8,128)(2,1)}, bf16[512,768]{1,0:T(8,128)(2,1)}, u32[]{:S(2)}, u32[]{:S(2)}) %collective-permute-start.9) | collective-permute-done | bytes 786464 | tf_op jit(solution)/shard_map/ppermute | solution.py:78
  176.7 16.3 %collective-permute-done.14 = bf16[256,1024]{1,0:T(8,128)(2,1)S(1)} collective-permute-done((bf16[256,1024]{1,0:T(8,128)(2,1)S(1)}, bf16[256,1024]{1,0:T(8,128)(2,1)S(1)}, u32[]{:S(2)}, u32[]{:S(2)}) %collective-permute-start.14) | collective-permute-done | bytes 524320 | tf_op jit(solution)/shard_map/ppermute | solution.py:78
  203.8 9.2 %fusion.7 = f32[2048,768]{1,0:T(8,128)S(1)} fusion(bf16[2048,768]{1,0:T(8,128)(2,1)} %constant_dynamic-update-slice_fusion.1, bf16[2048,2048]{1,0:T(8,128)(2,1)S(1)} %copy-done.27, f32[2048]{0:T(1024)S(1)} %constant_dynamic-update-slice_fusion.30, f32[2048]{0:T(1024)S(1)} %add_rsqrt_fusion), kind=kOutput, calls=%fused_computation.33 | convolution fusion | flops 6459228160 | bytes 17842176 | tf_op jit(solution)/shard_map/dot_general | solution.py:30
  230.5 14.3 %collective-permute-done.18 = bf16[256,1024]{1,0:T(8,128)(2,1)} collective-permute-done((bf16[256,1024]{1,0:T(8,128)(2,1)}, bf16[256,1024]{1,0:T(8,128)(2,1)}, u32[]{:S(2)}, u32[]{:S(2)}) %collective-permute-start.18) | collective-permute-done | bytes 524320 | tf_op jit(solution)/shard_map/ppermute | solution.py:78
  256.2 21.1 %all-to-all-done.2 = bf16[8,256,256]{2,1,0:T(8,128)(2,1)} async-done(((bf16[8,256,256]{2,1,0:T(8,128)(2,1)}), bf16[8,256,256]{2,1,0:T(8,128)(2,1)}, u32[]{:S(2)}, u32[]{:S(2)}) %all-to-all-start.2) | async-done | bytes 1048608 | tf_op jit(solution)/shard_map/all_to_all | solution.py:142
  293.1 7.6 collective-permute-done.21
  318.9 18.0 %collective-permute-done.24 = bf16[128,2048]{1,0:T(8,128)(2,1)S(1)} collective-permute-done((bf16[128,2048]{1,0:T(8,128)(2,1)S(1)}, bf16[128,2048]{1,0:T(8,128)(2,1)S(1)}, u32[]{:S(2)}, u32[]{:S(2)}) %collective-permute-start.24) | collective-permute-done | bytes 524320 | tf_op jit(solution)/shard_map/ppermute | solution.py:78
  336.9 8.1 collective-permute-done.25
  349.5 8.2 collective-permute-done.27
  360.2 14.4 %fusion.92 = f32[2048,1024]{1,0:T(8,128)} fusion(bf16[2048,2048]{1,0:T(8,128)(2,1)} %all-gather.12.cloned.1.call-done, bf16[2048,1024]{1,0:T(8,128)(2,1)} %constant_dynamic-update-slice_fusion.17), kind=kOutput, calls=%fused_computation.343 | convolution fusion | flops 8589934592 | bytes 20971520 | tf_op jit(solution)/shard_map/dot_general | solution.py:30
  374.6 34.0 %all-gather.10.cloned.1.call-done = bf16[2048,2048]{1,0:T(8,128)(2,1)} async-done(((bf16[256,2048]{1,0:T(8,128)(2,1)}), bf16[2048,2048]{1,0:T(8,128)(2,1)}) %all-gather.10.cloned.1.call-update) | async-done | bytes 8388624 | tf_op jit(solution)/shard_map/all_gather | solution.py:138
  408.6 14.1 %fusion.62 = f32[2048,1024]{1,0:T(8,128)} fusion(bf16[2048,2048]{1,0:T(8,128)(2,1)} %all-gather.10.cloned.1.call-done, bf16[256,2048]{1,0:T(8,128)(2,1)} %get-tuple-element.251, bf16[256,2048]{1,0:T(8,128)(2,1)} %get-tuple-element.252, bf16[256,2048]{1,0:T(8,128)(2,1)} %get-tuple-element.253, bf16[256,2048]{1,0:T(8,128)(2,1)S(1)} %get-tuple-element.250), kind=kOutput, calls=%fused_computation.140 | convolution fusion | flops 8606711808 | bytes 20971520 | tf_op jit(solution)/shard_map/dot_general | solution.py:40
  422.8 21.9 %multiply_convert_fusion = (bf16[2048,1024]{1,0:T(8,128)(2,1)}, bf16[2048,1024]{1,0:T(8,128)(2,1)}, bf16[2048,1024]{1,0:T(8,128)(2,1)}) fusion(f32[2048,1024]{1,0:T(8,128)} %fusion.92, f32[2048,1024]{1,0:T(8,128)} %fusion.62, bf16[2048,2048]{1,0:T(8,128)(2,1)} %all-gather.12.cloned.1.call-done, bf16[2048,1024]{1,0:T(8,128)(2,1)} %copy-done.65), kind=kOutput, calls=%fused_computation.6 | convolution fusion | flops 8621391872 | bytes 41943040 | tf_op jit(solution)/shard_map/dot_general | solution.py:30
  444.7 13.5 %convolution_convert_fusion = bf16[2048,2048]{1,0:T(8,128)(2,1)} fusion(bf16[2048,1024]{1,0:T(8,128)(2,1)} %get-tuple-element.151, bf16[256,2048]{1,0:T(8,128)(2,1)S(1)} %copy-done.53, bf16[256,2048]{1,0:T(8,128)(2,1)S(1)} %copy-done.54, bf16[256,2048]{1,0:T(8,128)(2,1)S(1)} %copy-done.55, bf16[256,2048]{1,0:T(8,128)(2,1)S(1)} %get-tuple-element.250), kind=kOutput, calls=%fused_computation.12 | convolution fusion | flops 8610906112 | bytes 16777216 | tf_op jit(solution)/shard_map/dot_general | solution.py:30
  458.3 12.7 %convolution_convert_fusion.1 = bf16[1024,2048]{1,0:T(8,128)(2,1)S(1)} fusion(bf16[2048,1024]{1,0:T(8,128)(2,1)} %get-tuple-element.151, bf16[2048,2048]{1,0:T(8,128)(2,1)} %all-gather.10.cloned.1.call-done), kind=kOutput, calls=%fused_computation.15 | convolution fusion | flops 8592031744 | bytes 16777216 | tf_op jit(solution)/shard_map/dot_general | solution.py:34
  477.8 10.9 %fusion.25 = f32[1024,2048]{1,0:T(8,128)} fusion(bf16[2048,1024]{1,0:T(8,128)(2,1)} %copy-done.65, bf16[256,1024]{1,0:T(8,128)(2,1)} %get-tuple-element.242, bf16[256,1024]{1,0:T(8,128)(2,1)} %get-tuple-element.243, bf16[256,1024]{1,0:T(8,128)(2,1)} %get-tuple-element.244, bf16[256,1024]{1,0:T(8,128)(2,1)} %get-tuple-element.245), kind=kOutput, calls=%fused_computation.55 | convolution fusion | flops 4303355904 | bytes 14680064 | tf_op jit(solution)/shard_map/dot_general | solution.py:40
  488.7 7.3 fusion.40
  496.0 11.9 %add_convert_fusion.1 = bf16[1024,2048]{1,0:T(8,128)(2,1)} fusion(f32[1024,2048]{1,0:T(8,128)} %fusion.25, bf16[2048,1024]{1,0:T(8,128)(2,1)} %constant_dynamic-update-slice_fusion.17, bf16[256,1024]{1,0:T(8,128)(2,1)} %get-tuple-element.308, bf16[256,1024]{1,0:T(8,128)(2,1)} %get-tuple-element.307, bf16[256,1024]{1,0:T(8,128)(2,1)} %get-tuple-element.306, ...), kind=kOutput, calls=%fused_computation.7 | convolution fusion | flops 4307550208 | bytes 18874368 | tf_op jit(solution)/shard_map/dot_general | solution.py:40
  507.9 11.8 %add_convert_fusion = bf16[1024,2048]{1,0:T(8,128)(2,1)} fusion(f32[1024,2048]{1,0:T(8,128)} %fusion.40, bf16[2048,1024]{1,0:T(8,128)(2,1)} %constant_dynamic-update-slice_fusion.17, bf16[256,1024]{1,0:T(8,128)(2,1)} %get-tuple-element.311, bf16[256,1024]{1,0:T(8,128)(2,1)S(1)} %get-tuple-element.310, bf16[256,1024]{1,0:T(8,128)(2,1)S(1)} %get-tuple-element.309, ...), kind=kOutput, calls=%fused_computation.5 | convolution fusion | flops 4307550208 | bytes 18874368 | tf_op jit(solution)/shard_map/dot_general | solution.py:40
  519.7 13.0 %convolution_convert_fusion.5 = bf16[2048,1024]{1,0:T(8,128)(2,1)} fusion(bf16[2048,2048]{1,0:T(8,128)(2,1)} %all-gather.12.cloned.1.call-done, bf16[2048,1024]{1,0:T(8,128)(2,1)S(1)} %copy-done.35), kind=kOutput, calls=%fused_computation.19 | convolution fusion | flops 8592031744 | bytes 16777216 | tf_op jit(solution)/shard_map/dot_general | solution.py:34
  541.6 11.6 %convolution_convert_fusion.4 = bf16[2048,1024]{1,0:T(8,128)(2,1)S(1)} fusion(bf16[2048,2048]{1,0:T(8,128)(2,1)} %all-gather.12.cloned.1.call-done, bf16[2048,1024]{1,0:T(8,128)(2,1)S(1)} %copy-done.34), kind=kOutput, calls=%fused_computation.18 | convolution fusion | flops 8592031744 | bytes 16777216 | tf_op jit(solution)/shard_map/dot_general | solution.py:34
  559.0 25.6 %collective-permute-done.33 = bf16[256,2048]{1,0:T(8,128)(2,1)S(1)} collective-permute-done((bf16[256,2048]{1,0:T(8,128)(2,1)S(1)}, bf16[256,2048]{1,0:T(8,128)(2,1)S(1)}, u32[]{:S(2)}, u32[]{:S(2)}) %collective-permute-start.33) | collective-permute-done | bytes 1048608 | tf_op jit(solution)/shard_map/ppermute | solution.py:78
  602.8 39.3 %collective-permute-done.36 = bf16[512,1024]{1,0:T(8,128)(2,1)} collective-permute-done((bf16[512,1024]{1,0:T(8,128)(2,1)}, bf16[512,1024]{1,0:T(8,128)(2,1)}, u32[]{:S(2)}, u32[]{:S(2)}) %collective-permute-start.36) | collective-permute-done | bytes 1048608 | tf_op jit(solution)/shard_map/ppermute | solution.py:78
  662.2 28.9 %all_to_all.35 = bf16[8,256,256]{2,1,0:T(8,128)(2,1)S(1)} all-to-all(bf16[8,256,256]{2,1,0:T(8,128)(2,1)S(1)} %bitcast.157), channel_id=1, replica_groups=mesh['h'=2,'l'=2,'y'=2,'x'=2,'c'=2] {'l','x','c'}, dimensions={0} | all-to-all | bytes 2097152 | tf_op jit(solution)/shard_map/all_to_all | solution.py:142
  710.8 9.1 convolution_convert_fusion.6
  731.5 43.2 %collective-permute-done.43 = bf16[512,1024]{1,0:T(8,128)(2,1)} collective-permute-done((bf16[512,1024]{1,0:T(8,128)(2,1)}, bf16[512,1024]{1,0:T(8,128)(2,1)}, u32[]{:S(2)}, u32[]{:S(2)}) %collective-permute-start.43) | collective-permute-done | bytes 1048608 | tf_op jit(solution)/shard_map/ppermute | solution.py:78
  792.1 24.6 %collective-permute-done.44 = bf16[1024,768]{1,0:T(8,128)(2,1)S(1)} collective-permute-done((bf16[1024,768]{1,0:T(8,128)(2,1)S(1)}, bf16[1024,768]{1,0:T(8,128)(2,1)S(1)}, u32[]{:S(2)}, u32[]{:S(2)}) %collective-permute-start.44) | collective-permute-done | bytes 1572896 | tf_op jit(solution)/shard_map/ppermute | solution.py:73
  846.5 7.9 collective-permute-done.47
  856.6 14.0 %collective-permute-done.46 = bf16[256,2048]{1,0:T(8,128)(2,1)} collective-permute-done((bf16[256,2048]{1,0:T(8,128)(2,1)}, bf16[256,2048]{1,0:T(8,128)(2,1)}, u32[]{:S(2)}, u32[]{:S(2)}) %collective-permute-start.46) | collective-permute-done | bytes 1048608 | tf_op jit(solution)/shard_map/ppermute | solution.py:73
  876.3 8.6 all-to-all-done.6
  (493 shorter events, 320.0 us)
Async XLA Ops:
  36.0 45.5 %all-to-all-start = ((bf16[8,64,768]{2,1,0:T(8,128)(2,1)}), bf16[8,64,768]{2,1,0:T(8,128)(2,1)}, u32[]{:S(2)}, u32[]{:S(2)}) async-start(bf16[8,64,768]{2,1,0:T(8,128)(2,1)} %get-tuple-element.113), calls=%async_computation | async-start | bytes 1572864 | tf_op jit(solution)/shard_map/all_to_all | solution.py:142
  40.3 155.4 %all-gather.6.cloned.1.call-start = ((), (), s32[]{:S(2)}) async-start(), calls=%async_computation.9 | async-start | bytes 9437184 | tf_op jit(solution)/shard_map/all_gather | solution.py:138
  43.5 38.0 %collective-permute-start.7 = (bf16[128,2048]{1,0:T(8,128)(2,1)}, bf16[128,2048]{1,0:T(8,128)(2,1)}, u32[]{:S(2)}, u32[]{:S(2)}) collective-permute-start(bf16[128,2048]{1,0:T(8,128)(2,1)} %get-tuple-element.281), channel_id=1, source_target_pairs={{16,0},{0,16},{17,1},{1,17},{18,2},{2,18},{19,3},{3,19},{20,4},{4,... | collective-permute-start | bytes 1572872 | tf_op jit(solution)/shard_map/ppermute | solution.py:78
  46.1 35.4 %collective-permute-start.8 = (bf16[128,2048]{1,0:T(8,128)(2,1)}, bf16[128,2048]{1,0:T(8,128)(2,1)}, u32[]{:S(2)}, u32[]{:S(2)}) collective-permute-start(bf16[128,2048]{1,0:T(8,128)(2,1)} %get-tuple-element.281), channel_id=1, source_target_pairs={{0,4},{4,0},{1,5},{5,1},{2,6},{6,2},{3,7},{7,3},{8,12},{12,8},{9,1... | collective-permute-start | bytes 1572872 | tf_op jit(solution)/shard_map/ppermute | solution.py:73
  81.5 78.5 %all-to-all-start.1 = ((bf16[8,64,2048]{2,1,0:T(8,128)(2,1)}), bf16[8,64,2048]{2,1,0:T(8,128)(2,1)}, u32[]{:S(2)}, u32[]{:S(2)}) async-start(bf16[8,64,2048]{2,1,0:T(8,128)(2,1)} %copy-done.9), calls=%async_computation.1 | async-start | bytes 4194304 | tf_op jit(solution)/shard_map/all_to_all | solution.py:142
  85.9 193.6 %all-gather.8.cloned.1.call-start = ((), (), s32[]{:S(2)}) async-start(), calls=%async_computation.10 | async-start | bytes 9437184 | tf_op jit(solution)/shard_map/all_gather | solution.py:138
  86.2 37.0 %collective-permute-start.10 = (bf16[512,768]{1,0:T(8,128)(2,1)}, bf16[512,768]{1,0:T(8,128)(2,1)}, u32[]{:S(2)}, u32[]{:S(2)}) collective-permute-start(bf16[512,768]{1,0:T(8,128)(2,1)} %bitcast.11), channel_id=1, source_target_pairs={{0,4},{4,0},{1,5},{5,1},{2,6},{6,2},{3,7},{7,3},{8,12},{12,8},{9,1... | collective-permute-start | bytes 2359304 | tf_op jit(solution)/shard_map/ppermute | solution.py:73
  86.7 73.4 %collective-permute-start.9 = (bf16[512,768]{1,0:T(8,128)(2,1)}, bf16[512,768]{1,0:T(8,128)(2,1)}, u32[]{:S(2)}, u32[]{:S(2)}) collective-permute-start(bf16[512,768]{1,0:T(8,128)(2,1)} %bitcast.11), channel_id=1, source_target_pairs={{16,0},{0,16},{17,1},{1,17},{18,2},{2,18},{19,3},{3,19},{20,4},{4,... | collective-permute-start | bytes 2359304 | tf_op jit(solution)/shard_map/ppermute | solution.py:78
  88.7 34.5 %collective-permute-start.12 = (bf16[128,2048]{1,0:T(8,128)(2,1)}, bf16[128,2048]{1,0:T(8,128)(2,1)}, u32[]{:S(2)}, u32[]{:S(2)}) collective-permute-start(bf16[128,2048]{1,0:T(8,128)(2,1)} %collective-permute-done.7), channel_id=1, source_target_pairs={{0,4},{4,0},{1,5},{5,1},{2,6},{6,2},{3,7},{7,3},{8,12},{12,8},{9,1... | collective-permute-start | bytes 1572872 | tf_op jit(solution)/shard_map/ppermute | solution.py:73
  251.0 109.2 %all-gather.12.cloned.1.call-start = ((), (), s32[]{:S(2)}) async-start(), calls=%async_computation.12 | async-start | bytes 9437184 | tf_op jit(solution)/shard_map/all_gather | solution.py:138
  251.6 49.1 %collective-permute-start.21 = (bf16[512,1024]{1,0:T(8,128)(2,1)}, bf16[512,1024]{1,0:T(8,128)(2,1)}, u32[]{:S(2)}, u32[]{:S(2)}) collective-permute-start(bf16[512,1024]{1,0:T(8,128)(2,1)} %slice.282), channel_id=1, source_target_pairs={{16,0},{0,16},{17,1},{1,17},{18,2},{2,18},{19,3},{3,19},{20,4},{4,... | collective-permute-start | bytes 3145736 | tf_op jit(solution)/shard_map/ppermute | solution.py:78
  254.2 46.5 %collective-permute-start.22 = (bf16[512,1024]{1,0:T(8,128)(2,1)}, bf16[512,1024]{1,0:T(8,128)(2,1)}, u32[]{:S(2)}, u32[]{:S(2)}) collective-permute-start(bf16[512,1024]{1,0:T(8,128)(2,1)} %slice.282), channel_id=1, source_target_pairs={{0,4},{4,0},{1,5},{5,1},{2,6},{6,2},{3,7},{7,3},{8,12},{12,8},{9,1... | collective-permute-start | bytes 3145736 | tf_op jit(solution)/shard_map/ppermute | solution.py:73
  255.9 37.3 %collective-permute-start.23 = (bf16[256,1024]{1,0:T(8,128)(2,1)}, bf16[256,1024]{1,0:T(8,128)(2,1)}, u32[]{:S(2)}, u32[]{:S(2)}) collective-permute-start(bf16[256,1024]{1,0:T(8,128)(2,1)} %collective-permute-done.18), channel_id=1, source_target_pairs={{0,4},{4,0},{1,5},{5,1},{2,6},{6,2},{3,7},{7,3},{8,12},{12,8},{9,1... | collective-permute-start | bytes 1572872 | tf_op jit(solution)/shard_map/ppermute | solution.py:73
  300.7 107.9 %all-gather.10.cloned.1.call-start = ((), (), s32[]{:S(2)}) async-start(), calls=%async_computation.11 | async-start | bytes 9437184 | tf_op jit(solution)/shard_map/all_gather | solution.py:138
  301.3 346.7 %reduce-scatter.5.cloned.1.call-start = ((), (), s32[]{:S(2)}) async-start(), calls=%async_computation.13 | async-start | bytes 9437184 | tf_op jit(solution)/shard_map/reduce_scatter | solution.py:496
  308.9 36.1 %collective-permute-start.26 = (bf16[512,1024]{1,0:T(8,128)(2,1)}, bf16[512,1024]{1,0:T(8,128)(2,1)S(1)}, u32[]{:S(2)}, u32[]{:S(2)}) collective-permute-start(bf16[512,1024]{1,0:T(8,128)(2,1)} %collective-permute-done.21), channel_id=1, source_target_pairs={{0,4},{4,0},{1,5},{5,1},{2,6},{6,2},{3,7},{7,3},{8,12},{12,8},{9,1... | collective-permute-start | bytes 3145736 | tf_op jit(solution)/shard_map/ppermute | solution.py:73
  458.2 261.7 %all-gather.14.cloned.1.call-start = ((), (), s32[]{:S(2)}) async-start(), calls=%async_computation.14 | async-start | bytes 9437184 | tf_op jit(solution)/shard_map/all_gather | solution.py:138
  472.5 60.3 %collective-permute-start.28 = (bf16[512,2048]{1,0:T(8,128)(2,1)S(1)}, bf16[512,2048]{1,0:T(8,128)(2,1)S(1)}, u32[]{:S(2)}, u32[]{:S(2)}) collective-permute-start(bf16[512,2048]{1,0:T(8,128)(2,1)S(1)} %slice.313), channel_id=1, source_target_pairs={{0,4},{4,0},{1,5},{5,1},{2,6},{6,2},{3,7},{7,3},{8,12},{12,8},{9,1... | collective-permute-start | bytes 6291464 | tf_op jit(solution)/shard_map/ppermute | solution.py:73
  535.8 48.9 %collective-permute-start.33 = (bf16[256,2048]{1,0:T(8,128)(2,1)S(1)}, bf16[256,2048]{1,0:T(8,128)(2,1)S(1)}, u32[]{:S(2)}, u32[]{:S(2)}) collective-permute-start(bf16[256,2048]{1,0:T(8,128)(2,1)S(1)} %slice.319), channel_id=1, source_target_pairs={{16,0},{0,16},{17,1},{1,17},{18,2},{2,18},{19,3},{3,19},{20,4},{4,... | collective-permute-start | bytes 3145736 | tf_op jit(solution)/shard_map/ppermute | solution.py:78
  540.0 47.7 %collective-permute-start.32 = (bf16[1024,1024]{1,0:T(8,128)(2,1)S(1)}, bf16[1024,1024]{1,0:T(8,128)(2,1)S(1)}, u32[]{:S(2)}, u32[]{:S(2)}) collective-permute-start(bf16[1024,1024]{1,0:T(8,128)(2,1)S(1)} %slice.317), channel_id=1, source_target_pairs={{0,4},{4,0},{1,5},{5,1},{2,6},{6,2},{3,7},{7,3},{8,12},{12,8},{9,1... | collective-permute-start | bytes 6291464 | tf_op jit(solution)/shard_map/ppermute | solution.py:73
  556.8 35.4 %collective-permute-start.30 = (bf16[128,2048]{1,0:T(8,128)(2,1)S(1)}, bf16[128,2048]{1,0:T(8,128)(2,1)S(1)}, u32[]{:S(2)}, u32[]{:S(2)}) collective-permute-start(bf16[128,2048]{1,0:T(8,128)(2,1)S(1)} %get-tuple-element.278), channel_id=1, source_target_pairs={{0,8},{8,0},{1,9},{9,1},{2,10},{10,2},{3,11},{11,3},{4,12},{12,4},... | collective-permute-start | bytes 1572872 | tf_op jit(solution)/shard_map/ppermute | solution.py:73
  593.9 50.8 %collective-permute-start.37 = (bf16[1024,1024]{1,0:T(8,128)(2,1)}, bf16[1024,1024]{1,0:T(8,128)(2,1)}, u32[]{:S(2)}, u32[]{:S(2)}) collective-permute-start(bf16[1024,1024]{1,0:T(8,128)(2,1)} %slice.323), channel_id=1, source_target_pairs={{0,4},{4,0},{1,5},{5,1},{2,6},{6,2},{3,7},{7,3},{8,12},{12,8},{9,1... | collective-permute-start | bytes 6291464 | tf_op jit(solution)/shard_map/ppermute | solution.py:73
  595.4 46.7 %collective-permute-start.36 = (bf16[512,1024]{1,0:T(8,128)(2,1)}, bf16[512,1024]{1,0:T(8,128)(2,1)}, u32[]{:S(2)}, u32[]{:S(2)}) collective-permute-start(bf16[512,1024]{1,0:T(8,128)(2,1)} %slice.321), channel_id=1, source_target_pairs={{16,0},{0,16},{17,1},{1,17},{18,2},{2,18},{19,3},{3,19},{20,4},{4,... | collective-permute-start | bytes 3145736 | tf_op jit(solution)/shard_map/ppermute | solution.py:78
  600.3 47.7 %collective-permute-start.34 = (bf16[256,2048]{1,0:T(8,128)(2,1)S(1)}, bf16[256,2048]{1,0:T(8,128)(2,1)}, u32[]{:S(2)}, u32[]{:S(2)}) collective-permute-start(bf16[256,2048]{1,0:T(8,128)(2,1)S(1)} %get-tuple-element.228), channel_id=1, source_target_pairs={{0,2},{2,0},{1,3},{3,1},{4,6},{6,4},{5,7},{7,5},{8,10},{10,8},{9,1... | collective-permute-start | bytes 3145736 | tf_op jit(solution)/shard_map/ppermute | solution.py:73
  602.4 45.6 %collective-permute-start.35 = (bf16[256,2048]{1,0:T(8,128)(2,1)S(1)}, bf16[256,2048]{1,0:T(8,128)(2,1)}, u32[]{:S(2)}, u32[]{:S(2)}) collective-permute-start(bf16[256,2048]{1,0:T(8,128)(2,1)S(1)} %get-tuple-element.227), channel_id=1, source_target_pairs={{0,8},{8,0},{1,9},{9,1},{2,10},{10,2},{3,11},{11,3},{4,12},{12,4},... | collective-permute-start | bytes 3145736 | tf_op jit(solution)/shard_map/ppermute | solution.py:73
  655.9 175.8 %reduce-scatter.7.cloned.1.call-start = ((), (), s32[]{:S(2)}) async-start(), calls=%async_computation.15 | async-start | bytes 163840
  719.9 68.2 %collective-permute-start.40 = (bf16[1024,2048]{1,0:T(8,128)(2,1)}, bf16[1024,2048]{1,0:T(8,128)(2,1)}, u32[]{:S(2)}, u32[]{:S(2)}) collective-permute-start(bf16[1024,2048]{1,0:T(8,128)(2,1)} %convolution_convert_fusion.3), channel_id=1, source_target_pairs={{0,1},{1,0},{2,3},{3,2},{4,5},{5,4},{6,7},{7,6},{8,9},{9,8},{10,11... | collective-permute-start | bytes 12582920 | tf_op jit(solution)/shard_map/ppermute | solution.py:73
  722.3 52.4 %collective-permute-start.43 = (bf16[512,1024]{1,0:T(8,128)(2,1)}, bf16[512,1024]{1,0:T(8,128)(2,1)}, u32[]{:S(2)}, u32[]{:S(2)}) collective-permute-start(bf16[512,1024]{1,0:T(8,128)(2,1)} %slice.339), channel_id=1, source_target_pairs={{16,0},{0,16},{17,1},{1,17},{18,2},{2,18},{19,3},{3,19},{20,4},{4,... | collective-permute-start | bytes 3145736 | tf_op jit(solution)/shard_map/ppermute | solution.py:78
  727.7 105.4 %all-to-all-start.5 = ((bf16[8,64,1024]{2,1,0:T(8,128)(2,1)}), bf16[8,64,1024]{2,1,0:T(8,128)(2,1)S(1)}, u32[]{:S(2)}, u32[]{:S(2)}) async-start(bf16[8,64,1024]{2,1,0:T(8,128)(2,1)} %bitcast.154), calls=%async_computation.6 | async-start | bytes 2097152 | tf_op jit(solution)/shard_map/all_to_all | solution.py:142
  777.7 39.1 %collective-permute-start.44 = (bf16[1024,768]{1,0:T(8,128)(2,1)S(1)}, bf16[1024,768]{1,0:T(8,128)(2,1)S(1)}, u32[]{:S(2)}, u32[]{:S(2)}) collective-permute-start(bf16[1024,768]{1,0:T(8,128)(2,1)S(1)} %slice.341), channel_id=1, source_target_pairs={{0,4},{4,0},{1,5},{5,1},{2,6},{6,2},{3,7},{7,3},{8,12},{12,8},{9,1... | collective-permute-start | bytes 4718600 | tf_op jit(solution)/shard_map/ppermute | solution.py:73
  827.3 43.2 %collective-permute-start.46 = (bf16[256,2048]{1,0:T(8,128)(2,1)}, bf16[256,2048]{1,0:T(8,128)(2,1)}, u32[]{:S(2)}, u32[]{:S(2)}) collective-permute-start(bf16[256,2048]{1,0:T(8,128)(2,1)} %get-tuple-element.224), channel_id=1, source_target_pairs={{0,8},{8,0},{1,9},{9,1},{2,10},{10,2},{3,11},{11,3},{4,12},{12,4},... | collective-permute-start | bytes 3145736 | tf_op jit(solution)/shard_map/ppermute | solution.py:73
  841.4 43.5 %all-to-all-start.6 = ((bf16[8,64,1024]{2,1,0:T(8,128)(2,1)}), bf16[8,64,1024]{2,1,0:T(8,128)(2,1)S(1)}, u32[]{:S(2)}, u32[]{:S(2)}) async-start(bf16[8,64,1024]{2,1,0:T(8,128)(2,1)} %bitcast.155), calls=%async_computation.7 | async-start | bytes 2097152 | tf_op jit(solution)/shard_map/all_to_all | solution.py:142
  (129 other events, 1648.1 us)
Sparse Core Ops, SparseCore 0:
  81.7 82.2 all-gather.5
  166.1 53.7 all-gather.7
  300.9 59.3 all-gather.11
  361.7 46.9 all-gather.9
  458.3 85.8 reduce-scatter.4
  656.0 57.0 all-gather.13
  727.8 40.8 reduce-scatter.6

commit v3 on v1

v3 whole, which is shorter than its diff:
```python
import functools

import jax
import jax.numpy as jnp
from jax import lax
from jax.experimental import pallas as pl
from jax.experimental.pallas import tpu as pltpu
from jax.sharding import Mesh
from jax.sharding import PartitionSpec as P

SEQ_BASE = 8192
STEP = 10

EPS_NORM = 1e-05
BETA_ONE = 0.9
BETA_TWO = 0.95
ADAM_EPS = 1e-08
DECAY_RATE = 0.1
RATE_MATRIX = 0.01
RATE_VECTOR = 0.3

AXES = ("p", "y", "x", "c")
PLANE = ("y", "x", "c")
LOW = jnp.bfloat16
F32 = jnp.float32


def forward_dot(operand, partner):
    return jnp.dot(operand, partner, preferred_element_type=jnp.float32)


def over_tokens(operand, partner):
    return lax.dot_general(
        operand, partner, (((0,), (0,)), ((), ())), preferred_element_type=jnp.float32
    )


def against_rows(operand, partner):
    return lax.dot_general(
        operand, partner, (((1,), (1,)), ((), ())), preferred_element_type=jnp.float32
    )


def rms_parts(values):
    scale = lax.rsqrt(jnp.mean(values * values, axis=-1, keepdims=True) + EPS_NORM)
    return (scale, values * scale)


def norm_back(upstream, normal, scale, gain):
    scaled = upstream * gain
    return scale * (scaled - normal * jnp.mean(scaled * normal, axis=-1, keepdims=True))


def adamw(weight, first, second, grad, rate, decay):
    first_new = BETA_ONE * first + (1.0 - BETA_ONE) * grad
    second_new = BETA_TWO * second + (1.0 - BETA_TWO) * grad * grad
    fix_one = 1.0 - BETA_ONE**STEP
    fix_two = 1.0 - BETA_TWO**STEP
    stepped = first_new / fix_one / (jnp.sqrt(second_new / fix_two) + ADAM_EPS)
    return (first_new, second_new, weight - rate * (stepped + decay * weight))


def after(value, *others):
    return lax.optimization_barrier((value, *others))[0]


def together(*values):
    return lax.optimization_barrier(values)


def swap(block, axis):
    return lax.ppermute(block, axis, [(0, 1), (1, 0)])


def along(block, distance):
    count = lax.axis_size("p")
    route = [(i - distance, i) for i in range(count) if 0 <= i - distance < count]
    return lax.ppermute(block, "p", route)


def over(block, axis):
    other = swap(block, axis)
    first = lax.axis_index(axis) == 0
    return jnp.stack([jnp.where(first, block, other), jnp.where(first, other, block)])


def over_planes(block):
    count = lax.axis_size("p")
    if count > 4:
        return lax.all_gather(block, "p", axis=0, tiled=False)
    pieces = [block]
    for distance in range(1, count):
        route = [((i + distance) % count, i) for i in range(count)]
        pieces.append(lax.ppermute(block, "p", route))
    return jnp.roll(jnp.stack(pieces), lax.axis_index("p"), axis=0)


def plane_blocks(block):
    half = block.shape[0] // 2
    by_x, by_y = swap(block, "x"), swap(block, "y")
    own_far = swap(block, "c")
    corner = jnp.concatenate([swap(by_x[:half], "y"), swap(by_y[half:], "x")], axis=0)
    near = [block, by_x, by_y, corner]
    return near, [own_far] + [swap(piece, "c") for piece in near[1:]]


def plane_gather(block):
    rows = block.shape[0]
    mine_y, mine_x, mine_c = (lax.axis_index(axis) for axis in PLANE)
    out = jnp.zeros((8 * rows, block.shape[1]), block.dtype)
    for dc, pieces in enumerate(plane_blocks(block)):
        for k, piece in enumerate(pieces):
            at = ((mine_y ^ (k >> 1)) * 2 + (mine_x ^ (k & 1))) * 2 + (mine_c ^ dc)
            out = lax.dynamic_update_slice_in_dim(out, piece, at * rows, axis=0)
    return out


def plane_gather_here(block):
    near, far = plane_blocks(block)
    return jnp.concatenate(near + far, axis=0)


def plane_exchange(blocks):
    return lax.all_to_all(blocks, PLANE, split_axis=0, concat_axis=0, tiled=True)


def core_rows(array, own):
    core = lax.axis_index("c") if own else 1 - lax.axis_index("c")
    rows = array.shape[0] // 8
    return jnp.concatenate(
        [lax.dynamic_slice_in_dim(array, (2 * i + core) * rows, rows, axis=0) for i in range(4)],
        axis=0,
    )


def plane_corner(near, got, here=False):
    quarter = near.shape[0] // 4
    half = quarter // 2
    mine_y, mine_x = lax.axis_index("y"), lax.axis_index("x")

    def block(dy, dx):
        if here:
            place = 2 * dy + dx
            return tuple(part[place * quarter : (place + 1) * quarter] for part in (near, got))
        place = (mine_y ^ dy) * 2 + (mine_x ^ dx)
        return tuple(
            lax.dynamic_slice_in_dim(part, place * quarter, quarter, axis=0) for part in (near, got)
        )

    corner = sum(block(1, 1))
    return swap(corner[:half], "y"), swap(corner[half:], "x"), block


def plane_settle(from_y, from_x, block):
    near_x, got_x = block(0, 1)
    near_y, got_y = block(1, 0)
    by_x = near_x + got_x + jnp.concatenate([from_y, jnp.zeros_like(from_y)], axis=0)
    by_y = near_y + got_y + jnp.concatenate([jnp.zeros_like(from_x), from_x], axis=0)
    return sum(block(0, 0)), swap(by_x, "x"), swap(by_y, "y")


def planes_gather(block):
    return lax.all_gather(block, "p", axis=0, tiled=True)


def planes_scatter(term):
    return lax.psum_scatter(term, "p", scatter_dimension=0, tiled=True)


def shifted(block, distance):
    count = lax.axis_size("p")
    return lax.ppermute(block, "p", [((i + distance) % count, i) for i in range(count)])


def planes_gather_small(block):
    count = lax.axis_size("p")
    if count > 4:
        return planes_gather(block)
    pieces = jnp.stack([block] + [shifted(block, i) for i in range(1, count)])
    mine = lax.axis_index("p")
    picked = [
        lax.dynamic_index_in_dim(pieces, (i - mine) % count, axis=0, keepdims=False)
        for i in range(count)
    ]
    return jnp.concatenate(picked, axis=0)


def planes_scatter_small(term):
    count = lax.axis_size("p")
    if count > 4:
        return planes_scatter(term)
    rows = term.shape[0] // count
    mine = lax.axis_index("p")
    total = lax.dynamic_slice_in_dim(term, mine * rows, rows, axis=0).astype(F32)
    for i in range(1, count):
        piece = lax.dynamic_slice_in_dim(term, (mine - i) % count * rows, rows, axis=0)
        total = total + shifted(piece, i).astype(F32)
    return total


def half_body(rows_ref, upstream_ref, both_ref, down_ref, hidden_out, grads_out):
    both = forward_dot(rows_ref[...], both_ref[...])
    half = both.shape[1] // 2
    gate_value, up_value = both[:, :half], both[:, half:]
    sigmoid_gate = jax.nn.sigmoid(gate_value)
    silu_gate = gate_value * sigmoid_gate
    hidden_out[...] = (silu_gate * up_value).astype(LOW)
    hidden_grad = against_rows(upstream_ref[...], down_ref[...])
    gate_grad = hidden_grad * up_value * sigmoid_gate * (1.0 + gate_value * (1.0 - sigmoid_gate))
    grads_out[:, :half] = gate_grad.astype(LOW)
    grads_out[:, half:] = (hidden_grad * silu_gate).astype(LOW)


def half_ffn(rows, upstream, both, down):
    count, d = rows.shape
    half = both.shape[1] // 2
    tile = 512
    return pl.pallas_call(
        half_body,
        grid=(count // tile,),
        in_specs=[
            pl.BlockSpec((tile, d), lambda i: (i, 0)),
            pl.BlockSpec((tile, d), lambda i: (i, 0)),
            pl.BlockSpec(both.shape, lambda i: (0, 0)),
            pl.BlockSpec(down.shape, lambda i: (0, 0)),
        ],
        out_specs=[
            pl.BlockSpec((tile, half), lambda i: (i, 0)),
            pl.BlockSpec((tile, 2 * half), lambda i: (i, 0)),
        ],
        out_shape=[
            jax.ShapeDtypeStruct((count, half), LOW),
            jax.ShapeDtypeStruct((count, 2 * half), LOW),
        ],
        compiler_params=pltpu.CompilerParams(vmem_limit_bytes=48 * 2**20),
        cost_estimate=pl.CostEstimate(
            flops=6 * count * d * half, transcendentals=count * half, bytes_accessed=4 * count * d + 6 * d * half
        ),
    )(rows, upstream, both, down)


def pair_body(turned, a_ref, b_ref, c_ref, e_ref, out_ref):
    dot = against_rows if turned else forward_dot
    out_ref[...] = (dot(a_ref[...], c_ref[...]) + dot(b_ref[...], e_ref[...])).astype(LOW)


def pair_dot(first, second, first_weight, second_weight, far, turned):
    count, depth = first.shape
    width = first_weight.shape[0 if turned else 1]
    tile = 512
    steps = count // 2 // tile
    rows = pl.BlockSpec((tile, depth), lambda i: (i + (steps if far else 0), 0))
    whole = pl.BlockSpec(first_weight.shape, lambda i: (0, 0))
    return pl.pallas_call(
        functools.partial(pair_body, turned),
        grid=(steps,),
        in_specs=[rows, rows, whole, whole],
        out_specs=pl.BlockSpec((tile, width), lambda i: (i, 0)),
        out_shape=jax.ShapeDtypeStruct((count // 2, width), LOW),
        compiler_params=pltpu.CompilerParams(vmem_limit_bytes=48 * 2**20),
        cost_estimate=pl.CostEstimate(
            flops=2 * count * depth * width, transcendentals=0, bytes_accessed=2 * count * (depth + width // 2) + 4 * depth * width
        ),
    )(first, second, first_weight, second_weight)


def pack_body(count, inward_ref, gate_ref, up_ref, inward_out, ffn_out):
    d_rows = inward_ref.shape[1] // (24 * count)
    ff_rows = gate_ref.shape[1] // (8 * count)
    feats, units, width = count * d_rows, count * ff_rows, ff_rows // 2
    for p in range(count):
        for to in range(8):
            at = (p * 8 + to) * ff_rows
            for half in range(2):
                for kind, ref in enumerate((gate_ref, up_ref)):
                    lane = (half * 2 + kind) * units // 2 + p * width
                    block = ref[:, at + half * width : at + (half + 1) * width]
                    ffn_out[to, :, lane : lane + width] = block.astype(LOW)
    for part in range(3):
        for to in range(8):
            blocks = []
            for p in range(count):
                at = ((part * count + p) * 8 + to) * d_rows
                blocks.append(inward_ref[:, at : at + d_rows])
            block = jnp.concatenate(blocks, axis=1).astype(LOW)
            inward_out[to, :, part * feats : (part + 1) * feats] = block


def packed(inward, gate, up, count):
    d_rows, ff = gate.shape
    feats, units = inward.shape[1] // 24, ff // 8
    if d_rows % 64 or units % (256 * count):
        sent = inward.astype(LOW).reshape(d_rows, 3, count, 8, -1)
        sent = sent.transpose(3, 0, 1, 2, 4).reshape(8, d_rows, 3 * feats)
        both = jnp.stack([gate.astype(LOW), up.astype(LOW)], axis=1)
        both = both.reshape(d_rows, 2, count, 8, 2, -1).transpose(3, 0, 4, 1, 2, 5)
        return sent, both.reshape(8, d_rows, 2 * units)
    rows = 16
    return pl.pallas_call(
        functools.partial(pack_body, count),
        grid=(d_rows // rows,),
        in_specs=[
            pl.BlockSpec((rows, 24 * feats), lambda i: (i, 0)),
            pl.BlockSpec((rows, ff), lambda i: (i, 0)),
            pl.BlockSpec((rows, ff), lambda i: (i, 0)),
        ],
        out_specs=[
            pl.BlockSpec((8, rows, 3 * feats), lambda i: (0, i, 0)),
            pl.BlockSpec((8, rows, 2 * units), lambda i: (0, i, 0)),
        ],
        out_shape=[
            jax.ShapeDtypeStruct((8, d_rows, 3 * feats), LOW),
            jax.ShapeDtypeStruct((8, d_rows, 2 * units), LOW),
        ],
        compiler_params=pltpu.CompilerParams(vmem_limit_bytes=32 * 2**20),
        cost_estimate=pl.CostEstimate(
            flops=0, transcendentals=0, bytes_accessed=6 * d_rows * (24 * feats + 2 * ff)
        ),
    )(inward, gate, up)


def update_body(parts, width, pieces, *refs):
    got_refs = refs[:parts]
    weight_ref, first_ref, second_ref, first_out, second_out, weight_out, dot_out = refs[parts:]

    @pl.when(pl.program_id(0) == 0)
    def _():
        dot_out[...] = jnp.zeros_like(dot_out)

    total = jnp.zeros((weight_ref.shape[0], 128), F32)
    joined = 128 // width
    for group in range(0, len(pieces), joined):
        grad = [
            got_refs[which][tuple(at)][:, lane : lane + width].astype(F32)
            for which, *at, lane in pieces[group : group + joined]
        ]
        grad = jnp.concatenate(grad, axis=1) if joined > 1 else grad[0]
        here = slice(group * width, group * width + 128)
        weight = weight_ref[:, here]
        first, second, updated = adamw(
            weight, first_ref[:, here], second_ref[:, here], grad, RATE_MATRIX, DECAY_RATE
        )
        first_out[:, here] = first
        second_out[:, here] = second
        weight_out[:, here] = updated
        total += weight.astype(LOW).astype(F32) * grad
    dot_out[...] += total


def update_call(grid, got, got_specs, width, pieces, weight, first, second):
    rows, columns = weight.shape
    spec = pl.BlockSpec((rows, columns // grid), lambda k: (0, k))
    shape = jax.ShapeDtypeStruct(weight.shape, F32)
    *new, dots = pl.pallas_call(
        functools.partial(update_body, len(got), width, pieces),
        grid=(grid,),
        in_specs=[*got_specs, spec, spec, spec],
        out_specs=[spec, spec, spec, pl.BlockSpec((rows, 128), lambda k: (0, 0))],
        out_shape=[shape, shape, shape, jax.ShapeDtypeStruct((rows, 128), F32)],
        compiler_params=pltpu.CompilerParams(vmem_limit_bytes=32 * 2**20),
        cost_estimate=pl.CostEstimate(
            flops=20 * rows * columns, transcendentals=2 * rows * columns, bytes_accessed=26 * rows * columns
        ),
    )(*got, weight, first, second)
    return tuple(new), jnp.sum(dots, axis=1)


def updated_plainly(grad, weight, first, second):
    grad = grad.reshape(weight.shape).astype(F32)
    new = adamw(weight, first, second, grad, RATE_MATRIX, DECAY_RATE)
    return new, jnp.sum(weight.astype(LOW).astype(F32) * grad, axis=1)


def updated_inward(got, weight, first, second, count):
    rows, columns = weight.shape
    width = columns // (24 * count)
    if width % 64 or rows % 16:
        grad = got.reshape(8, rows, 3, count, width).transpose(1, 2, 3, 0, 4)
        return updated_plainly(grad, weight, first, second)
    spec = pl.BlockSpec((8, rows, count * width), lambda k: (0, 0, k))
    pieces = [(0, to, p * width) for p in range(count) for to in range(8)]
    return update_call(3, [got], [spec], width, pieces, weight, first, second)


def updated_ffn(got, kind, weight, first, second, count):
    rows, columns = weight.shape
    width = columns // (16 * count)
    if width % 128 or rows % 16:
        grad = jnp.stack(got).reshape(2, 8, rows, 2, count, width)[:, :, :, kind]
        return updated_plainly(grad.transpose(2, 3, 1, 0, 4), weight, first, second)
    spec = pl.BlockSpec((4, rows, width), lambda k: (k % 2, 0, kind * count + k // 2))
    pieces = [
        (half, q, lane) for q in range(4) for half in range(2) for lane in range(0, width, 128)
    ]
    return update_call(2 * count, got, [spec, spec], 128, pieces, weight, first, second)


def on_device(
    block_input,
    cotangent,
    inward_weight,
    inward_first,
    inward_second,
    outward_weight,
    outward_first,
    outward_second,
    gate_weight,
    gate_first,
    gate_second,
    up_weight,
    up_first,
    up_second,
    down_weight,
    down_first,
    down_second,
    norm_gains,
    gains_first,
    gains_second,
    conv_taps,
    taps_first,
    taps_second,
):
    count = lax.axis_size("p")
    tok_rows, d = block_input.shape
    d_rows = inward_weight.shape[0]
    ff = gate_weight.shape[1]
    ff_rows = down_weight.shape[0]
    plane_rows = 8 * tok_rows
    near_rows = 4 * tok_rows
    seq_len = min(SEQ_BASE, plane_rows * count)
    feats = d // 8
    units = ff // 8
    half = units // 2
    place = lax.axis_index(PLANE)

    down_low = down_weight.astype(LOW)
    block_here, outward_here, small = together(
        block_input, outward_weight, jnp.concatenate([norm_gains, conv_taps], axis=0), down_low
    )[:3]
    outward_low = outward_here.astype(LOW)
    down_a, down_b = down_low[: ff_rows // 2], down_low[ff_rows // 2 :]
    down_parts = [planes_gather(down_a)]
    inward_sent, ffn_sent = packed(after(inward_weight, down_low), gate_weight, up_weight, count)
    inward_got = plane_exchange(inward_sent).reshape(8 * d_rows, 3 * feats)
    inward_got, first_down = together(inward_got, down_parts[0])
    down_parts = [first_down]
    inward_part = planes_gather(inward_got)
    ffn_got = plane_exchange(after(ffn_sent, inward_got)).reshape(8 * d_rows, 2 * units)
    ffn_parts = [planes_gather(ffn_got[:, :units])]
    inputs_low = plane_gather(block_here)
    small = over(over(over(over_planes(small.astype(LOW)), "c"), "x"), "y").transpose(3, 0, 1, 2, 4, 5)
    outward_part = planes_gather_small(outward_low)
    inputs_low, small, outward_part, ffn_got = together(inputs_low, small, outward_part, ffn_got)
    upstream = plane_gather_here(after(cotangent, inputs_low))
    outward_full = plane_gather(after(outward_part, upstream))
    small = small.astype(F32)
    gain_one = small[..., 0, :].reshape(d)
    gain_two = small[..., 1, :].reshape(d)
    taps_here = lax.dynamic_index_in_dim(
        small.reshape(count, 8, 5, d_rows), place, axis=1, keepdims=False
    )
    taps_here = taps_here[:, 2:].transpose(1, 0, 2).reshape(3, feats)
    tap_zero, tap_one, tap_two = taps_here[0], taps_here[1], taps_here[2]

    _, normed_one = rms_parts(inputs_low.astype(F32))
    normed_one = (normed_one * gain_one).astype(LOW)
    mixed = forward_dot(normed_one, inward_part)
    b_part = mixed[:, :feats]
    c_part = mixed[:, feats : 2 * feats]
    x_part = mixed[:, 2 * feats :]
    gated = b_part * x_part
    starts_here = lax.axis_index("p") * plane_rows % seq_len == 0
    before = jnp.where(starts_here, 0.0, along(gated[plane_rows - 2 :], 1))
    extended = jnp.concatenate([before, gated], axis=0)
    convolved = (
        tap_zero * extended[:plane_rows]
        + tap_one * extended[1 : plane_rows + 1]
        + tap_two * extended[2:]
    )
    branch_feats = (c_part * convolved).astype(LOW)
    branch_got = plane_exchange(branch_feats.reshape(8, tok_rows, feats))
    branch_in = branch_got.transpose(1, 0, 2).reshape(tok_rows, d)
    branch_in, down_b, ffn_b = together(branch_in, down_b, ffn_got[:, units:])
    down_parts += [planes_gather(down_b)]
    ffn_parts += [planes_gather(ffn_b)]
    inputs = block_input.astype(F32)
    middle = inputs + forward_dot(branch_in, outward_full)
    scale_two, normal_two = rms_parts(middle)
    normed_two = plane_gather_here((normal_two * gain_two).astype(LOW))

    def terms_of(hidden, grads):
        return over_tokens(hidden, upstream).astype(LOW), over_tokens(normed_two, grads).astype(LOW)

    hidden_a, grads_a = half_ffn(normed_two, upstream, ffn_parts[0], down_parts[0])
    down_term, both_term = terms_of(hidden_a, grads_a)
    down_own, both_own = [planes_scatter(down_term)], [planes_scatter(both_term)]
    ffn_b, down_b, _, _ = together(ffn_parts[1], down_parts[1], down_term, both_term)
    hidden_b, grads_b = half_ffn(normed_two, upstream, ffn_b, down_b)
    far = pair_dot(grads_a, grads_b, ffn_parts[0], ffn_b, True, True)
    got = swap(far, "c")
    near = pair_dot(grads_a, grads_b, ffn_parts[0], ffn_b, False, True)
    got, near, hidden_b, grads_b = together(got, near, hidden_b, grads_b)
    from_y, from_x, block = plane_corner(near, got, True)
    both_term = over_tokens(normed_two, grads_b).astype(LOW)
    from_y, from_x, both_term = together(from_y, from_x, both_term)
    both_own += [planes_scatter(both_term)]
    down_term = over_tokens(hidden_b, upstream).astype(LOW)
    result_far = pair_dot(hidden_a, hidden_b, down_parts[0], down_b, True, False)
    *parts, down_term, result_far = together(
        *plane_settle(from_y, from_x, block), down_term, result_far
    )
    normed_two_grad = sum(part.astype(F32) for part in parts)

    result_got = swap(result_far, "c")
    result_near = pair_dot(hidden_a, hidden_b, down_parts[0], down_b, False, False)
    middle_grad = cotangent.astype(F32) + norm_back(
        normed_two_grad, normal_two, scale_two, gain_two
    )
    branch_grad = middle_grad.astype(LOW)
    branch_in_grad = against_rows(branch_grad, outward_full).astype(LOW)

    def outward_rows(own):
        core = lax.axis_index("c") if own else 1 - lax.axis_index("c")
        split = branch_got.reshape(4, 2, tok_rows, feats)
        part = lax.dynamic_index_in_dim(split, core, axis=1, keepdims=False)
        term = lax.dot_general(
            part, branch_grad, (((1,), (0,)), ((), ())), preferred_element_type=jnp.float32
        )
        return term.astype(LOW).reshape(d // 2, d)

    outward_far = outward_rows(False)
    branch_in_grad, result_got, result_near, outward_far = together(
        branch_in_grad, result_got, result_near, outward_far
    )
    branch_in_grad = plane_exchange(branch_in_grad.reshape(tok_rows, 8, feats).transpose(1, 0, 2))
    result_y, result_x, result_block = plane_corner(result_near, result_got, True)
    outward_got, outward_near = swap(outward_far, "c"), outward_rows(True)
    branch_in_grad, result_y, result_x, outward_got, outward_near = together(
        branch_in_grad, result_y, result_x, outward_got, outward_near
    )
    result_parts = plane_settle(result_y, result_x, result_block)
    outward_y, outward_x, outward_block = plane_corner(outward_near, outward_got)
    branch_in_grad = branch_in_grad.reshape(plane_rows, feats).astype(F32)
    c_grad = branch_in_grad * convolved
    conv_grad = branch_in_grad * c_part
    ext_grad = (
        jnp.pad(tap_zero * conv_grad, ((0, 2), (0, 0)))
        + jnp.pad(tap_one * conv_grad, ((1, 1), (0, 0)))
        + jnp.pad(tap_two * conv_grad, ((2, 0), (0, 0)))
    )
    tap_grads = jnp.stack(
        [
            jnp.sum(conv_grad * extended[offset : offset + plane_rows], axis=0)
            for offset in range(3)
        ],
        axis=1,
    )
    returned = along(jnp.where(starts_here, 0.0, ext_grad[:2]), -1)
    gated_grad = ext_grad[2:] + jnp.pad(returned, ((plane_rows - 2, 0), (0, 0)))
    mixed_grad = jnp.concatenate([gated_grad * x_part, c_grad, gated_grad * b_part], axis=1)
    mixed_grad = mixed_grad.astype(LOW)
    inward_term = over_tokens(normed_one, mixed_grad).astype(LOW)
    inward_term, mixed_grad, outward_y, outward_x, down_own[0], both_own[0], *result_parts = together(
        inward_term, mixed_grad, outward_y, outward_x, down_own[0], both_own[0], *result_parts
    )
    inward_own = planes_scatter(inward_term)
    block_output = (middle + sum(part.astype(F32) for part in result_parts)).astype(LOW)
    outward_parts = plane_settle(outward_y, outward_x, outward_block)
    far = against_rows(core_rows(mixed_grad, False), inward_part).astype(LOW)
    got = swap(far, "c")
    near = against_rows(core_rows(mixed_grad, True), inward_part).astype(LOW)
    got, near, both_own[1], *outward_parts = together(got, near, both_own[1], *outward_parts)
    outward_own = sum(part.astype(F32) for part in outward_parts).astype(LOW)
    from_y, from_x, block = plane_corner(near, got)
    from_y, from_x = together(from_y, from_x)
    parts = plane_settle(from_y, from_x, block)
    down_own += [planes_scatter(after(down_term, inward_own))]
    normed_one_grad = sum(part.astype(F32) for part in parts)
    scale_one, normal_one = rms_parts(inputs)
    input_grad = middle_grad + norm_back(normed_one_grad, normal_one, scale_one, gain_one)

    outward_sum = planes_scatter_small(outward_own).astype(F32)

    both_got = [plane_exchange(own.reshape(8, d_rows, units)) for own in both_own]
    down_sum = jnp.concatenate(down_own, axis=0).astype(F32)
    inward_own = plane_exchange(inward_own.reshape(8, d_rows, 3 * feats))

    gate_new, gate_dots = updated_ffn(both_got, 0, gate_weight, gate_first, gate_second, count)
    up_new, up_dots = updated_ffn(both_got, 1, up_weight, up_first, up_second, count)
    inward_new, inward_dots = updated_inward(
        inward_own, inward_weight, inward_first, inward_second, count
    )
    own_gains = norm_gains.astype(LOW).astype(F32)
    gain_one_grad = inward_dots / own_gains[0]
    gain_two_grad = (gate_dots + up_dots) / own_gains[1]
    gains_grad = jnp.stack([gain_one_grad, gain_two_grad])
    taps_grad = planes_scatter_small(tap_grads).T

    outward_new = adamw(
        outward_weight, outward_first, outward_second, outward_sum, RATE_MATRIX, DECAY_RATE
    )
    down_new = adamw(down_weight, down_first, down_second, down_sum, RATE_MATRIX, DECAY_RATE)
    gains_new = adamw(norm_gains, gains_first, gains_second, gains_grad, RATE_VECTOR, 0.0)
    taps_new = adamw(conv_taps, taps_first, taps_second, taps_grad, RATE_VECTOR, 0.0)
    return (
        block_output,
        input_grad,
        *inward_new,
        *outward_new,
        *gate_new,
        *up_new,
        *down_new,
        *gains_new,
        *taps_new,
    )


def solution(mesh):
    devices = mesh.devices.reshape(-1, 2, 2, 2)
    rows = P(AXES, None)
    columns = P(None, AXES)
    return jax.shard_map(
        on_device,
        mesh=Mesh(devices, AXES),
        in_specs=(rows,) * 17 + (columns,) * 6,
        out_specs=(rows,) * 17 + (columns,) * 6,
        check_vma=False,
    )
```

time: 1330 us -> 767 us (0.58)
  waiting for transfers between devices: 811 us -> 253 us
  blocking collectives: 162 us -> 0 us
  Pallas kernels: 0 us -> 99.4 us
  matrix products: 183 us -> 95 us
  starting transfers between devices: 22.2 us -> 88.7 us
  local copies, waits for them, and re-layouts: 74.5 us -> 121 us
  other arithmetic: 57.8 us -> 83.8 us
    reduce_scatter x7 -> x5, waiting for transfers between devices: 324 us -> 14.6 us  [planes_scatter(): return lax.psum_scatter(term, 'p', scatter_dimension=0, tiled=True)]
    all_gather x9 -> x5, waiting for transfers between devices: 319 us -> 42.8 us  [planes_gather(): return lax.all_gather(block, 'p', axis=0, tiled=True)]
    ppermute x2 -> x69, waiting for transfers between devices: 4.99 us -> 179 us  [the longest x55 147 us: swap(): return lax.ppermute(block, axis, [(0, 1), (1, 0)])]
    all_to_all x4 -> x0, blocking collectives: 121 us -> none  [exchange(): return lax.all_to_all(blocks, axes, split_axis=0, concat_axis=0, tiled=True)]
    unnamed x20 -> x10, waiting for transfers between devices: 112 us -> 0.17 us
    pallas_call x0 -> x10, Pallas kernels: none -> 99.4 us  [the longest x4 44.8 us: pair_dot(): pl.pallas_call(functools.partial(pair_body, turned), grid=(steps,), in_sp...]
    ppermute x2 -> x69, starting transfers between devices: 4.93 us -> 61.5 us  [the longest x55 39.6 us: swap(): return lax.ppermute(block, axis, [(0, 1), (1, 0)])]
    dot_general x5 -> x3, matrix products: 71.4 us -> 16.2 us  [against_rows(): lax.dot_general(operand, partner, (((1,), (1,)), ((), ())), preferred_ele...]
  transfers between devices with their start and end apart: 24 -> 86, of which waited for: 20 -> 30; matrix products, arithmetic and copies ran while one was open for 19% -> 34% of each run, Pallas kernels for 0% -> 13%
where the time goes in v3:
time: 767 us; the launch traced here: 757 us
  waiting for transfers between devices  253 us (33%)
  local copies, waits for them, and re-layouts  121 us (16%)
  Pallas kernels  99.4 us (13%)
  matrix products  95 us (12%)
  starting transfers between devices  88.7 us (12%)
  other arithmetic  83.8 us (11%)
  between operations  15.6 us (2%)
    ppermute x55, waiting for transfers between devices, swap(): return lax.ppermute(block, axis, [(0, 1), (1, 0)])  147 us
    unnamed x172, local copies, waits for them, and re-layouts  56.4 us
    dot_general x5, matrix products, over_tokens(): lax.dot_general(operand, partner, (((0,), (0,)), ((), ())), preferred_ele...  56.3 us
    pallas_call x4, Pallas kernels, pair_dot(): pl.pallas_call(functools.partial(pair_body, turned), grid=(steps,), in_sp...  44.8 us
    all_gather x5, waiting for transfers between devices, planes_gather(): return lax.all_gather(block, 'p', axis=0, tiled=True)  42.8 us
    ppermute x55, starting transfers between devices, swap(): return lax.ppermute(block, axis, [(0, 1), (1, 0)])  39.6 us
    pallas_call x2, Pallas kernels, half_ffn(): pl.pallas_call(half_body, grid=(count // tile,), in_specs=[pl.BlockSpec((...  38 us
    dynamic_update_slice x16, local copies, waits for them, and re-layouts, plane_gather(): out = lax.dynamic_update_slice_in_dim(out, piece, at * rows, axis=0)  31.2 us
  transfers between devices with their start and end apart: 86, of which 30 were waited for; matrix products, arithmetic and copies ran while one was open for 34% of the time, Pallas kernels for 13%

profile of v3, /device:TPU:0, one launch (start us, length us, event | category | flops | bytes accessed | tf_op | source)
XLA Modules:
  0.0 756.5 jit_solution(3980524949725498448)
XLA Ops:
  38.0 20.2 %collective-permute-done.12 = bf16[2,4,5,64]{3,2,1,0:T(8,128)(2,1)S(1)} collective-permute-done((bf16[2,4,5,64]{3,2,1,0:T(8,128)(2,1)S(1)}, bf16[2,4,5,64]{3,2,1,0:T(8,128)(2,1)S(1)}, u32[]{:S(2)}, u32[]{:S(2)}) %collective-permute-start.12) | collective-permute-done | bytes 5152 | tf_op jit(solution)/shard_map/ppermute | solution.py:72
  64.7 15.4 %all-gather.6.cloned.1.call-done.down_ref.c_ref = bf16[512,2048]{1,0:T(8,128)(2,1)} async-done(((bf16[128,2048]{1,0:T(8,128)(2,1)}), bf16[512,2048]{1,0:T(8,128)(2,1)}) %all-gather.6.cloned.1.call-update) | async-done | bytes 2097168 | tf_op jit(solution)/shard_map/all_gather | solution.py:163
  114.6 9.0 %all-to-all-done.1 = bf16[8,64,2048]{2,1,0:T(8,128)(2,1)S(1)} async-done(((bf16[8,64,2048]{2,1,0:T(8,128)(2,1)}), bf16[8,64,2048]{2,1,0:T(8,128)(2,1)S(1)}, u32[]{:S(2)}, u32[]{:S(2)}) %all-to-all-start.1) | async-done | bytes 2097184 | tf_op jit(solution)/shard_map/all_to_all | solution.py:124
  133.2 14.1 %collective-permute-done.19 = bf16[256,2048]{1,0:T(8,128)(2,1)S(1)} collective-permute-done((bf16[256,2048]{1,0:T(8,128)(2,1)}, bf16[256,2048]{1,0:T(8,128)(2,1)S(1)}, u32[]{:S(2)}, u32[]{:S(2)}) %collective-permute-start.19) | collective-permute-done | bytes 1048608 | tf_op jit(solution)/shard_map/ppermute | solution.py:72
  176.3 10.1 %fusion.6 = f32[2048,768]{1,0:T(8,128)S(1)} fusion(bf16[2048,768]{1,0:T(8,128)(2,1)} %all-gather.8.cloned.1.call-done, bf16[2048,2048]{1,0:T(8,128)(2,1)} %constant_dynamic-update-slice_fusion.38, f32[2048]{0:T(1024)S(1)} %mul.494, f32[2048]{0:T(1024)S(1)} %add_rsqrt_fusion), kind=kOutput, calls=%fused_computation.25 | convolution fusion | flops 6459228160 | bytes 17842176 | tf_op jit(solution)/shard_map/dot_general | solution.py:29
  190.7 8.8 %collective-permute-done.27 = bf16[256,2048]{1,0:T(8,128)(2,1)S(1)} collective-permute-done((bf16[256,2048]{1,0:T(8,128)(2,1)}, bf16[256,2048]{1,0:T(8,128)(2,1)S(1)}, u32[]{:S(2)}, u32[]{:S(2)}) %collective-permute-start.27) | collective-permute-done | bytes 1048608 | tf_op jit(solution)/shard_map/ppermute | solution.py:72
  213.3 7.6 %collective-permute-done.28 = bf16[128,2048]{1,0:T(8,128)(2,1)} collective-permute-done((bf16[128,2048]{1,0:T(8,128)(2,1)}, bf16[128,2048]{1,0:T(8,128)(2,1)}, u32[]{:S(2)}, u32[]{:S(2)}) %collective-permute-start.28) | collective-permute-done | bytes 524320 | tf_op jit(solution)/shard_map/ppermute | solution.py:72
  239.0 5.9 multiply_reduce_fusion.4
  247.4 23.4 %collective-permute-done.35 = bf16[256,2048]{1,0:T(8,128)(2,1)} collective-permute-done((bf16[256,2048]{1,0:T(8,128)(2,1)S(1)}, bf16[256,2048]{1,0:T(8,128)(2,1)}, u32[]{:S(2)}, u32[]{:S(2)}) %collective-permute-start.35) | collective-permute-done | bytes 1048608 | tf_op jit(solution)/shard_map/ppermute | solution.py:72
  278.3 6.6 collective-permute-done.37
  291.9 19.1 %shard_map.399 = (bf16[2048,512]{1,0:T(8,128)(2,1)S(1)}, bf16[2048,1024]{1,0:T(8,128)(2,1)}) custom-call(bf16[2048,2048]{1,0:T(8,128)(2,1)} %constant_dynamic-update-slice_fusion.21.rows_ref, bf16[2048,2048]{1,0:T(8,128)(2,1)} %constant_dynamic-update-slice_fusion.10.upstream_ref, bf16[2048,1024]{1,0:T(8,128)(2,1)} %all-gather.10.cloned.1.call-done.both_ref.c_ref, ...), custom_call_target="tpu_custom_call" | custom-call | flops 12884901888 | bytes 23068672 | tf_op jit(solution)/shard_map/pallas_call | solution.py:218
  311.0 9.1 %convolution_convert_fusion.8 = bf16[512,2048]{1,0:T(8,128)(2,1)} fusion(bf16[2048,512]{1,0:T(8,128)(2,1)S(1)} %get-tuple-element.117.a_ref, bf16[2048,2048]{1,0:T(8,128)(2,1)} %constant_dynamic-update-slice_fusion.10.upstream_ref), kind=kOutput, calls=%fused_computation.18 | convolution fusion | flops 4296015872 | bytes 12582912 | tf_op jit(solution)/shard_map/dot_general | solution.py:33
  321.5 14.0 %convolution_convert_fusion.5 = bf16[2048,1024]{1,0:T(8,128)(2,1)} fusion(bf16[2048,2048]{1,0:T(8,128)(2,1)} %constant_dynamic-update-slice_fusion.21.rows_ref, bf16[2048,1024]{1,0:T(8,128)(2,1)} %get-tuple-element.114.a_ref), kind=kOutput, calls=%fused_computation.10 | convolution fusion | flops 8592031744 | bytes 16777216 | tf_op jit(solution)/shard_map/dot_general | solution.py:33
  336.0 27.3 %all-gather.12.cloned.1.call-done.both_ref.e_ref = bf16[2048,1024]{1,0:T(8,128)(2,1)} async-done(((bf16[512,1024]{1,0:T(8,128)(2,1)}), bf16[2048,1024]{1,0:T(8,128)(2,1)}) %all-gather.12.cloned.1.call-update) | async-done | bytes 4194320 | tf_op jit(solution)/shard_map/all_gather | solution.py:163
  364.9 18.9 %shard_map.400 = (bf16[2048,512]{1,0:T(8,128)(2,1)S(1)}, bf16[2048,1024]{1,0:T(8,128)(2,1)}) custom-call(bf16[2048,2048]{1,0:T(8,128)(2,1)} %constant_dynamic-update-slice_fusion.21.rows_ref, bf16[2048,2048]{1,0:T(8,128)(2,1)} %constant_dynamic-update-slice_fusion.10.upstream_ref, bf16[2048,1024]{1,0:T(8,128)(2,1)} %all-gather.12.cloned.1.call-done.both_ref.e_ref, ...), custom_call_target="tpu_custom_call" | custom-call | flops 12884901888 | bytes 23068672 | tf_op jit(solution)/shard_map/pallas_call | solution.py:218
  385.1 14.6 %shard_map.401 = bf16[1024,2048]{1,0:T(8,128)(2,1)} custom-call(bf16[2048,1024]{1,0:T(8,128)(2,1)} %get-tuple-element.114.a_ref, bf16[2048,1024]{1,0:T(8,128)(2,1)} %get-tuple-element.124.b_ref, bf16[2048,1024]{1,0:T(8,128)(2,1)} %all-gather.10.cloned.1.call-done.both_ref.c_ref, bf16[2048,1024]{1,0:T(8,128)(2,1)} %all-gather.12.cloned.1.call-done.both_ref.e_ref), custom_call_target="tpu_custom_call" | custom-call | flops 8589934592 | bytes 16777216 | tf_op jit(solution)/shard_map/pallas_call | solution.py:254
  400.0 13.2 %shard_map.402 = bf16[1024,2048]{1,0:T(8,128)(2,1)S(1)} custom-call(bf16[2048,1024]{1,0:T(8,128)(2,1)} %get-tuple-element.114.a_ref, bf16[2048,1024]{1,0:T(8,128)(2,1)} %get-tuple-element.124.b_ref, bf16[2048,1024]{1,0:T(8,128)(2,1)} %all-gather.10.cloned.1.call-done.both_ref.c_ref, bf16[2048,1024]{1,0:T(8,128)(2,1)} %all-gather.12.cloned.1.call-done.both_ref.e_ref), custom_call_target="tpu_custom_call" | custom-call | flops 8589934592 | bytes 16777216 | tf_op jit(solution)/shard_map/pallas_call | solution.py:254
  419.5 12.7 %convolution_convert_fusion.4 = bf16[2048,1024]{1,0:T(8,128)(2,1)} fusion(bf16[2048,2048]{1,0:T(8,128)(2,1)} %constant_dynamic-update-slice_fusion.21.rows_ref, bf16[2048,1024]{1,0:T(8,128)(2,1)S(1)} %copy-done.69), kind=kOutput, calls=%fused_computation.9 | convolution fusion | flops 8592031744 | bytes 16777216 | tf_op jit(solution)/shard_map/dot_general | solution.py:33
  433.9 8.4 %shard_map.403 = bf16[1024,2048]{1,0:T(8,128)(2,1)} custom-call(bf16[2048,512]{1,0:T(8,128)(2,1)S(1)} %copy-done.17, bf16[2048,512]{1,0:T(8,128)(2,1)S(1)} %copy-done.19, bf16[512,2048]{1,0:T(8,128)(2,1)} %all-gather.6.cloned.1.call-done.down_ref.c_ref, bf16[512,2048]{1,0:T(8,128)(2,1)} %all-gather.14.cloned.1.call-done.down_ref.e_ref), custom_call_target="tpu_custom_call" | custom-call | flops 4294967296 | bytes 10485760 | tf_op jit(solution)/shard_map/pallas_call | solution.py:254
  448.9 9.4 %convolution_convert_fusion.7 = bf16[512,2048]{1,0:T(8,128)(2,1)} fusion(bf16[2048,512]{1,0:T(8,128)(2,1)S(1)} %copy-done.19, bf16[2048,2048]{1,0:T(8,128)(2,1)} %constant_dynamic-update-slice_fusion.10.upstream_ref), kind=kOutput, calls=%fused_computation.17 | convolution fusion | flops 4296015872 | bytes 12582912 | tf_op jit(solution)/shard_map/dot_general | solution.py:33
  458.3 14.3 %collective-permute-done.46 = bf16[256,2048]{1,0:T(8,128)(2,1)} collective-permute-done((bf16[256,2048]{1,0:T(8,128)(2,1)}, bf16[256,2048]{1,0:T(8,128)(2,1)}, u32[]{:S(2)}, u32[]{:S(2)}) %collective-permute-start.46) | collective-permute-done | bytes 1048608 | tf_op jit(solution)/shard_map/ppermute | solution.py:72
  474.7 8.5 %shard_map.404 = bf16[1024,2048]{1,0:T(8,128)(2,1)} custom-call(bf16[2048,512]{1,0:T(8,128)(2,1)S(1)} %copy-done.17, bf16[2048,512]{1,0:T(8,128)(2,1)S(1)} %copy-done.20, bf16[512,2048]{1,0:T(8,128)(2,1)} %all-gather.6.cloned.1.call-done.down_ref.c_ref, bf16[512,2048]{1,0:T(8,128)(2,1)} %all-gather.14.cloned.1.call-done.down_ref.e_ref), custom_call_target="tpu_custom_call" | custom-call | flops 4294967296 | bytes 10485760 | tf_op jit(solution)/shard_map/pallas_call | solution.py:254
  511.8 16.5 %collective-permute-done.49 = bf16[128,2048]{1,0:T(8,128)(2,1)} collective-permute-done((bf16[128,2048]{1,0:T(8,128)(2,1)}, bf16[128,2048]{1,0:T(8,128)(2,1)}, u32[]{:S(2)}, u32[]{:S(2)}) %collective-permute-start.49) | collective-permute-done | bytes 524320 | tf_op jit(solution)/shard_map/ppermute | solution.py:72
  550.3 11.0 %convolution_convert_fusion.6 = bf16[2048,768]{1,0:T(8,128)(2,1)} fusion(bf16[2048,2048]{1,0:T(8,128)(2,1)} %constant_dynamic-update-slice_fusion.38, f32[2048]{0:T(1024)S(1)} %copy-done.54, f32[2048]{0:T(1024)S(1)} %copy-done.58, bf16[2048,256]{1,0:T(8,128)(2,1)S(1)} %get-tuple-element.197, bf16[2048,256]{1,0:T(8,128)(2,1)S(1)} %get-tuple-element.227, ...), kind=kOutput, calls=%fused_computation.11 | convolution fusion | flops 6470238208 | bytes 14696448 | tf_op jit(solution)/shard_map/dot_general | solution.py:33
  563.3 7.5 collective-permute-done.55
  584.5 5.9 pad_add_fusion.3
  596.6 7.8 %convolution_convert_fusion.2 = bf16[1024,2048]{1,0:T(8,128)(2,1)} fusion(bf16[2048,768]{1,0:T(8,128)(2,1)} %all-gather.8.cloned.1.call-done, bf16[256,768]{1,0:T(8,128)(2,1)} %get-tuple-element.210, bf16[256,768]{1,0:T(8,128)(2,1)} %get-tuple-element.211, bf16[256,768]{1,0:T(8,128)(2,1)} %get-tuple-element.212, bf16[256,768]{1,0:T(8,128)(2,1)S(1)} %get-tuple-element.209), kind=kOutput, calls=%fused_computation.7 | convolution fusion | flops 3229614080 | bytes 8912896 | tf_op jit(solution)/shard_map/dot_general | solution.py:39
  604.4 12.3 %collective-permute-done.58 = bf16[256,2048]{1,0:T(8,128)(2,1)S(1)} collective-permute-done((bf16[256,2048]{1,0:T(8,128)(2,1)}, bf16[256,2048]{1,0:T(8,128)(2,1)S(1)}, u32[]{:S(2)}, u32[]{:S(2)}) %collective-permute-start.58) | collective-permute-done | bytes 1048608 | tf_op jit(solution)/shard_map/ppermute | solution.py:72
  619.6 14.5 %reduce-scatter.12.cloned.1.call-done = bf16[512,768]{1,0:T(8,128)(2,1)} async-done(((bf16[2048,768]{1,0:T(8,128)(2,1)}), bf16[512,768]{1,0:T(8,128)(2,1)}) %reduce-scatter.12.cloned.1.call-update) | async-done | bytes 786448 | tf_op jit(solution)/shard_map/reduce_scatter | solution.py:167
  668.7 24.2 %collective-permute-done.64 = bf16[64,2048]{1,0:T(8,128)(2,1)} collective-permute-done((bf16[64,2048]{1,0:T(8,128)(2,1)}, bf16[64,2048]{1,0:T(8,128)(2,1)}, u32[]{:S(2)}, u32[]{:S(2)}) %collective-permute-start.64) | collective-permute-done | bytes 262176 | tf_op jit(solution)/shard_map/ppermute | solution.py:172
  728.1 7.0 all-to-all-done.4.refs_0_
  742.5 6.9 multiply_subtract_fusion
  (459 shorter events, 336.8 us)
Async XLA Ops:
  7.2 72.9 %all-gather.6.cloned.1.call-start = ((), (), s32[]{:S(2)}) async-start(), calls=%async_computation.12 | async-start | bytes 2621440 | tf_op jit(solution)/shard_map/all_gather | solution.py:163
  19.6 60.6 %collective-permute-start.15 = (bf16[64,2048]{1,0:T(8,128)(2,1)S(1)}, bf16[64,2048]{1,0:T(8,128)(2,1)}, u32[]{:S(2)}, u32[]{:S(2)}) collective-permute-start(bf16[64,2048]{1,0:T(8,128)(2,1)S(1)} %convert_element_type.144), channel_id=1, source_target_pairs={{16,0},{24,8},{0,16},{8,24},{17,1},{25,9},{1,17},{9,25},{18,2},{26... | collective-permute-start | bytes 786440 | tf_op jit(solution)/shard_map/ppermute | solution.py:172
  20.5 59.8 %collective-permute-start.14 = (bf16[64,2048]{1,0:T(8,128)(2,1)S(1)}, bf16[64,2048]{1,0:T(8,128)(2,1)}, u32[]{:S(2)}, u32[]{:S(2)}) collective-permute-start(bf16[64,2048]{1,0:T(8,128)(2,1)S(1)} %convert_element_type.144), channel_id=1, source_target_pairs={{8,0},{16,8},{24,16},{0,24},{9,1},{17,9},{25,17},{1,25},{10,2},{18... | collective-permute-start | bytes 786440 | tf_op jit(solution)/shard_map/ppermute | solution.py:172
  22.9 62.1 %collective-permute-start.1 = (bf16[256,2048]{1,0:T(8,128)(2,1)S(1)}, bf16[256,2048]{1,0:T(8,128)(2,1)}, u32[]{:S(2)}, u32[]{:S(2)}) collective-permute-start(bf16[256,2048]{1,0:T(8,128)(2,1)S(1)} %copy-done.25), channel_id=1, source_target_pairs={{0,4},{4,0},{1,5},{5,1},{2,6},{6,2},{3,7},{7,3},{8,12},{12,8},{9,1... | collective-permute-start | bytes 3145736 | tf_op jit(solution)/shard_map/ppermute | solution.py:72
  24.4 57.1 %collective-permute-start = (bf16[256,2048]{1,0:T(8,128)(2,1)S(1)}, bf16[256,2048]{1,0:T(8,128)(2,1)}, u32[]{:S(2)}, u32[]{:S(2)}) collective-permute-start(bf16[256,2048]{1,0:T(8,128)(2,1)S(1)} %copy-done.25), channel_id=1, source_target_pairs={{0,2},{2,0},{1,3},{3,1},{4,6},{6,4},{5,7},{7,5},{8,10},{10,8},{9,1... | collective-permute-start | bytes 3145736 | tf_op jit(solution)/shard_map/ppermute | solution.py:72
  31.3 33.4 %all-to-all-start = ((bf16[8,64,768]{2,1,0:T(8,128)(2,1)}), bf16[8,64,768]{2,1,0:T(8,128)(2,1)S(1)}, u32[]{:S(2)}, u32[]{:S(2)}) async-start(bf16[8,64,768]{2,1,0:T(8,128)(2,1)} %get-tuple-element.103), calls=%async_computation | async-start | bytes 1572864 | tf_op jit(solution)/shard_map/all_to_all | solution.py:124
  34.9 141.4 %all-gather.8.cloned.1.call-start = ((), (), s32[]{:S(2)}) async-start(), calls=%async_computation.13 | async-start | bytes 3932160 | tf_op jit(solution)/shard_map/all_gather | solution.py:163
  80.2 26.3 %collective-permute-start.4 = (bf16[256,2048]{1,0:T(8,128)(2,1)S(1)}, bf16[256,2048]{1,0:T(8,128)(2,1)}, u32[]{:S(2)}, u32[]{:S(2)}) collective-permute-start(bf16[256,2048]{1,0:T(8,128)(2,1)S(1)} %copy-done.25), channel_id=1, source_target_pairs={{0,1},{1,0},{2,3},{3,2},{4,5},{5,4},{6,7},{7,6},{8,9},{9,8},{10,11... | collective-permute-start | bytes 3145736 | tf_op jit(solution)/shard_map/ppermute | solution.py:72
  92.2 31.3 %all-to-all-start.1 = ((bf16[8,64,2048]{2,1,0:T(8,128)(2,1)}), bf16[8,64,2048]{2,1,0:T(8,128)(2,1)S(1)}, u32[]{:S(2)}, u32[]{:S(2)}) async-start(bf16[8,64,2048]{2,1,0:T(8,128)(2,1)} %get-tuple-element.105), calls=%async_computation.1 | async-start | bytes 4194304 | tf_op jit(solution)/shard_map/all_to_all | solution.py:124
  95.9 196.1 %all-gather.10.cloned.1.call-start = ((), (), s32[]{:S(2)}) async-start(), calls=%async_computation.14 | async-start | bytes 5242880 | tf_op jit(solution)/shard_map/all_gather | solution.py:163
  130.8 37.3 %collective-permute-start.22 = (bf16[256,2048]{1,0:T(8,128)(2,1)}, bf16[256,2048]{1,0:T(8,128)(2,1)}, u32[]{:S(2)}, u32[]{:S(2)}) collective-permute-start(bf16[256,2048]{1,0:T(8,128)(2,1)} %param.24), channel_id=1, source_target_pairs={{0,1},{1,0},{2,3},{3,2},{4,5},{5,4},{6,7},{7,6},{8,9},{9,8},{10,11... | collective-permute-start | bytes 3145736 | tf_op jit(solution)/shard_map/ppermute | solution.py:72
  173.6 56.0 %collective-permute-start.30 = (bf16[256,2048]{1,0:T(8,128)(2,1)}, bf16[256,2048]{1,0:T(8,128)(2,1)}, u32[]{:S(2)}, u32[]{:S(2)}) collective-permute-start(bf16[256,2048]{1,0:T(8,128)(2,1)} %pad_maximum_fusion.3), channel_id=1, source_target_pairs={{0,1},{1,0},{2,3},{3,2},{4,5},{5,4},{6,7},{7,6},{8,9},{9,8},{10,11... | collective-permute-start | bytes 3145736 | tf_op jit(solution)/shard_map/ppermute | solution.py:72
  174.5 27.6 %collective-permute-start.26 = (bf16[256,2048]{1,0:T(8,128)(2,1)}, bf16[256,2048]{1,0:T(8,128)(2,1)S(1)}, u32[]{:S(2)}, u32[]{:S(2)}) collective-permute-start(bf16[256,2048]{1,0:T(8,128)(2,1)} %pad_maximum_fusion.3), channel_id=1, source_target_pairs={{0,2},{2,0},{1,3},{3,1},{4,6},{6,4},{5,7},{7,5},{8,10},{10,8},{9,1... | collective-permute-start | bytes 3145736 | tf_op jit(solution)/shard_map/ppermute | solution.py:72
  210.3 125.6 %all-gather.14.cloned.1.call-start = ((), (), s32[]{:S(2)}) async-start(), calls=%async_computation.16 | async-start | bytes 2621440 | tf_op jit(solution)/shard_map/all_gather | solution.py:163
  227.2 136.1 %all-gather.12.cloned.1.call-start = ((), (), s32[]{:S(2)}) async-start(), calls=%async_computation.15 | async-start | bytes 5242880 | tf_op jit(solution)/shard_map/all_gather | solution.py:163
  274.1 289.1 %reduce-scatter.6.cloned.1.call-start = ((), (), s32[]{:S(2)}) async-start(), calls=%async_computation.17 | async-start | bytes 2621440 | tf_op jit(solution)/shard_map/reduce_scatter | solution.py:167
  335.5 227.8 %reduce-scatter.8.cloned.1.call-start = ((), (), s32[]{:S(2)}) async-start(), calls=%async_computation.18 | async-start | bytes 5242880 | tf_op jit(solution)/shard_map/reduce_scatter | solution.py:167
  399.7 204.7 %reduce-scatter.10.cloned.1.call-start = ((), (), s32[]{:S(2)}) async-start(), calls=%async_computation.19 | async-start | bytes 5242880 | tf_op jit(solution)/shard_map/reduce_scatter | solution.py:167
  495.5 32.8 %collective-permute-start.50 = (bf16[1024,2048]{1,0:T(8,128)(2,1)}, bf16[1024,2048]{1,0:T(8,128)(2,1)}, u32[]{:S(2)}, u32[]{:S(2)}) collective-permute-start(bf16[1024,2048]{1,0:T(8,128)(2,1)} %bitcast.30), channel_id=1, source_target_pairs={{0,1},{1,0},{2,3},{3,2},{4,5},{5,4},{6,7},{7,6},{8,9},{9,8},{10,11... | collective-permute-start | bytes 12582920 | tf_op jit(solution)/shard_map/ppermute | solution.py:72
  498.1 30.1 %all-to-all-start.3 = ((bf16[8,256,256]{2,1,0:T(8,128)(2,1)}), bf16[8,256,256]{2,1,0:T(8,128)(2,1)}, u32[]{:S(2)}, u32[]{:S(2)}) async-start(bf16[8,256,256]{2,1,0:T(8,128)(2,1)} %bitcast.122), calls=%async_computation.3 | async-start | bytes 2097152 | tf_op jit(solution)/shard_map/all_to_all | solution.py:124
  502.4 131.6 %reduce-scatter.12.cloned.1.call-start = ((), (), s32[]{:S(2)}) async-start(), calls=%async_computation.20 | async-start | bytes 3932160 | tf_op jit(solution)/shard_map/reduce_scatter | solution.py:167
  531.4 31.8 %collective-permute-start.53 = (bf16[128,2048]{1,0:T(8,128)(2,1)}, bf16[128,2048]{1,0:T(8,128)(2,1)}, u32[]{:S(2)}, u32[]{:S(2)}) collective-permute-start(bf16[128,2048]{1,0:T(8,128)(2,1)} %get-tuple-element.225), channel_id=1, source_target_pairs={{0,2},{2,0},{1,3},{3,1},{4,6},{6,4},{5,7},{7,5},{8,10},{10,8},{9,1... | collective-permute-start | bytes 1572872 | tf_op jit(solution)/shard_map/ppermute | solution.py:72
  532.8 30.5 %collective-permute-start.52 = (bf16[128,2048]{1,0:T(8,128)(2,1)}, bf16[128,2048]{1,0:T(8,128)(2,1)}, u32[]{:S(2)}, u32[]{:S(2)}) collective-permute-start(bf16[128,2048]{1,0:T(8,128)(2,1)} %get-tuple-element.226), channel_id=1, source_target_pairs={{0,4},{4,0},{1,5},{5,1},{2,6},{6,2},{3,7},{7,3},{8,12},{12,8},{9,1... | collective-permute-start | bytes 1572872 | tf_op jit(solution)/shard_map/ppermute | solution.py:72
  579.7 37.5 %collective-permute-start.56 = (bf16[1024,2048]{1,0:T(8,128)(2,1)}, bf16[1024,2048]{1,0:T(8,128)(2,1)}, u32[]{:S(2)}, u32[]{:S(2)}) collective-permute-start(bf16[1024,2048]{1,0:T(8,128)(2,1)} %convolution_convert_fusion.3), channel_id=1, source_target_pairs={{0,1},{1,0},{2,3},{3,2},{4,5},{5,4},{6,7},{7,6},{8,9},{9,8},{10,11... | collective-permute-start | bytes 12582920 | tf_op jit(solution)/shard_map/ppermute | solution.py:72
  590.4 26.2 %collective-permute-start.58 = (bf16[256,2048]{1,0:T(8,128)(2,1)}, bf16[256,2048]{1,0:T(8,128)(2,1)S(1)}, u32[]{:S(2)}, u32[]{:S(2)}) collective-permute-start(bf16[256,2048]{1,0:T(8,128)(2,1)} %get-tuple-element.200), channel_id=1, source_target_pairs={{0,4},{4,0},{1,5},{5,1},{2,6},{6,2},{3,7},{7,3},{8,12},{12,8},{9,1... | collective-permute-start | bytes 3145736 | tf_op jit(solution)/shard_map/ppermute | solution.py:72
  590.8 26.4 %collective-permute-start.57 = (bf16[256,2048]{1,0:T(8,128)(2,1)}, bf16[256,2048]{1,0:T(8,128)(2,1)}, u32[]{:S(2)}, u32[]{:S(2)}) collective-permute-start(bf16[256,2048]{1,0:T(8,128)(2,1)} %get-tuple-element.201), channel_id=1, source_target_pairs={{0,2},{2,0},{1,3},{3,1},{4,6},{6,4},{5,7},{7,5},{8,10},{10,8},{9,1... | collective-permute-start | bytes 3145736 | tf_op jit(solution)/shard_map/ppermute | solution.py:72
  592.8 62.1 %all-to-all-start.5 = ((bf16[8,64,1024]{2,1,0:T(8,128)(2,1)}), bf16[8,64,1024]{2,1,0:T(8,128)(2,1)S(1)}, u32[]{:S(2)}, u32[]{:S(2)}) async-start(bf16[8,64,1024]{2,1,0:T(8,128)(2,1)} %bitcast.37), calls=%async_computation.9 | async-start | bytes 2097152 | tf_op jit(solution)/shard_map/all_to_all | solution.py:124
  596.4 146.2 %reduce-scatter.14.cloned.1.call-start = ((), (), s32[]{:S(2)}) async-start(), calls=%async_computation.21 | async-start | bytes 2621440 | tf_op jit(solution)/shard_map/reduce_scatter | solution.py:167
  643.2 49.7 %collective-permute-start.64 = (bf16[64,2048]{1,0:T(8,128)(2,1)}, bf16[64,2048]{1,0:T(8,128)(2,1)}, u32[]{:S(2)}, u32[]{:S(2)}) collective-permute-start(bf16[64,2048]{1,0:T(8,128)(2,1)} %get-tuple-element.222), channel_id=1, source_target_pairs={{16,0},{24,8},{0,16},{8,24},{17,1},{25,9},{1,17},{9,25},{18,2},{26... | collective-permute-start | bytes 786440 | tf_op jit(solution)/shard_map/ppermute | solution.py:172
  652.9 62.8 %collective-permute-start.61 = (bf16[256,2048]{1,0:T(8,128)(2,1)}, bf16[256,2048]{1,0:T(8,128)(2,1)}, u32[]{:S(2)}, u32[]{:S(2)}) collective-permute-start(bf16[256,2048]{1,0:T(8,128)(2,1)} %get-tuple-element.198), channel_id=1, source_target_pairs={{0,2},{2,0},{1,3},{3,1},{4,6},{6,4},{5,7},{7,5},{8,10},{10,8},{9,1... | collective-permute-start | bytes 3145736 | tf_op jit(solution)/shard_map/ppermute | solution.py:72
  653.5 62.2 %collective-permute-start.62 = (bf16[256,2048]{1,0:T(8,128)(2,1)}, bf16[256,2048]{1,0:T(8,128)(2,1)}, u32[]{:S(2)}, u32[]{:S(2)}) collective-permute-start(bf16[256,2048]{1,0:T(8,128)(2,1)} %get-tuple-element.199), channel_id=1, source_target_pairs={{0,4},{4,0},{1,5},{5,1},{2,6},{6,2},{3,7},{7,3},{8,12},{12,8},{9,1... | collective-permute-start | bytes 3145736 | tf_op jit(solution)/shard_map/ppermute | solution.py:72
  654.9 40.6 %all-to-all-start.6 = ((bf16[8,64,1024]{2,1,0:T(8,128)(2,1)}), bf16[8,64,1024]{2,1,0:T(8,128)(2,1)S(1)}, u32[]{:S(2)}, u32[]{:S(2)}) async-start(bf16[8,64,1024]{2,1,0:T(8,128)(2,1)} %bitcast.124), calls=%async_computation.10 | async-start | bytes 2097152 | tf_op jit(solution)/shard_map/all_to_all | solution.py:124
  (128 other events, 1476.4 us)
Sparse Core Ops, SparseCore 0:
  17.3 62.8 all-gather.5
  82.3 63.2 all-gather.7
  154.9 80.3 all-gather.9
  237.3 44.4 all-gather.13
  283.8 79.4 all-gather.11
  366.0 42.3 reduce-scatter.5
  410.8 76.0 reduce-scatter.7
  496.0 74.6 reduce-scatter.9
  573.1 60.9 reduce-scatter.11
  636.3 61.2 reduce-scatter.13

commit v4 on v3

--- a/solution.py
+++ b/solution.py
@@ -84,31 +84,24 @@
     return jnp.stack([jnp.where(first, block, other), jnp.where(first, other, block)])
 
 
-def over_planes(block):
-    count = lax.axis_size("p")
-    if count > 4:
-        return lax.all_gather(block, "p", axis=0, tiled=False)
-    pieces = [block]
-    for distance in range(1, count):
-        route = [((i + distance) % count, i) for i in range(count)]
-        pieces.append(lax.ppermute(block, "p", route))
-    return jnp.roll(jnp.stack(pieces), lax.axis_index("p"), axis=0)
-
-
-def plane_blocks(block):
+def plane_near(block):
+    return block, swap(block, "x"), swap(block, "y"), swap(block, "c")
+
+
+def plane_blocks(block, by_x=None, by_y=None, own_far=None):
+    if by_x is None:
+        block, by_x, by_y, own_far = plane_near(block)
     half = block.shape[0] // 2
-    by_x, by_y = swap(block, "x"), swap(block, "y")
-    own_far = swap(block, "c")
     corner = jnp.concatenate([swap(by_x[:half], "y"), swap(by_y[half:], "x")], axis=0)
     near = [block, by_x, by_y, corner]
     return near, [own_far] + [swap(piece, "c") for piece in near[1:]]
 
 
-def plane_gather(block):
+def plane_gather(block, *near):
     rows = block.shape[0]
     mine_y, mine_x, mine_c = (lax.axis_index(axis) for axis in PLANE)
     out = jnp.zeros((8 * rows, block.shape[1]), block.dtype)
-    for dc, pieces in enumerate(plane_blocks(block)):
+    for dc, pieces in enumerate(plane_blocks(block, *near)):
         for k, piece in enumerate(pieces):
             at = ((mine_y ^ (k >> 1)) * 2 + (mine_x ^ (k & 1))) * 2 + (mine_c ^ dc)
             out = lax.dynamic_update_slice_in_dim(out, piece, at * rows, axis=0)
@@ -172,30 +165,17 @@
     return lax.ppermute(block, "p", [((i + distance) % count, i) for i in range(count)])
 
 
-def planes_gather_small(block):
-    count = lax.axis_size("p")
-    if count > 4:
-        return planes_gather(block)
-    pieces = jnp.stack([block] + [shifted(block, i) for i in range(1, count)])
-    mine = lax.axis_index("p")
-    picked = [
-        lax.dynamic_index_in_dim(pieces, (i - mine) % count, axis=0, keepdims=False)
-        for i in range(count)
-    ]
-    return jnp.concatenate(picked, axis=0)
-
-
 def planes_scatter_small(term):
     count = lax.axis_size("p")
     if count > 4:
-        return planes_scatter(term)
+        return [planes_scatter(term)]
     rows = term.shape[0] // count
     mine = lax.axis_index("p")
-    total = lax.dynamic_slice_in_dim(term, mine * rows, rows, axis=0).astype(F32)
+    parts = [lax.dynamic_slice_in_dim(term, mine * rows, rows, axis=0)]
     for i in range(1, count):
         piece = lax.dynamic_slice_in_dim(term, (mine - i) % count * rows, rows, axis=0)
-        total = total + shifted(piece, i).astype(F32)
-    return total
+        parts.append(shifted(piece, i))
+    return parts
 
 
 def half_body(rows_ref, upstream_ref, both_ref, down_ref, hidden_out, grads_out):
@@ -434,25 +414,28 @@
     place = lax.axis_index(PLANE)
 
     down_low = down_weight.astype(LOW)
-    block_here, outward_here, small = together(
-        block_input, outward_weight, jnp.concatenate([norm_gains, conv_taps], axis=0), down_low
-    )[:3]
-    outward_low = outward_here.astype(LOW)
     down_a, down_b = down_low[: ff_rows // 2], down_low[ff_rows // 2 :]
-    down_parts = [planes_gather(down_a)]
-    inward_sent, ffn_sent = packed(after(inward_weight, down_low), gate_weight, up_weight, count)
+    small = jnp.concatenate([norm_gains, conv_taps], axis=0).astype(LOW)
+    small = jnp.pad(small, ((0, 11), (0, d - d_rows)))
+    first = jnp.concatenate([down_a, outward_weight.astype(LOW), small], axis=0)
+    first_part = planes_gather(first)
+    block_here, inward_here, _ = together(block_input, inward_weight, first)
+    inward_sent, ffn_sent = packed(inward_here, gate_weight, up_weight, count)
     inward_got = plane_exchange(inward_sent).reshape(8 * d_rows, 3 * feats)
-    inward_got, first_down = together(inward_got, down_parts[0])
-    down_parts = [first_down]
+    ffn_got = plane_exchange(after(ffn_sent, inward_got)).reshape(8 * d_rows, 2 * units)
+    *inputs_near, inward_got, ffn_got, first_part = together(
+        *plane_near(block_here), inward_got, ffn_got, first_part
+    )
     inward_part = planes_gather(inward_got)
-    ffn_got = plane_exchange(after(ffn_sent, inward_got)).reshape(8 * d_rows, 2 * units)
-    ffn_parts = [planes_gather(ffn_got[:, :units])]
-    inputs_low = plane_gather(block_here)
-    small = over(over(over(over_planes(small.astype(LOW)), "c"), "x"), "y").transpose(3, 0, 1, 2, 4, 5)
-    outward_part = planes_gather_small(outward_low)
-    inputs_low, small, outward_part, ffn_got = together(inputs_low, small, outward_part, ffn_got)
-    upstream = plane_gather_here(after(cotangent, inputs_low))
-    outward_full = plane_gather(after(outward_part, upstream))
+    ffn_parts = [planes_gather(ffn_got[:, :units]), planes_gather(ffn_got[:, units:])]
+    first_part = first_part.reshape(count, -1, d)
+    down_parts = [first_part[:, : ff_rows // 2].reshape(-1, d), planes_gather(down_b)]
+    outward_part = first_part[:, ff_rows // 2 : ff_rows // 2 + d_rows].reshape(-1, d)
+    small = first_part[:, ff_rows // 2 + d_rows :][:, :5, :d_rows]
+    small = over(over(over(small, "c"), "x"), "y").transpose(3, 0, 1, 2, 4, 5)
+    inputs_low = plane_gather(*inputs_near)
+    inputs_low, small, outward_part = together(inputs_low, small, outward_part)
+    outward_full = plane_gather(outward_part)
     small = small.astype(F32)
     gain_one = small[..., 0, :].reshape(d)
     gain_two = small[..., 1, :].reshape(d)
@@ -465,6 +448,8 @@
     _, normed_one = rms_parts(inputs_low.astype(F32))
     normed_one = (normed_one * gain_one).astype(LOW)
     mixed = forward_dot(normed_one, inward_part)
+    mixed, cotangent_here = together(mixed, cotangent)
+    upstream = plane_gather_here(cotangent_here)
     b_part = mixed[:, :feats]
     c_part = mixed[:, feats : 2 * feats]
     x_part = mixed[:, 2 * feats :]
@@ -480,9 +465,7 @@
     branch_feats = (c_part * convolved).astype(LOW)
     branch_got = plane_exchange(branch_feats.reshape(8, tok_rows, feats))
     branch_in = branch_got.transpose(1, 0, 2).reshape(tok_rows, d)
-    branch_in, down_b, ffn_b = together(branch_in, down_b, ffn_got[:, units:])
-    down_parts += [planes_gather(down_b)]
-    ffn_parts += [planes_gather(ffn_b)]
+    branch_in, upstream = together(branch_in, upstream)
     inputs = block_input.astype(F32)
     middle = inputs + forward_dot(branch_in, outward_full)
     scale_two, normal_two = rms_parts(middle)
@@ -506,13 +489,13 @@
     both_own += [planes_scatter(both_term)]
     down_term = over_tokens(hidden_b, upstream).astype(LOW)
     result_far = pair_dot(hidden_a, hidden_b, down_parts[0], down_b, True, False)
-    *parts, down_term, result_far = together(
-        *plane_settle(from_y, from_x, block), down_term, result_far
+    result_near = pair_dot(hidden_a, hidden_b, down_parts[0], down_b, False, False)
+    *parts, down_term, result_far, result_near = together(
+        *plane_settle(from_y, from_x, block), down_term, result_far, result_near
     )
     normed_two_grad = sum(part.astype(F32) for part in parts)
 
     result_got = swap(result_far, "c")
-    result_near = pair_dot(hidden_a, hidden_b, down_parts[0], down_b, False, False)
     middle_grad = cotangent.astype(F32) + norm_back(
         normed_two_grad, normal_two, scale_two, gain_two
     )
@@ -535,11 +518,7 @@
     branch_in_grad = plane_exchange(branch_in_grad.reshape(tok_rows, 8, feats).transpose(1, 0, 2))
     result_y, result_x, result_block = plane_corner(result_near, result_got, True)
     outward_got, outward_near = swap(outward_far, "c"), outward_rows(True)
-    branch_in_grad, result_y, result_x, outward_got, outward_near = together(
-        branch_in_grad, result_y, result_x, outward_got, outward_near
-    )
-    result_parts = plane_settle(result_y, result_x, result_block)
-    outward_y, outward_x, outward_block = plane_corner(outward_near, outward_got)
+    branch_in_grad, outward_got, outward_near = together(branch_in_grad, outward_got, outward_near)
     branch_in_grad = branch_in_grad.reshape(plane_rows, feats).astype(F32)
     c_grad = branch_in_grad * convolved
     conv_grad = branch_in_grad * c_part
@@ -559,34 +538,39 @@
     gated_grad = ext_grad[2:] + jnp.pad(returned, ((plane_rows - 2, 0), (0, 0)))
     mixed_grad = jnp.concatenate([gated_grad * x_part, c_grad, gated_grad * b_part], axis=1)
     mixed_grad = mixed_grad.astype(LOW)
+    mixed_grad, result_y, result_x = together(mixed_grad, result_y, result_x)
+    result_parts = plane_settle(result_y, result_x, result_block)
+    outward_y, outward_x, outward_block = plane_corner(outward_near, outward_got)
     inward_term = over_tokens(normed_one, mixed_grad).astype(LOW)
     inward_term, mixed_grad, outward_y, outward_x, down_own[0], both_own[0], *result_parts = together(
         inward_term, mixed_grad, outward_y, outward_x, down_own[0], both_own[0], *result_parts
     )
     inward_own = planes_scatter(inward_term)
+    down_own += [planes_scatter(down_term)]
     block_output = (middle + sum(part.astype(F32) for part in result_parts)).astype(LOW)
     outward_parts = plane_settle(outward_y, outward_x, outward_block)
     far = against_rows(core_rows(mixed_grad, False), inward_part).astype(LOW)
     got = swap(far, "c")
     near = against_rows(core_rows(mixed_grad, True), inward_part).astype(LOW)
     got, near, both_own[1], *outward_parts = together(got, near, both_own[1], *outward_parts)
+    both_got = [plane_exchange(both_own[0].reshape(8, d_rows, units))]
     outward_own = sum(part.astype(F32) for part in outward_parts).astype(LOW)
     from_y, from_x, block = plane_corner(near, got)
-    from_y, from_x = together(from_y, from_x)
+    from_y, from_x, both_got[0] = together(from_y, from_x, both_got[0])
+    both_got += [plane_exchange(both_own[1].reshape(8, d_rows, units))]
     parts = plane_settle(from_y, from_x, block)
-    down_own += [planes_scatter(after(down_term, inward_own))]
+    *parts, both_got[1], down_own[1] = together(*parts, both_got[1], down_own[1])
     normed_one_grad = sum(part.astype(F32) for part in parts)
     scale_one, normal_one = rms_parts(inputs)
     input_grad = middle_grad + norm_back(normed_one_grad, normal_one, scale_one, gain_one)
 
-    outward_sum = planes_scatter_small(outward_own).astype(F32)
-
-    both_got = [plane_exchange(own.reshape(8, d_rows, units)) for own in both_own]
     down_sum = jnp.concatenate(down_own, axis=0).astype(F32)
-    inward_own = plane_exchange(inward_own.reshape(8, d_rows, 3 * feats))
 
     gate_new, gate_dots = updated_ffn(both_got, 0, gate_weight, gate_first, gate_second, count)
     up_new, up_dots = updated_ffn(both_got, 1, up_weight, up_first, up_second, count)
+    outward_own = planes_scatter_small(after(outward_own, parts[0]))
+    inward_own, _, _, input_grad = together(inward_own, gate_new[0], up_new[0], input_grad)
+    inward_own = plane_exchange(inward_own.reshape(8, d_rows, 3 * feats))
     inward_new, inward_dots = updated_inward(
         inward_own, inward_weight, inward_first, inward_second, count
     )
@@ -594,8 +578,10 @@
     gain_one_grad = inward_dots / own_gains[0]
     gain_two_grad = (gate_dots + up_dots) / own_gains[1]
     gains_grad = jnp.stack([gain_one_grad, gain_two_grad])
-    taps_grad = planes_scatter_small(tap_grads).T
-
+    taps_grad = sum(part.astype(F32) for part in planes_scatter_small(tap_grads)).T
+
+    *outward_own, _ = together(*outward_own, inward_new[0])
+    outward_sum = sum(part.astype(F32) for part in outward_own)
     outward_new = adamw(
         outward_weight, outward_first, outward_second, outward_sum, RATE_MATRIX, DECAY_RATE
     )

time: 767 us -> 734 us (0.957)
  local copies, waits for them, and re-layouts: 121 us -> 90 us
  blocking collectives: 0 us -> 17.6 us
  waiting for transfers between devices: 253 us -> 240 us
    ppermute x55, waiting for transfers between devices: 147 us -> 192 us  [swap(): return lax.ppermute(block, axis, [(0, 1), (1, 0)])]
    ppermute x9 -> x6, waiting for transfers between devices: 30.1 us -> 4.34 us  [shifted(): lax.ppermute(block, 'p', [((i + distance) % count, i) for i in range(coun...]
    all_gather x5, waiting for transfers between devices: 42.8 us -> 25 us  [planes_gather(): return lax.all_gather(block, 'p', axis=0, tiled=True)]
    all_to_all x0 -> x1, blocking collectives: none -> 17.6 us  [plane_exchange(): lax.all_to_all(blocks, PLANE, split_axis=0, concat_axis=0, tiled=True)]
    dynamic_update_slice x16, local copies, waits for them, and re-layouts: 31.2 us -> 15.7 us  [plane_gather(): out = lax.dynamic_update_slice_in_dim(out, piece, at * rows, axis=0)]
    reduce_scatter x5, waiting for transfers between devices: 14.6 us -> 0.01 us  [planes_scatter(): return lax.psum_scatter(term, 'p', scatter_dimension=0, tiled=True)]
    unnamed x172 -> x158, local copies, waits for them, and re-layouts: 56.4 us -> 44.8 us
    ppermute x55, starting transfers between devices: 39.6 us -> 50.2 us  [swap(): return lax.ppermute(block, axis, [(0, 1), (1, 0)])]
  transfers between devices with their start and end apart: 86 -> 79, of which waited for: 30 -> 24; matrix products, arithmetic and copies ran while one was open for 34% -> 32% of each run, Pallas kernels for 13% -> 14%
where the time goes in v4:
time: 734 us; the launch traced here: 724 us
  waiting for transfers between devices  240 us (33%)
  Pallas kernels  98 us (13%)
  matrix products  96.3 us (13%)
  local copies, waits for them, and re-layouts  90 us (12%)
  starting transfers between devices  86.8 us (12%)
  other arithmetic  79.5 us (11%)
  blocking collectives  17.6 us (2%)
  between operations  15.9 us (2%)
    ppermute x55, waiting for transfers between devices, swap(): return lax.ppermute(block, axis, [(0, 1), (1, 0)])  192 us
    dot_general x5, matrix products, over_tokens(): lax.dot_general(operand, partner, (((0,), (0,)), ((), ())), preferred_ele...  54.2 us
    ppermute x55, starting transfers between devices, swap(): return lax.ppermute(block, axis, [(0, 1), (1, 0)])  50.2 us
    pallas_call x4, Pallas kernels, pair_dot(): pl.pallas_call(functools.partial(pair_body, turned), grid=(steps,), in_sp...  44.8 us
    unnamed x158, local copies, waits for them, and re-layouts  44.8 us
    pallas_call x2, Pallas kernels, half_ffn(): pl.pallas_call(half_body, grid=(count // tile,), in_specs=[pl.BlockSpec((...  37.9 us
    all_gather x5, waiting for transfers between devices, planes_gather(): return lax.all_gather(block, 'p', axis=0, tiled=True)  25 us
    add x4, other arithmetic, plane_settle(): near_y + got_y + jnp.concatenate([jnp.zeros_like(from_x), from_x], axis=0)  23 us
  transfers between devices with their start and end apart: 79, of which 24 were waited for; matrix products, arithmetic and copies ran while one was open for 32% of the time, Pallas kernels for 14%

profile of v4, /device:TPU:0, one launch (start us, length us, event | category | flops | bytes accessed | tf_op | source)
XLA Modules:
  0.0 724.2 jit_solution(4014339270506547499)
XLA Ops:
  19.3 17.6 %all_to_all.35 = bf16[8,64,768]{2,1,0:T(8,128)(2,1)} all-to-all(bf16[8,64,768]{2,1,0:T(8,128)(2,1)S(1)} %get-tuple-element.115), channel_id=1, replica_groups=mesh['p'=4,'y'=2,'x'=2,'c'=2] {'y','x','c'}, dimensions={0} | all-to-all | bytes 1572864 | tf_op jit(solution)/shard_map/all_to_all | solution.py:117
  44.4 44.4 %collective-permute-done.1 = bf16[256,2048]{1,0:T(8,128)(2,1)S(1)} collective-permute-done((bf16[256,2048]{1,0:T(8,128)(2,1)S(1)}, bf16[256,2048]{1,0:T(8,128)(2,1)S(1)}, u32[]{:S(2)}, u32[]{:S(2)}) %collective-permute-start.1) | collective-permute-done | bytes 1048608 | tf_op jit(solution)/shard_map/ppermute | solution.py:72
  100.9 9.4 %collective-permute-done.9 = bf16[2,4,5,64]{3,1,2,0:T(4,128)(2,1)S(1)} collective-permute-done((bf16[2,4,5,64]{3,1,2,0:T(4,128)(2,1)S(1)}, bf16[2,4,5,64]{3,1,2,0:T(4,128)(2,1)S(1)}, u32[]{:S(2)}, u32[]{:S(2)}) %collective-permute-start.9) | collective-permute-done | bytes 5152 | tf_op jit(solution)/shard_map/ppermute | solution.py:72
  128.5 16.9 %collective-permute-done.20 = bf16[256,2048]{1,0:T(8,128)(2,1)S(1)} collective-permute-done((bf16[256,2048]{1,0:T(8,128)(2,1)S(1)}, bf16[256,2048]{1,0:T(8,128)(2,1)S(1)}, u32[]{:S(2)}, u32[]{:S(2)}) %collective-permute-start.20) | collective-permute-done | bytes 1048608 | tf_op jit(solution)/shard_map/ppermute | solution.py:72
  154.4 6.3 collective-permute-done.22
  170.4 10.2 %fusion.6 = f32[2048,768]{1,0:T(8,128)S(1)} fusion(bf16[2048,768]{1,0:T(8,128)(2,1)} %all-gather.8.cloned.1.call-done, bf16[2048,2048]{1,0:T(8,128)(2,1)} %copy-done.23, f32[2048]{0:T(1024)S(1)} %mul.494, f32[2048]{0:T(1024)S(1)} %add_rsqrt_fusion), kind=kOutput, calls=%fused_computation.25 | convolution fusion | flops 6459228160 | bytes 17842176 | tf_op jit(solution)/shard_map/dot_general | solution.py:29
  191.8 14.5 %collective-permute-done.13 = bf16[256,2048]{1,0:T(8,128)(2,1)S(1)} collective-permute-done((bf16[256,2048]{1,0:T(8,128)(2,1)}, bf16[256,2048]{1,0:T(8,128)(2,1)S(1)}, u32[]{:S(2)}, u32[]{:S(2)}) %collective-permute-start.13) | collective-permute-done | bytes 1048608 | tf_op jit(solution)/shard_map/ppermute | solution.py:72
  236.9 5.8 multiply_reduce_fusion.4
  250.4 20.3 %collective-permute-done.29 = bf16[256,2048]{1,0:T(8,128)(2,1)S(1)} collective-permute-done((bf16[256,2048]{1,0:T(8,128)(2,1)S(1)}, bf16[256,2048]{1,0:T(8,128)(2,1)S(1)}, u32[]{:S(2)}, u32[]{:S(2)}) %collective-permute-start.29) | collective-permute-done | bytes 1048608 | tf_op jit(solution)/shard_map/ppermute | solution.py:72
  279.2 7.4 %collective-permute-done.31 = bf16[128,2048]{1,0:T(8,128)(2,1)S(1)} collective-permute-done((bf16[128,2048]{1,0:T(8,128)(2,1)S(1)}, bf16[128,2048]{1,0:T(8,128)(2,1)S(1)}, u32[]{:S(2)}, u32[]{:S(2)}) %collective-permute-start.31) | collective-permute-done | bytes 524320 | tf_op jit(solution)/shard_map/ppermute | solution.py:72
  294.5 18.9 %shard_map.399 = (bf16[2048,512]{1,0:T(8,128)(2,1)S(1)}, bf16[2048,1024]{1,0:T(8,128)(2,1)}) custom-call(bf16[2048,2048]{1,0:T(8,128)(2,1)} %constant_dynamic-update-slice_fusion.13.rows_ref, bf16[2048,2048]{1,0:T(8,128)(2,1)} %constant_dynamic-update-slice_fusion.2.upstream_ref, bf16[2048,1024]{1,0:T(8,128)(2,1)} %all-gather.10.cloned.1.call-done.both_ref.c_ref, ...), custom_call_target="tpu_custom_call" | custom-call | flops 12884901888 | bytes 23068672 | tf_op jit(solution)/shard_map/pallas_call | solution.py:198
  313.4 9.2 %convolution_convert_fusion.8 = bf16[512,2048]{1,0:T(8,128)(2,1)} fusion(bf16[2048,512]{1,0:T(8,128)(2,1)S(1)} %get-tuple-element.133.a_ref, bf16[2048,2048]{1,0:T(8,128)(2,1)} %constant_dynamic-update-slice_fusion.2.upstream_ref), kind=kOutput, calls=%fused_computation.18 | convolution fusion | flops 4296015872 | bytes 12582912 | tf_op jit(solution)/shard_map/dot_general | solution.py:33
  324.2 14.1 %convolution_convert_fusion.5 = bf16[2048,1024]{1,0:T(8,128)(2,1)} fusion(bf16[2048,2048]{1,0:T(8,128)(2,1)} %constant_dynamic-update-slice_fusion.13.rows_ref, bf16[2048,1024]{1,0:T(8,128)(2,1)} %get-tuple-element.132.a_ref), kind=kOutput, calls=%fused_computation.10 | convolution fusion | flops 8592031744 | bytes 16777216 | tf_op jit(solution)/shard_map/dot_general | solution.py:33
  338.3 25.0 %all-gather.12.cloned.1.call-done.both_ref.e_ref = bf16[2048,1024]{1,0:T(8,128)(2,1)} async-done(((bf16[512,1024]{1,0:T(8,128)(2,1)}), bf16[2048,1024]{1,0:T(8,128)(2,1)}) %all-gather.12.cloned.1.call-update) | async-done | bytes 4194320 | tf_op jit(solution)/shard_map/all_gather | solution.py:156
  364.9 18.9 %shard_map.400 = (bf16[2048,512]{1,0:T(8,128)(2,1)S(1)}, bf16[2048,1024]{1,0:T(8,128)(2,1)}) custom-call(bf16[2048,2048]{1,0:T(8,128)(2,1)} %constant_dynamic-update-slice_fusion.13.rows_ref, bf16[2048,2048]{1,0:T(8,128)(2,1)} %constant_dynamic-update-slice_fusion.2.upstream_ref, bf16[2048,1024]{1,0:T(8,128)(2,1)} %all-gather.12.cloned.1.call-done.both_ref.e_ref, ...), custom_call_target="tpu_custom_call" | custom-call | flops 12884901888 | bytes 23068672 | tf_op jit(solution)/shard_map/pallas_call | solution.py:198
  383.8 14.5 %shard_map.401 = bf16[1024,2048]{1,0:T(8,128)(2,1)} custom-call(bf16[2048,1024]{1,0:T(8,128)(2,1)} %get-tuple-element.132.a_ref, bf16[2048,1024]{1,0:T(8,128)(2,1)} %get-tuple-element.140.b_ref, bf16[2048,1024]{1,0:T(8,128)(2,1)} %all-gather.10.cloned.1.call-done.both_ref.c_ref, bf16[2048,1024]{1,0:T(8,128)(2,1)} %all-gather.12.cloned.1.call-done.both_ref.e_ref), custom_call_target="tpu_custom_call" | custom-call | flops 8589934592 | bytes 16777216 | tf_op jit(solution)/shard_map/pallas_call | solution.py:234
  398.9 13.2 %shard_map.402 = bf16[1024,2048]{1,0:T(8,128)(2,1)S(1)} custom-call(bf16[2048,1024]{1,0:T(8,128)(2,1)} %get-tuple-element.132.a_ref, bf16[2048,1024]{1,0:T(8,128)(2,1)} %get-tuple-element.140.b_ref, bf16[2048,1024]{1,0:T(8,128)(2,1)} %all-gather.10.cloned.1.call-done.both_ref.c_ref, bf16[2048,1024]{1,0:T(8,128)(2,1)} %all-gather.12.cloned.1.call-done.both_ref.e_ref), custom_call_target="tpu_custom_call" | custom-call | flops 8589934592 | bytes 16777216 | tf_op jit(solution)/shard_map/pallas_call | solution.py:234
  418.5 12.7 %convolution_convert_fusion.4 = bf16[2048,1024]{1,0:T(8,128)(2,1)} fusion(bf16[2048,2048]{1,0:T(8,128)(2,1)} %constant_dynamic-update-slice_fusion.13.rows_ref, bf16[2048,1024]{1,0:T(8,128)(2,1)S(1)} %copy-done.65), kind=kOutput, calls=%fused_computation.9 | convolution fusion | flops 8592031744 | bytes 16777216 | tf_op jit(solution)/shard_map/dot_general | solution.py:33
  432.8 8.4 %shard_map.404 = bf16[1024,2048]{1,0:T(8,128)(2,1)} custom-call(bf16[2048,512]{1,0:T(8,128)(2,1)S(1)} %copy-done.18, bf16[2048,512]{1,0:T(8,128)(2,1)S(1)} %get-tuple-element.143.b_ref, bf16[512,2048]{1,0:T(8,128)(2,1)} %bitcast.90, bf16[512,2048]{1,0:T(8,128)(2,1)} %all-gather.14.cloned.1.call-done.down_ref.e_ref), custom_call_target="tpu_custom_call" | custom-call | flops 4294967296 | bytes 10485760 | tf_op jit(solution)/shard_map/pallas_call | solution.py:234
  441.2 8.6 %shard_map.403 = bf16[1024,2048]{1,0:T(8,128)(2,1)} custom-call(bf16[2048,512]{1,0:T(8,128)(2,1)S(1)} %copy-done.19, bf16[2048,512]{1,0:T(8,128)(2,1)S(1)} %get-tuple-element.143.b_ref, bf16[512,2048]{1,0:T(8,128)(2,1)} %bitcast.91, bf16[512,2048]{1,0:T(8,128)(2,1)} %all-gather.14.cloned.1.call-done.down_ref.e_ref), custom_call_target="tpu_custom_call" | custom-call | flops 4294967296 | bytes 10485760 | tf_op jit(solution)/shard_map/pallas_call | solution.py:234
  456.3 9.1 %convolution_convert_fusion.7 = bf16[512,2048]{1,0:T(8,128)(2,1)} fusion(bf16[2048,512]{1,0:T(8,128)(2,1)S(1)} %get-tuple-element.143.b_ref, bf16[2048,2048]{1,0:T(8,128)(2,1)} %constant_dynamic-update-slice_fusion.2.upstream_ref), kind=kOutput, calls=%fused_computation.17 | convolution fusion | flops 4296015872 | bytes 12582912 | tf_op jit(solution)/shard_map/dot_general | solution.py:33
  465.5 14.8 %collective-permute-done.40 = bf16[256,2048]{1,0:T(8,128)(2,1)} collective-permute-done((bf16[256,2048]{1,0:T(8,128)(2,1)}, bf16[256,2048]{1,0:T(8,128)(2,1)}, u32[]{:S(2)}, u32[]{:S(2)}) %collective-permute-start.40) | collective-permute-done | bytes 1048608 | tf_op jit(solution)/shard_map/ppermute | solution.py:72
  490.2 6.7 convolution_convert_fusion.9
  511.4 9.8 %all-to-all-done.3 = bf16[8,256,256]{2,1,0:T(8,128)(2,1)S(1)} async-done(((bf16[8,256,256]{2,1,0:T(8,128)(2,1)}), bf16[8,256,256]{2,1,0:T(8,128)(2,1)S(1)}, u32[]{:S(2)}, u32[]{:S(2)}) %all-to-all-start.3) | async-done | bytes 1048608 | tf_op jit(solution)/shard_map/all_to_all | solution.py:117
  543.4 9.1 %convolution_convert_fusion.6 = bf16[2048,768]{1,0:T(8,128)(2,1)} fusion(bf16[2048,768]{1,0:T(8,128)(2,1)S(1)} %pad_maximum_fusion, bf16[2048,2048]{1,0:T(8,128)(2,1)S(1)} %bitcast.93, f32[2048]{0:T(1024)S(1)} %copy-done.51, f32[2048]{0:T(1024)S(1)} %copy-done.53), kind=kOutput, calls=%fused_computation.11 | convolution fusion | flops 6460801024 | bytes 14696448 | tf_op jit(solution)/shard_map/dot_general | solution.py:33
  552.4 14.0 %collective-permute-done.49 = bf16[256,2048]{1,0:T(8,128)(2,1)} collective-permute-done((bf16[256,2048]{1,0:T(8,128)(2,1)}, bf16[256,2048]{1,0:T(8,128)(2,1)}, u32[]{:S(2)}, u32[]{:S(2)}) %collective-permute-start.49) | collective-permute-done | bytes 1048608 | tf_op jit(solution)/shard_map/ppermute | solution.py:72
  573.9 6.4 pad_add_fusion.3
  587.0 7.8 %convolution_convert_fusion.2 = bf16[1024,2048]{1,0:T(8,128)(2,1)} fusion(bf16[2048,768]{1,0:T(8,128)(2,1)} %all-gather.8.cloned.1.call-done, bf16[256,768]{1,0:T(8,128)(2,1)} %get-tuple-element.240, bf16[256,768]{1,0:T(8,128)(2,1)} %get-tuple-element.241, bf16[256,768]{1,0:T(8,128)(2,1)} %get-tuple-element.242, bf16[256,768]{1,0:T(8,128)(2,1)S(1)} %get-tuple-element.239), kind=kOutput, calls=%fused_computation.7 | convolution fusion | flops 3229614080 | bytes 8912896 | tf_op jit(solution)/shard_map/dot_general | solution.py:39
  594.8 11.7 %collective-permute-done.52 = bf16[256,2048]{1,0:T(8,128)(2,1)S(1)} collective-permute-done((bf16[256,2048]{1,0:T(8,128)(2,1)}, bf16[256,2048]{1,0:T(8,128)(2,1)S(1)}, u32[]{:S(2)}, u32[]{:S(2)}) %collective-permute-start.52) | collective-permute-done | bytes 1048608 | tf_op jit(solution)/shard_map/ppermute | solution.py:72
  629.4 5.9 pad_add_fusion.1
  644.4 18.4 %collective-permute-done.56 = bf16[256,2048]{1,0:T(8,128)(2,1)} collective-permute-done((bf16[256,2048]{1,0:T(8,128)(2,1)}, bf16[256,2048]{1,0:T(8,128)(2,1)}, u32[]{:S(2)}, u32[]{:S(2)}) %collective-permute-start.56) | collective-permute-done | bytes 1048608 | tf_op jit(solution)/shard_map/ppermute | solution.py:72
  693.9 7.2 multiply_subtract_fusion
  (430 shorter events, 291.1 us)
Async XLA Ops:
  7.2 82.6 %all-gather.6.cloned.1.call-start = ((), (), s32[]{:S(2)}) async-start(), calls=%async_computation.12 | async-start | bytes 4259840 | tf_op jit(solution)/shard_map/all_gather | solution.py:156
  37.0 52.8 %all-to-all-start.1 = ((bf16[8,64,2048]{2,1,0:T(8,128)(2,1)}), bf16[8,64,2048]{2,1,0:T(8,128)(2,1)S(1)}, u32[]{:S(2)}, u32[]{:S(2)}) async-start(bf16[8,64,2048]{2,1,0:T(8,128)(2,1)} %copy-done.9), calls=%async_computation.1 | async-start | bytes 4194304 | tf_op jit(solution)/shard_map/all_to_all | solution.py:117
  40.7 129.7 %all-gather.8.cloned.1.call-start = ((), (), s32[]{:S(2)}) async-start(), calls=%async_computation.13 | async-start | bytes 3932160 | tf_op jit(solution)/shard_map/all_gather | solution.py:156
  41.2 47.6 %collective-permute-start.1 = (bf16[256,2048]{1,0:T(8,128)(2,1)S(1)}, bf16[256,2048]{1,0:T(8,128)(2,1)S(1)}, u32[]{:S(2)}, u32[]{:S(2)}) collective-permute-start(bf16[256,2048]{1,0:T(8,128)(2,1)S(1)} %copy-done.26), channel_id=1, source_target_pairs={{0,4},{4,0},{1,5},{5,1},{2,6},{6,2},{3,7},{7,3},{8,12},{12,8},{9,1... | collective-permute-start | bytes 3145736 | tf_op jit(solution)/shard_map/ppermute | solution.py:72
  42.9 46.9 %collective-permute-start = (bf16[256,2048]{1,0:T(8,128)(2,1)S(1)}, bf16[256,2048]{1,0:T(8,128)(2,1)}, u32[]{:S(2)}, u32[]{:S(2)}) collective-permute-start(bf16[256,2048]{1,0:T(8,128)(2,1)S(1)} %copy-done.26), channel_id=1, source_target_pairs={{0,2},{2,0},{1,3},{3,1},{4,6},{6,4},{5,7},{7,5},{8,10},{10,8},{9,1... | collective-permute-start | bytes 3145736 | tf_op jit(solution)/shard_map/ppermute | solution.py:72
  89.8 204.7 %all-gather.10.cloned.1.call-start = ((), (), s32[]{:S(2)}) async-start(), calls=%async_computation.14 | async-start | bytes 5242880 | tf_op jit(solution)/shard_map/all_gather | solution.py:156
  91.4 246.9 %all-gather.14.cloned.1.call-start = ((), (), s32[]{:S(2)}) async-start(), calls=%async_computation.16 | async-start | bytes 2621440 | tf_op jit(solution)/shard_map/all_gather | solution.py:156
  92.0 271.3 %all-gather.12.cloned.1.call-start = ((), (), s32[]{:S(2)}) async-start(), calls=%async_computation.15 | async-start | bytes 5242880 | tf_op jit(solution)/shard_map/all_gather | solution.py:156
  119.4 46.5 %collective-permute-start.24 = (bf16[256,2048]{1,0:T(8,128)(2,1)S(1)}, bf16[256,2048]{1,0:T(8,128)(2,1)}, u32[]{:S(2)}, u32[]{:S(2)}) collective-permute-start(bf16[256,2048]{1,0:T(8,128)(2,1)S(1)} %bitcast.103), channel_id=1, source_target_pairs={{0,1},{1,0},{2,3},{3,2},{4,5},{5,4},{6,7},{7,6},{8,9},{9,8},{10,11... | collective-permute-start | bytes 3145736 | tf_op jit(solution)/shard_map/ppermute | solution.py:72
  119.6 29.4 %collective-permute-start.21 = (bf16[256,2048]{1,0:T(8,128)(2,1)S(1)}, bf16[256,2048]{1,0:T(8,128)(2,1)S(1)}, u32[]{:S(2)}, u32[]{:S(2)}) collective-permute-start(bf16[256,2048]{1,0:T(8,128)(2,1)S(1)} %bitcast.104), channel_id=1, source_target_pairs={{0,4},{4,0},{1,5},{5,1},{2,6},{6,2},{3,7},{7,3},{8,12},{12,8},{9,1... | collective-permute-start | bytes 3145736 | tf_op jit(solution)/shard_map/ppermute | solution.py:72
  180.6 25.7 %collective-permute-start.13 = (bf16[256,2048]{1,0:T(8,128)(2,1)}, bf16[256,2048]{1,0:T(8,128)(2,1)S(1)}, u32[]{:S(2)}, u32[]{:S(2)}) collective-permute-start(bf16[256,2048]{1,0:T(8,128)(2,1)} %param.24), channel_id=1, source_target_pairs={{0,4},{4,0},{1,5},{5,1},{2,6},{6,2},{3,7},{7,3},{8,12},{12,8},{9,1... | collective-permute-start | bytes 3145736 | tf_op jit(solution)/shard_map/ppermute | solution.py:72
  181.9 26.4 %collective-permute-start.12 = (bf16[256,2048]{1,0:T(8,128)(2,1)}, bf16[256,2048]{1,0:T(8,128)(2,1)S(1)}, u32[]{:S(2)}, u32[]{:S(2)}) collective-permute-start(bf16[256,2048]{1,0:T(8,128)(2,1)} %param.24), channel_id=1, source_target_pairs={{0,2},{2,0},{1,3},{3,1},{4,6},{6,4},{5,7},{7,5},{8,10},{10,8},{9,1... | collective-permute-start | bytes 3145736 | tf_op jit(solution)/shard_map/ppermute | solution.py:72
  185.6 45.8 %collective-permute-start.16 = (bf16[256,2048]{1,0:T(8,128)(2,1)}, bf16[256,2048]{1,0:T(8,128)(2,1)}, u32[]{:S(2)}, u32[]{:S(2)}) collective-permute-start(bf16[256,2048]{1,0:T(8,128)(2,1)} %param.24), channel_id=1, source_target_pairs={{0,1},{1,0},{2,3},{3,2},{4,5},{5,4},{6,7},{7,6},{8,9},{9,8},{10,11... | collective-permute-start | bytes 3145736 | tf_op jit(solution)/shard_map/ppermute | solution.py:72
  218.2 334.2 %reduce-scatter.6.cloned.1.call-start = ((), (), s32[]{:S(2)}) async-start(), calls=%async_computation.17 | async-start | bytes 2621440 | tf_op jit(solution)/shard_map/reduce_scatter | solution.py:160
  244.0 26.7 %collective-permute-start.29 = (bf16[256,2048]{1,0:T(8,128)(2,1)S(1)}, bf16[256,2048]{1,0:T(8,128)(2,1)S(1)}, u32[]{:S(2)}, u32[]{:S(2)}) collective-permute-start(bf16[256,2048]{1,0:T(8,128)(2,1)S(1)} %get-tuple-element.222), channel_id=1, source_target_pairs={{0,4},{4,0},{1,5},{5,1},{2,6},{6,2},{3,7},{7,3},{8,12},{12,8},{9,1... | collective-permute-start | bytes 3145736 | tf_op jit(solution)/shard_map/ppermute | solution.py:72
  246.9 27.5 %collective-permute-start.28 = (bf16[256,2048]{1,0:T(8,128)(2,1)S(1)}, bf16[256,2048]{1,0:T(8,128)(2,1)S(1)}, u32[]{:S(2)}, u32[]{:S(2)}) collective-permute-start(bf16[256,2048]{1,0:T(8,128)(2,1)S(1)} %get-tuple-element.222), channel_id=1, source_target_pairs={{0,2},{2,0},{1,3},{3,1},{4,6},{6,4},{5,7},{7,5},{8,10},{10,8},{9,1... | collective-permute-start | bytes 3145736 | tf_op jit(solution)/shard_map/ppermute | solution.py:72
  324.0 228.5 %reduce-scatter.8.cloned.1.call-start = ((), (), s32[]{:S(2)}) async-start(), calls=%async_computation.18 | async-start | bytes 5242880 | tf_op jit(solution)/shard_map/reduce_scatter | solution.py:160
  398.4 196.4 %reduce-scatter.12.cloned.1.call-start = ((), (), s32[]{:S(2)}) async-start(), calls=%async_computation.20 | async-start | bytes 5242880 | tf_op jit(solution)/shard_map/reduce_scatter | solution.py:160
  415.5 34.4 %collective-permute-start.38 = (bf16[128,2048]{1,0:T(8,128)(2,1)}, bf16[128,2048]{1,0:T(8,128)(2,1)}, u32[]{:S(2)}, u32[]{:S(2)}) collective-permute-start(bf16[128,2048]{1,0:T(8,128)(2,1)} %get-tuple-element.263), channel_id=1, source_target_pairs={{0,2},{2,0},{1,3},{3,1},{4,6},{6,4},{5,7},{7,5},{8,10},{10,8},{9,1... | collective-permute-start | bytes 1572872 | tf_op jit(solution)/shard_map/ppermute | solution.py:72
  417.0 32.9 %collective-permute-start.37 = (bf16[128,2048]{1,0:T(8,128)(2,1)}, bf16[128,2048]{1,0:T(8,128)(2,1)}, u32[]{:S(2)}, u32[]{:S(2)}) collective-permute-start(bf16[128,2048]{1,0:T(8,128)(2,1)} %get-tuple-element.264), channel_id=1, source_target_pairs={{0,4},{4,0},{1,5},{5,1},{2,6},{6,2},{3,7},{7,3},{8,12},{12,8},{9,1... | collective-permute-start | bytes 1572872 | tf_op jit(solution)/shard_map/ppermute | solution.py:72
  456.3 188.1 %reduce-scatter.14.cloned.1.call-start = ((), (), s32[]{:S(2)}) async-start(), calls=%async_computation.21 | async-start | bytes 2621440 | tf_op jit(solution)/shard_map/reduce_scatter | solution.py:160
  505.3 184.8 %reduce-scatter.10.cloned.1.call-start = ((), (), s32[]{:S(2)}) async-start(), calls=%async_computation.19 | async-start | bytes 3932160 | tf_op jit(solution)/shard_map/reduce_scatter | solution.py:160
  508.0 27.1 %collective-permute-start.45 = (bf16[128,2048]{1,0:T(8,128)(2,1)}, bf16[128,2048]{1,0:T(8,128)(2,1)}, u32[]{:S(2)}, u32[]{:S(2)}) collective-permute-start(bf16[128,2048]{1,0:T(8,128)(2,1)} %get-tuple-element.260), channel_id=1, source_target_pairs={{0,2},{2,0},{1,3},{3,1},{4,6},{6,4},{5,7},{7,5},{8,10},{10,8},{9,1... | collective-permute-start | bytes 1572872 | tf_op jit(solution)/shard_map/ppermute | solution.py:72
  573.8 33.0 %collective-permute-start.50 = (bf16[1024,2048]{1,0:T(8,128)(2,1)}, bf16[1024,2048]{1,0:T(8,128)(2,1)}, u32[]{:S(2)}, u32[]{:S(2)}) collective-permute-start(bf16[1024,2048]{1,0:T(8,128)(2,1)} %convolution_convert_fusion.3), channel_id=1, source_target_pairs={{0,1},{1,0},{2,3},{3,2},{4,5},{5,4},{6,7},{7,6},{8,9},{9,8},{10,11... | collective-permute-start | bytes 12582920 | tf_op jit(solution)/shard_map/ppermute | solution.py:72
  580.3 26.2 %collective-permute-start.52 = (bf16[256,2048]{1,0:T(8,128)(2,1)}, bf16[256,2048]{1,0:T(8,128)(2,1)S(1)}, u32[]{:S(2)}, u32[]{:S(2)}) collective-permute-start(bf16[256,2048]{1,0:T(8,128)(2,1)} %get-tuple-element.230), channel_id=1, source_target_pairs={{0,4},{4,0},{1,5},{5,1},{2,6},{6,2},{3,7},{7,3},{8,12},{12,8},{9,1... | collective-permute-start | bytes 3145736 | tf_op jit(solution)/shard_map/ppermute | solution.py:72
  580.5 26.3 %collective-permute-start.51 = (bf16[256,2048]{1,0:T(8,128)(2,1)}, bf16[256,2048]{1,0:T(8,128)(2,1)}, u32[]{:S(2)}, u32[]{:S(2)}) collective-permute-start(bf16[256,2048]{1,0:T(8,128)(2,1)} %get-tuple-element.231), channel_id=1, source_target_pairs={{0,2},{2,0},{1,3},{3,1},{4,6},{6,4},{5,7},{7,5},{8,10},{10,8},{9,1... | collective-permute-start | bytes 3145736 | tf_op jit(solution)/shard_map/ppermute | solution.py:72
  583.2 38.0 %all-to-all-start.4 = ((bf16[8,64,1024]{2,1,0:T(8,128)(2,1)}), bf16[8,64,1024]{2,1,0:T(8,128)(2,1)S(1)}, u32[]{:S(2)}, u32[]{:S(2)}) async-start(bf16[8,64,1024]{2,1,0:T(8,128)(2,1)} %bitcast.27), calls=%async_computation.8 | async-start | bytes 2097152 | tf_op jit(solution)/shard_map/all_to_all | solution.py:117
  635.3 27.5 %collective-permute-start.56 = (bf16[256,2048]{1,0:T(8,128)(2,1)}, bf16[256,2048]{1,0:T(8,128)(2,1)}, u32[]{:S(2)}, u32[]{:S(2)}) collective-permute-start(bf16[256,2048]{1,0:T(8,128)(2,1)} %get-tuple-element.227), channel_id=1, source_target_pairs={{0,4},{4,0},{1,5},{5,1},{2,6},{6,2},{3,7},{7,3},{8,12},{12,8},{9,1... | collective-permute-start | bytes 3145736 | tf_op jit(solution)/shard_map/ppermute | solution.py:72
  637.1 25.6 %collective-permute-start.55 = (bf16[256,2048]{1,0:T(8,128)(2,1)}, bf16[256,2048]{1,0:T(8,128)(2,1)}, u32[]{:S(2)}, u32[]{:S(2)}) collective-permute-start(bf16[256,2048]{1,0:T(8,128)(2,1)} %get-tuple-element.228), channel_id=1, source_target_pairs={{0,2},{2,0},{1,3},{3,1},{4,6},{6,4},{5,7},{7,5},{8,10},{10,8},{9,1... | collective-permute-start | bytes 3145736 | tf_op jit(solution)/shard_map/ppermute | solution.py:72
  664.8 48.3 %collective-permute-start.59 = (bf16[64,2048]{1,0:T(8,128)(2,1)}, bf16[64,2048]{1,0:T(8,128)(2,1)}, u32[]{:S(2)}, u32[]{:S(2)}) collective-permute-start(bf16[64,2048]{1,0:T(8,128)(2,1)} %get-tuple-element.252), channel_id=1, source_target_pairs={{24,0},{0,8},{8,16},{16,24},{25,1},{1,9},{9,17},{17,25},{26,2},{2,... | collective-permute-start | bytes 786440 | tf_op jit(solution)/shard_map/ppermute | solution.py:165
  667.0 46.1 %collective-permute-start.58 = (bf16[64,2048]{1,0:T(8,128)(2,1)}, bf16[64,2048]{1,0:T(8,128)(2,1)}, u32[]{:S(2)}, u32[]{:S(2)}) collective-permute-start(bf16[64,2048]{1,0:T(8,128)(2,1)} %get-tuple-element.253), channel_id=1, source_target_pairs={{16,0},{24,8},{0,16},{8,24},{17,1},{25,9},{1,17},{9,25},{18,2},{26... | collective-permute-start | bytes 786440 | tf_op jit(solution)/shard_map/ppermute | solution.py:165
  668.6 44.5 %collective-permute-start.57 = (bf16[64,2048]{1,0:T(8,128)(2,1)}, bf16[64,2048]{1,0:T(8,128)(2,1)}, u32[]{:S(2)}, u32[]{:S(2)}) collective-permute-start(bf16[64,2048]{1,0:T(8,128)(2,1)} %get-tuple-element.254), channel_id=1, source_target_pairs={{8,0},{16,8},{24,16},{0,24},{9,1},{17,9},{25,17},{1,25},{10,2},{18... | collective-permute-start | bytes 786440 | tf_op jit(solution)/shard_map/ppermute | solution.py:165
  (117 other events, 1308.3 us)
Sparse Core Ops, SparseCore 0:
  14.0 70.5 all-gather.5
  89.9 63.7 all-gather.7
  155.9 79.3 all-gather.9
  237.3 44.4 all-gather.13
  283.8 79.4 all-gather.11
  366.0 42.3 reduce-scatter.5
  410.9 76.0 reduce-scatter.7
  489.3 77.3 reduce-scatter.11
  569.6 44.3 reduce-scatter.13
  616.2 68.3 reduce-scatter.9

commit v5 on v4

--- a/solution.py
+++ b/solution.py
@@ -518,7 +518,9 @@
     branch_in_grad = plane_exchange(branch_in_grad.reshape(tok_rows, 8, feats).transpose(1, 0, 2))
     result_y, result_x, result_block = plane_corner(result_near, result_got, True)
     outward_got, outward_near = swap(outward_far, "c"), outward_rows(True)
-    branch_in_grad, outward_got, outward_near = together(branch_in_grad, outward_got, outward_near)
+    branch_in_grad, outward_got, outward_near, down_own[0], both_own[0] = together(
+        branch_in_grad, outward_got, outward_near, down_own[0], both_own[0]
+    )
     branch_in_grad = branch_in_grad.reshape(plane_rows, feats).astype(F32)
     c_grad = branch_in_grad * convolved
     conv_grad = branch_in_grad * c_part
@@ -542,35 +544,34 @@
     result_parts = plane_settle(result_y, result_x, result_block)
     outward_y, outward_x, outward_block = plane_corner(outward_near, outward_got)
     inward_term = over_tokens(normed_one, mixed_grad).astype(LOW)
-    inward_term, mixed_grad, outward_y, outward_x, down_own[0], both_own[0], *result_parts = together(
-        inward_term, mixed_grad, outward_y, outward_x, down_own[0], both_own[0], *result_parts
+    both_got = [plane_exchange(both_own[0].reshape(8, d_rows, units))]
+    inward_term, mixed_grad, outward_y, outward_x, both_own[1], both_got[0], *result_parts = together(
+        inward_term, mixed_grad, outward_y, outward_x, both_own[1], both_got[0], *result_parts
     )
     inward_own = planes_scatter(inward_term)
-    down_own += [planes_scatter(down_term)]
     block_output = (middle + sum(part.astype(F32) for part in result_parts)).astype(LOW)
     outward_parts = plane_settle(outward_y, outward_x, outward_block)
     far = against_rows(core_rows(mixed_grad, False), inward_part).astype(LOW)
     got = swap(far, "c")
     near = against_rows(core_rows(mixed_grad, True), inward_part).astype(LOW)
-    got, near, both_own[1], *outward_parts = together(got, near, both_own[1], *outward_parts)
-    both_got = [plane_exchange(both_own[0].reshape(8, d_rows, units))]
+    both_got += [plane_exchange(both_own[1].reshape(8, d_rows, units))]
+    got, near, down_term, *outward_parts = together(got, near, down_term, *outward_parts)
+    down_own += [planes_scatter(down_term)]
     outward_own = sum(part.astype(F32) for part in outward_parts).astype(LOW)
     from_y, from_x, block = plane_corner(near, got)
-    from_y, from_x, both_got[0] = together(from_y, from_x, both_got[0])
-    both_got += [plane_exchange(both_own[1].reshape(8, d_rows, units))]
-    parts = plane_settle(from_y, from_x, block)
-    *parts, both_got[1], down_own[1] = together(*parts, both_got[1], down_own[1])
+    from_y, from_x, both_got[1] = together(from_y, from_x, both_got[1])
+
+    gate_new, gate_dots = updated_ffn(both_got, 0, gate_weight, gate_first, gate_second, count)
+    up_new, up_dots = updated_ffn(both_got, 1, up_weight, up_first, up_second, count)
+    inward_own = plane_exchange(inward_own.reshape(8, d_rows, 3 * feats))
+    outward_own = planes_scatter_small(outward_own)
+    *parts, inward_own, gate_dots, up_dots = together(
+        *plane_settle(from_y, from_x, block), inward_own, gate_dots, up_dots
+    )
     normed_one_grad = sum(part.astype(F32) for part in parts)
     scale_one, normal_one = rms_parts(inputs)
     input_grad = middle_grad + norm_back(normed_one_grad, normal_one, scale_one, gain_one)
-
     down_sum = jnp.concatenate(down_own, axis=0).astype(F32)
-
-    gate_new, gate_dots = updated_ffn(both_got, 0, gate_weight, gate_first, gate_second, count)
-    up_new, up_dots = updated_ffn(both_got, 1, up_weight, up_first, up_second, count)
-    outward_own = planes_scatter_small(after(outward_own, parts[0]))
-    inward_own, _, _, input_grad = together(inward_own, gate_new[0], up_new[0], input_grad)
-    inward_own = plane_exchange(inward_own.reshape(8, d_rows, 3 * feats))
     inward_new, inward_dots = updated_inward(
         inward_own, inward_weight, inward_first, inward_second, count
     )

time: 734 us -> 733 us (level)
  the two profiles are of different devices: /device:TPU:0 before, /device:TPU:9 now
where the time goes in v5:
time: 733 us; the launch traced here: 723 us
  waiting for transfers between devices  220 us (30%)
  starting transfers between devices  100 us (14%)
  local copies, waits for them, and re-layouts  98.6 us (13%)
  Pallas kernels  98.1 us (13%)
  matrix products  94.5 us (13%)
  other arithmetic  81.1 us (11%)
  between operations  15.6 us (2%)
  blocking collectives  15.5 us (2%)
    ppermute x55, waiting for transfers between devices, swap(): return lax.ppermute(block, axis, [(0, 1), (1, 0)])  165 us
    dot_general x5, matrix products, over_tokens(): lax.dot_general(operand, partner, (((0,), (0,)), ((), ())), preferred_ele...  54.4 us
    unnamed x166, local copies, waits for them, and re-layouts  52.1 us
    ppermute x55, starting transfers between devices, swap(): return lax.ppermute(block, axis, [(0, 1), (1, 0)])  50.1 us
    pallas_call x4, Pallas kernels, pair_dot(): pl.pallas_call(functools.partial(pair_body, turned), grid=(steps,), in_sp...  44.8 us
    pallas_call x2, Pallas kernels, half_ffn(): pl.pallas_call(half_body, grid=(count // tile,), in_specs=[pl.BlockSpec((...  37.9 us
    all_to_all x6, starting transfers between devices, plane_exchange(): lax.all_to_all(blocks, PLANE, split_axis=0, concat_axis=0, tiled=True)  30.6 us
    add x4, other arithmetic, plane_settle(): near_y + got_y + jnp.concatenate([jnp.zeros_like(from_x), from_x], axis=0)  22.4 us
  transfers between devices with their start and end apart: 79, of which 25 were waited for; matrix products, arithmetic and copies ran while one was open for 33% of the time, Pallas kernels for 14%

profile of v5, /device:TPU:9, one launch (start us, length us, event | category | flops | bytes accessed | tf_op | source)
XLA Modules:
  0.0 723.2 jit_solution(18225876149430322276)
XLA Ops:
  19.3 15.5 %all_to_all.35 = bf16[8,64,768]{2,1,0:T(8,128)(2,1)} all-to-all(bf16[8,64,768]{2,1,0:T(8,128)(2,1)S(1)} %get-tuple-element.115), channel_id=1, replica_groups=mesh['p'=4,'y'=2,'x'=2,'c'=2] {'y','x','c'}, dimensions={0} | all-to-all | bytes 1572864 | tf_op jit(solution)/shard_map/all_to_all | solution.py:117
  42.9 44.4 %collective-permute-done.1 = bf16[256,2048]{1,0:T(8,128)(2,1)S(1)} collective-permute-done((bf16[256,2048]{1,0:T(8,128)(2,1)S(1)}, bf16[256,2048]{1,0:T(8,128)(2,1)S(1)}, u32[]{:S(2)}, u32[]{:S(2)}) %collective-permute-start.1) | collective-permute-done | bytes 1048608 | tf_op jit(solution)/shard_map/ppermute | solution.py:72
  97.8 9.3 %collective-permute-done.9 = bf16[2,4,5,64]{3,1,2,0:T(4,128)(2,1)S(1)} collective-permute-done((bf16[2,4,5,64]{3,1,2,0:T(4,128)(2,1)S(1)}, bf16[2,4,5,64]{3,1,2,0:T(4,128)(2,1)S(1)}, u32[]{:S(2)}, u32[]{:S(2)}) %collective-permute-start.9) | collective-permute-done | bytes 5152 | tf_op jit(solution)/shard_map/ppermute | solution.py:72
  125.4 16.0 %collective-permute-done.20 = bf16[256,2048]{1,0:T(8,128)(2,1)S(1)} collective-permute-done((bf16[256,2048]{1,0:T(8,128)(2,1)S(1)}, bf16[256,2048]{1,0:T(8,128)(2,1)S(1)}, u32[]{:S(2)}, u32[]{:S(2)}) %collective-permute-start.20) | collective-permute-done | bytes 1048608 | tf_op jit(solution)/shard_map/ppermute | solution.py:72
  167.5 10.2 %fusion.6 = f32[2048,768]{1,0:T(8,128)S(1)} fusion(bf16[2048,768]{1,0:T(8,128)(2,1)} %all-gather.8.cloned.1.call-done, bf16[2048,2048]{1,0:T(8,128)(2,1)} %copy-done.22, f32[2048]{0:T(1024)S(1)} %mul.494, f32[2048]{0:T(1024)S(1)} %add_rsqrt_fusion), kind=kOutput, calls=%fused_computation.25 | convolution fusion | flops 6459228160 | bytes 17842176 | tf_op jit(solution)/shard_map/dot_general | solution.py:29
  188.4 14.4 %collective-permute-done.13 = bf16[256,2048]{1,0:T(8,128)(2,1)S(1)} collective-permute-done((bf16[256,2048]{1,0:T(8,128)(2,1)}, bf16[256,2048]{1,0:T(8,128)(2,1)S(1)}, u32[]{:S(2)}, u32[]{:S(2)}) %collective-permute-start.13) | collective-permute-done | bytes 1048608 | tf_op jit(solution)/shard_map/ppermute | solution.py:72
  220.4 6.1 collective-permute-start.19
  235.9 5.8 multiply_reduce_fusion.4
  246.1 22.1 %collective-permute-done.29 = bf16[256,2048]{1,0:T(8,128)(2,1)S(1)} collective-permute-done((bf16[256,2048]{1,0:T(8,128)(2,1)S(1)}, bf16[256,2048]{1,0:T(8,128)(2,1)S(1)}, u32[]{:S(2)}, u32[]{:S(2)}) %collective-permute-start.29) | collective-permute-done | bytes 1048608 | tf_op jit(solution)/shard_map/ppermute | solution.py:72
  297.4 19.0 %shard_map.399 = (bf16[2048,512]{1,0:T(8,128)(2,1)S(1)}, bf16[2048,1024]{1,0:T(8,128)(2,1)}) custom-call(bf16[2048,2048]{1,0:T(8,128)(2,1)} %constant_dynamic-update-slice_fusion.13.rows_ref, bf16[2048,2048]{1,0:T(8,128)(2,1)} %constant_dynamic-update-slice_fusion.2.upstream_ref, bf16[2048,1024]{1,0:T(8,128)(2,1)} %all-gather.10.cloned.1.call-done.both_ref.c_ref, ...), custom_call_target="tpu_custom_call" | custom-call | flops 12884901888 | bytes 23068672 | tf_op jit(solution)/shard_map/pallas_call | solution.py:198
  316.4 9.1 %convolution_convert_fusion.8 = bf16[512,2048]{1,0:T(8,128)(2,1)} fusion(bf16[2048,512]{1,0:T(8,128)(2,1)S(1)} %get-tuple-element.133.a_ref, bf16[2048,2048]{1,0:T(8,128)(2,1)} %constant_dynamic-update-slice_fusion.2.upstream_ref), kind=kOutput, calls=%fused_computation.18 | convolution fusion | flops 4296015872 | bytes 12582912 | tf_op jit(solution)/shard_map/dot_general | solution.py:33
  326.9 14.0 %convolution_convert_fusion.5 = bf16[2048,1024]{1,0:T(8,128)(2,1)} fusion(bf16[2048,2048]{1,0:T(8,128)(2,1)} %constant_dynamic-update-slice_fusion.13.rows_ref, bf16[2048,1024]{1,0:T(8,128)(2,1)} %get-tuple-element.132.a_ref), kind=kOutput, calls=%fused_computation.10 | convolution fusion | flops 8592031744 | bytes 16777216 | tf_op jit(solution)/shard_map/dot_general | solution.py:33
  341.4 17.8 %all-gather.12.cloned.1.call-done.both_ref.e_ref = bf16[2048,1024]{1,0:T(8,128)(2,1)} async-done(((bf16[512,1024]{1,0:T(8,128)(2,1)}), bf16[2048,1024]{1,0:T(8,128)(2,1)}) %all-gather.12.cloned.1.call-update) | async-done | bytes 4194320 | tf_op jit(solution)/shard_map/all_gather | solution.py:156
  360.9 18.9 %shard_map.400 = (bf16[2048,512]{1,0:T(8,128)(2,1)S(1)}, bf16[2048,1024]{1,0:T(8,128)(2,1)}) custom-call(bf16[2048,2048]{1,0:T(8,128)(2,1)} %constant_dynamic-update-slice_fusion.13.rows_ref, bf16[2048,2048]{1,0:T(8,128)(2,1)} %constant_dynamic-update-slice_fusion.2.upstream_ref, bf16[2048,1024]{1,0:T(8,128)(2,1)} %all-gather.12.cloned.1.call-done.both_ref.e_ref, ...), custom_call_target="tpu_custom_call" | custom-call | flops 12884901888 | bytes 23068672 | tf_op jit(solution)/shard_map/pallas_call | solution.py:198
  379.8 14.6 %shard_map.401 = bf16[1024,2048]{1,0:T(8,128)(2,1)} custom-call(bf16[2048,1024]{1,0:T(8,128)(2,1)} %get-tuple-element.132.a_ref, bf16[2048,1024]{1,0:T(8,128)(2,1)} %get-tuple-element.140.b_ref, bf16[2048,1024]{1,0:T(8,128)(2,1)} %all-gather.10.cloned.1.call-done.both_ref.c_ref, bf16[2048,1024]{1,0:T(8,128)(2,1)} %all-gather.12.cloned.1.call-done.both_ref.e_ref), custom_call_target="tpu_custom_call" | custom-call | flops 8589934592 | bytes 16777216 | tf_op jit(solution)/shard_map/pallas_call | solution.py:234
  395.1 13.3 %shard_map.402 = bf16[1024,2048]{1,0:T(8,128)(2,1)S(1)} custom-call(bf16[2048,1024]{1,0:T(8,128)(2,1)} %get-tuple-element.132.a_ref, bf16[2048,1024]{1,0:T(8,128)(2,1)} %get-tuple-element.140.b_ref, bf16[2048,1024]{1,0:T(8,128)(2,1)} %all-gather.10.cloned.1.call-done.both_ref.c_ref, bf16[2048,1024]{1,0:T(8,128)(2,1)} %all-gather.12.cloned.1.call-done.both_ref.e_ref), custom_call_target="tpu_custom_call" | custom-call | flops 8589934592 | bytes 16777216 | tf_op jit(solution)/shard_map/pallas_call | solution.py:234
  410.5 12.7 %convolution_convert_fusion.4 = bf16[2048,1024]{1,0:T(8,128)(2,1)} fusion(bf16[2048,2048]{1,0:T(8,128)(2,1)} %constant_dynamic-update-slice_fusion.13.rows_ref, bf16[2048,1024]{1,0:T(8,128)(2,1)S(1)} %copy-done.69), kind=kOutput, calls=%fused_computation.9 | convolution fusion | flops 8592031744 | bytes 16777216 | tf_op jit(solution)/shard_map/dot_general | solution.py:33
  427.9 8.3 %shard_map.404 = bf16[1024,2048]{1,0:T(8,128)(2,1)} custom-call(bf16[2048,512]{1,0:T(8,128)(2,1)S(1)} %copy-done.18, bf16[2048,512]{1,0:T(8,128)(2,1)S(1)} %get-tuple-element.143.b_ref, bf16[512,2048]{1,0:T(8,128)(2,1)} %bitcast.94, bf16[512,2048]{1,0:T(8,128)(2,1)} %all-gather.14.cloned.1.call-done.down_ref.e_ref), custom_call_target="tpu_custom_call" | custom-call | flops 4294967296 | bytes 10485760 | tf_op jit(solution)/shard_map/pallas_call | solution.py:234
  436.2 8.6 %shard_map.403 = bf16[1024,2048]{1,0:T(8,128)(2,1)} custom-call(bf16[2048,512]{1,0:T(8,128)(2,1)S(1)} %copy-done.18, bf16[2048,512]{1,0:T(8,128)(2,1)S(1)} %get-tuple-element.143.b_ref, bf16[512,2048]{1,0:T(8,128)(2,1)} %bitcast.95, bf16[512,2048]{1,0:T(8,128)(2,1)} %all-gather.14.cloned.1.call-done.down_ref.e_ref), custom_call_target="tpu_custom_call" | custom-call | flops 4294967296 | bytes 10485760 | tf_op jit(solution)/shard_map/pallas_call | solution.py:234
  450.0 9.2 %convolution_convert_fusion.7 = bf16[512,2048]{1,0:T(8,128)(2,1)} fusion(bf16[2048,512]{1,0:T(8,128)(2,1)S(1)} %get-tuple-element.143.b_ref, bf16[2048,2048]{1,0:T(8,128)(2,1)} %constant_dynamic-update-slice_fusion.2.upstream_ref), kind=kOutput, calls=%fused_computation.17 | convolution fusion | flops 4296015872 | bytes 12582912 | tf_op jit(solution)/shard_map/dot_general | solution.py:33
  459.2 14.8 %collective-permute-done.40 = bf16[256,2048]{1,0:T(8,128)(2,1)} collective-permute-done((bf16[256,2048]{1,0:T(8,128)(2,1)}, bf16[256,2048]{1,0:T(8,128)(2,1)}, u32[]{:S(2)}, u32[]{:S(2)}) %collective-permute-start.40) | collective-permute-done | bytes 1048608 | tf_op jit(solution)/shard_map/ppermute | solution.py:72
  485.3 6.7 convolution_convert_fusion.9
  505.8 6.6 all-to-all-done.3
  513.4 7.5 %all-to-all-start.4 = ((bf16[8,64,1024]{2,1,0:T(8,128)(2,1)}), bf16[8,64,1024]{2,1,0:T(8,128)(2,1)S(1)}, u32[]{:S(2)}, u32[]{:S(2)}) async-start(bf16[8,64,1024]{2,1,0:T(8,128)(2,1)} %bitcast.116), calls=%async_computation.7 | async-start | bytes 2097152 | tf_op jit(solution)/shard_map/all_to_all | solution.py:117
  546.3 9.3 %convolution_convert_fusion.6 = bf16[2048,768]{1,0:T(8,128)(2,1)} fusion(bf16[2048,768]{1,0:T(8,128)(2,1)S(1)} %pad_maximum_fusion, bf16[2048,2048]{1,0:T(8,128)(2,1)S(1)} %bitcast.97, f32[2048]{0:T(1024)S(1)} %copy-done.57, f32[2048]{0:T(1024)S(1)} %copy-done.59), kind=kOutput, calls=%fused_computation.11 | convolution fusion | flops 6460801024 | bytes 14696448 | tf_op jit(solution)/shard_map/dot_general | solution.py:33
  555.6 13.5 %reduce-scatter.10.cloned.1.call-done = bf16[512,1024]{1,0:T(8,128)(2,1)} async-done(((bf16[2048,1024]{1,0:T(8,128)(2,1)}), bf16[512,1024]{1,0:T(8,128)(2,1)}) %reduce-scatter.10.cloned.1.call-update) | async-done | bytes 1048592 | tf_op jit(solution)/shard_map/reduce_scatter | solution.py:160
  580.6 6.2 pad_add_fusion.3
  599.7 12.3 %collective-permute-done.52 = bf16[256,2048]{1,0:T(8,128)(2,1)} collective-permute-done((bf16[256,2048]{1,0:T(8,128)(2,1)}, bf16[256,2048]{1,0:T(8,128)(2,1)}, u32[]{:S(2)}, u32[]{:S(2)}) %collective-permute-start.52) | collective-permute-done | bytes 1048608 | tf_op jit(solution)/shard_map/ppermute | solution.py:72
  623.3 11.9 %collective-permute-done.54 = bf16[128,2048]{1,0:T(8,128)(2,1)} collective-permute-done((bf16[128,2048]{1,0:T(8,128)(2,1)}, bf16[128,2048]{1,0:T(8,128)(2,1)}, u32[]{:S(2)}, u32[]{:S(2)}) %collective-permute-start.54) | collective-permute-done | bytes 524320 | tf_op jit(solution)/shard_map/ppermute | solution.py:72
  635.2 5.9 pad_add_fusion.1
  684.3 12.9 %collective-permute-done.58 = bf16[64,2048]{1,0:T(8,128)(2,1)} collective-permute-done((bf16[64,2048]{1,0:T(8,128)(2,1)}, bf16[64,2048]{1,0:T(8,128)(2,1)}, u32[]{:S(2)}, u32[]{:S(2)}) %collective-permute-start.58) | collective-permute-done | bytes 262176 | tf_op jit(solution)/shard_map/ppermute | solution.py:165
  709.8 6.3 multiply_subtract_fusion
  (439 shorter events, 304.2 us)
Async XLA Ops:
  7.2 81.0 %all-gather.6.cloned.1.call-start = ((), (), s32[]{:S(2)}) async-start(), calls=%async_computation.12 | async-start | bytes 4259840 | tf_op jit(solution)/shard_map/all_gather | solution.py:156
  34.9 53.4 %all-to-all-start.1 = ((bf16[8,64,2048]{2,1,0:T(8,128)(2,1)}), bf16[8,64,2048]{2,1,0:T(8,128)(2,1)S(1)}, u32[]{:S(2)}, u32[]{:S(2)}) async-start(bf16[8,64,2048]{2,1,0:T(8,128)(2,1)} %copy-done.9), calls=%async_computation.1 | async-start | bytes 4194304 | tf_op jit(solution)/shard_map/all_to_all | solution.py:117
  39.8 127.6 %all-gather.8.cloned.1.call-start = ((), (), s32[]{:S(2)}) async-start(), calls=%async_computation.13 | async-start | bytes 3932160 | tf_op jit(solution)/shard_map/all_gather | solution.py:156
  40.1 47.2 %collective-permute-start.1 = (bf16[256,2048]{1,0:T(8,128)(2,1)S(1)}, bf16[256,2048]{1,0:T(8,128)(2,1)S(1)}, u32[]{:S(2)}, u32[]{:S(2)}) collective-permute-start(bf16[256,2048]{1,0:T(8,128)(2,1)S(1)} %copy-done.25), channel_id=1, source_target_pairs={{0,4},{4,0},{1,5},{5,1},{2,6},{6,2},{3,7},{7,3},{8,12},{12,8},{9,1... | collective-permute-start | bytes 3145736 | tf_op jit(solution)/shard_map/ppermute | solution.py:72
  41.7 46.6 %collective-permute-start = (bf16[256,2048]{1,0:T(8,128)(2,1)S(1)}, bf16[256,2048]{1,0:T(8,128)(2,1)}, u32[]{:S(2)}, u32[]{:S(2)}) collective-permute-start(bf16[256,2048]{1,0:T(8,128)(2,1)S(1)} %copy-done.25), channel_id=1, source_target_pairs={{0,2},{2,0},{1,3},{3,1},{4,6},{6,4},{5,7},{7,5},{8,10},{10,8},{9,1... | collective-permute-start | bytes 3145736 | tf_op jit(solution)/shard_map/ppermute | solution.py:72
  88.3 209.2 %all-gather.10.cloned.1.call-start = ((), (), s32[]{:S(2)}) async-start(), calls=%async_computation.14 | async-start | bytes 5242880 | tf_op jit(solution)/shard_map/all_gather | solution.py:156
  89.9 251.6 %all-gather.14.cloned.1.call-start = ((), (), s32[]{:S(2)}) async-start(), calls=%async_computation.16 | async-start | bytes 2621440 | tf_op jit(solution)/shard_map/all_gather | solution.py:156
  115.5 47.5 %collective-permute-start.24 = (bf16[256,2048]{1,0:T(8,128)(2,1)S(1)}, bf16[256,2048]{1,0:T(8,128)(2,1)}, u32[]{:S(2)}, u32[]{:S(2)}) collective-permute-start(bf16[256,2048]{1,0:T(8,128)(2,1)S(1)} %bitcast.107), channel_id=1, source_target_pairs={{0,1},{1,0},{2,3},{3,2},{4,5},{5,4},{6,7},{7,6},{8,9},{9,8},{10,11... | collective-permute-start | bytes 3145736 | tf_op jit(solution)/shard_map/ppermute | solution.py:72
  115.9 28.1 %collective-permute-start.21 = (bf16[256,2048]{1,0:T(8,128)(2,1)S(1)}, bf16[256,2048]{1,0:T(8,128)(2,1)S(1)}, u32[]{:S(2)}, u32[]{:S(2)}) collective-permute-start(bf16[256,2048]{1,0:T(8,128)(2,1)S(1)} %bitcast.108), channel_id=1, source_target_pairs={{0,4},{4,0},{1,5},{5,1},{2,6},{6,2},{3,7},{7,3},{8,12},{12,8},{9,1... | collective-permute-start | bytes 3145736 | tf_op jit(solution)/shard_map/ppermute | solution.py:72
  178.1 27.0 %collective-permute-start.12 = (bf16[256,2048]{1,0:T(8,128)(2,1)}, bf16[256,2048]{1,0:T(8,128)(2,1)S(1)}, u32[]{:S(2)}, u32[]{:S(2)}) collective-permute-start(bf16[256,2048]{1,0:T(8,128)(2,1)} %param.24), channel_id=1, source_target_pairs={{0,2},{2,0},{1,3},{3,1},{4,6},{6,4},{5,7},{7,5},{8,10},{10,8},{9,1... | collective-permute-start | bytes 3145736 | tf_op jit(solution)/shard_map/ppermute | solution.py:72
  182.2 48.0 %collective-permute-start.16 = (bf16[256,2048]{1,0:T(8,128)(2,1)}, bf16[256,2048]{1,0:T(8,128)(2,1)}, u32[]{:S(2)}, u32[]{:S(2)}) collective-permute-start(bf16[256,2048]{1,0:T(8,128)(2,1)} %param.24), channel_id=1, source_target_pairs={{0,1},{1,0},{2,3},{3,2},{4,5},{5,4},{6,7},{7,6},{8,9},{9,8},{10,11... | collective-permute-start | bytes 3145736 | tf_op jit(solution)/shard_map/ppermute | solution.py:72
  209.6 26.3 %all-to-all-start.2 = ((bf16[8,256,256]{1,2,0:T(8,128)(2,1)}), bf16[8,256,256]{1,2,0:T(8,128)(2,1)S(1)}, u32[]{:S(2)}, u32[]{:S(2)}) async-start(bf16[8,256,256]{1,2,0:T(8,128)(2,1)} %copy.59), calls=%async_computation.2 | async-start | bytes 2097152 | tf_op jit(solution)/shard_map/all_to_all | solution.py:117
  214.3 144.9 %all-gather.12.cloned.1.call-start = ((), (), s32[]{:S(2)}) async-start(), calls=%async_computation.15 | async-start | bytes 5242880 | tf_op jit(solution)/shard_map/all_gather | solution.py:156
  243.4 28.5 %collective-permute-start.28 = (bf16[256,2048]{1,0:T(8,128)(2,1)S(1)}, bf16[256,2048]{1,0:T(8,128)(2,1)S(1)}, u32[]{:S(2)}, u32[]{:S(2)}) collective-permute-start(bf16[256,2048]{1,0:T(8,128)(2,1)S(1)} %get-tuple-element.222), channel_id=1, source_target_pairs={{0,2},{2,0},{1,3},{3,1},{4,6},{6,4},{5,7},{7,5},{8,10},{10,8},{9,1... | collective-permute-start | bytes 3145736 | tf_op jit(solution)/shard_map/ppermute | solution.py:72
  273.4 232.4 %reduce-scatter.6.cloned.1.call-start = ((), (), s32[]{:S(2)}) async-start(), calls=%async_computation.17 | async-start | bytes 2621440 | tf_op jit(solution)/shard_map/reduce_scatter | solution.py:160
  340.9 164.9 %reduce-scatter.8.cloned.1.call-start = ((), (), s32[]{:S(2)}) async-start(), calls=%async_computation.18 | async-start | bytes 5242880 | tf_op jit(solution)/shard_map/reduce_scatter | solution.py:160
  394.9 174.2 %reduce-scatter.10.cloned.1.call-start = ((), (), s32[]{:S(2)}) async-start(), calls=%async_computation.19 | async-start | bytes 5242880 | tf_op jit(solution)/shard_map/reduce_scatter | solution.py:160
  503.2 34.1 %collective-permute-start.45 = (bf16[128,2048]{1,0:T(8,128)(2,1)}, bf16[128,2048]{1,0:T(8,128)(2,1)}, u32[]{:S(2)}, u32[]{:S(2)}) collective-permute-start(bf16[128,2048]{1,0:T(8,128)(2,1)} %get-tuple-element.260), channel_id=1, source_target_pairs={{0,2},{2,0},{1,3},{3,1},{4,6},{6,4},{5,7},{7,5},{8,10},{10,8},{9,1... | collective-permute-start | bytes 1572872 | tf_op jit(solution)/shard_map/ppermute | solution.py:72
  504.6 32.7 %collective-permute-start.44 = (bf16[128,2048]{1,0:T(8,128)(2,1)}, bf16[128,2048]{1,0:T(8,128)(2,1)}, u32[]{:S(2)}, u32[]{:S(2)}) collective-permute-start(bf16[128,2048]{1,0:T(8,128)(2,1)} %get-tuple-element.261), channel_id=1, source_target_pairs={{0,4},{4,0},{1,5},{5,1},{2,6},{6,2},{3,7},{7,3},{8,12},{12,8},{9,1... | collective-permute-start | bytes 1572872 | tf_op jit(solution)/shard_map/ppermute | solution.py:72
  513.4 55.7 %all-to-all-start.4 = ((bf16[8,64,1024]{2,1,0:T(8,128)(2,1)}), bf16[8,64,1024]{2,1,0:T(8,128)(2,1)S(1)}, u32[]{:S(2)}, u32[]{:S(2)}) async-start(bf16[8,64,1024]{2,1,0:T(8,128)(2,1)} %bitcast.116), calls=%async_computation.7 | async-start | bytes 2097152 | tf_op jit(solution)/shard_map/all_to_all | solution.py:117
  520.9 123.8 %reduce-scatter.12.cloned.1.call-start = ((), (), s32[]{:S(2)}) async-start(), calls=%async_computation.20 | async-start | bytes 3932160 | tf_op jit(solution)/shard_map/reduce_scatter | solution.py:160
  533.7 35.3 %collective-permute-start.47 = (bf16[128,2048]{1,0:T(8,128)(2,1)}, bf16[128,2048]{1,0:T(8,128)(2,1)}, u32[]{:S(2)}, u32[]{:S(2)}) collective-permute-start(bf16[128,2048]{1,0:T(8,128)(2,1)} %get-tuple-element.258), channel_id=1, source_target_pairs={{0,2},{2,0},{1,3},{3,1},{4,6},{6,4},{5,7},{7,5},{8,10},{10,8},{9,1... | collective-permute-start | bytes 1572872 | tf_op jit(solution)/shard_map/ppermute | solution.py:72
  535.1 34.0 %collective-permute-start.46 = (bf16[128,2048]{1,0:T(8,128)(2,1)}, bf16[128,2048]{1,0:T(8,128)(2,1)}, u32[]{:S(2)}, u32[]{:S(2)}) collective-permute-start(bf16[128,2048]{1,0:T(8,128)(2,1)} %get-tuple-element.259), channel_id=1, source_target_pairs={{0,4},{4,0},{1,5},{5,1},{2,6},{6,2},{3,7},{7,3},{8,12},{12,8},{9,1... | collective-permute-start | bytes 1572872 | tf_op jit(solution)/shard_map/ppermute | solution.py:72
  579.3 33.3 %collective-permute-start.50 = (bf16[1024,2048]{1,0:T(8,128)(2,1)}, bf16[1024,2048]{1,0:T(8,128)(2,1)}, u32[]{:S(2)}, u32[]{:S(2)}) collective-permute-start(bf16[1024,2048]{1,0:T(8,128)(2,1)} %convolution_convert_fusion.3), channel_id=1, source_target_pairs={{0,1},{1,0},{2,3},{3,2},{4,5},{5,4},{6,7},{7,6},{8,9},{9,8},{10,11... | collective-permute-start | bytes 12582920 | tf_op jit(solution)/shard_map/ppermute | solution.py:72
  589.7 33.6 %all-to-all-start.5 = ((bf16[8,64,1024]{2,1,0:T(8,128)(2,1)}), bf16[8,64,1024]{2,1,0:T(8,128)(2,1)S(1)}, u32[]{:S(2)}, u32[]{:S(2)}) async-start(bf16[8,64,1024]{2,1,0:T(8,128)(2,1)} %bitcast.115), calls=%async_computation.8 | async-start | bytes 2097152 | tf_op jit(solution)/shard_map/all_to_all | solution.py:117
  593.7 116.1 %reduce-scatter.14.cloned.1.call-start = ((), (), s32[]{:S(2)}) async-start(), calls=%async_computation.21 | async-start | bytes 2621440 | tf_op jit(solution)/shard_map/reduce_scatter | solution.py:160
  641.1 35.1 %collective-permute-start.56 = (bf16[256,2048]{1,0:T(8,128)(2,1)}, bf16[256,2048]{1,0:T(8,128)(2,1)}, u32[]{:S(2)}, u32[]{:S(2)}) collective-permute-start(bf16[256,2048]{1,0:T(8,128)(2,1)} %get-tuple-element.227), channel_id=1, source_target_pairs={{0,4},{4,0},{1,5},{5,1},{2,6},{6,2},{3,7},{7,3},{8,12},{12,8},{9,1... | collective-permute-start | bytes 3145736 | tf_op jit(solution)/shard_map/ppermute | solution.py:72
  641.5 34.7 %collective-permute-start.55 = (bf16[256,2048]{1,0:T(8,128)(2,1)}, bf16[256,2048]{1,0:T(8,128)(2,1)}, u32[]{:S(2)}, u32[]{:S(2)}) collective-permute-start(bf16[256,2048]{1,0:T(8,128)(2,1)} %get-tuple-element.228), channel_id=1, source_target_pairs={{0,2},{2,0},{1,3},{3,1},{4,6},{6,4},{5,7},{7,5},{8,10},{10,8},{9,1... | collective-permute-start | bytes 3145736 | tf_op jit(solution)/shard_map/ppermute | solution.py:72
  644.7 31.5 %all-to-all-start.6 = ((bf16[8,64,768]{2,1,0:T(8,128)(2,1)}), bf16[8,64,768]{2,1,0:T(8,128)(2,1)S(1)}, u32[]{:S(2)}, u32[]{:S(2)}) async-start(bf16[8,64,768]{2,1,0:T(8,128)(2,1)} %bitcast.118), calls=%async_computation.10 | async-start | bytes 1572864 | tf_op jit(solution)/shard_map/all_to_all | solution.py:117
  652.3 32.0 %collective-permute-start.59 = (bf16[64,2048]{1,0:T(8,128)(2,1)}, bf16[64,2048]{1,0:T(8,128)(2,1)S(1)}, u32[]{:S(2)}, u32[]{:S(2)}) collective-permute-start(bf16[64,2048]{1,0:T(8,128)(2,1)} %get-tuple-element.252), channel_id=1, source_target_pairs={{24,0},{0,8},{8,16},{16,24},{25,1},{1,9},{9,17},{17,25},{26,2},{2,... | collective-permute-start | bytes 786440 | tf_op jit(solution)/shard_map/ppermute | solution.py:165
  654.1 43.1 %collective-permute-start.58 = (bf16[64,2048]{1,0:T(8,128)(2,1)}, bf16[64,2048]{1,0:T(8,128)(2,1)}, u32[]{:S(2)}, u32[]{:S(2)}) collective-permute-start(bf16[64,2048]{1,0:T(8,128)(2,1)} %get-tuple-element.253), channel_id=1, source_target_pairs={{16,0},{24,8},{0,16},{8,24},{17,1},{25,9},{1,17},{9,25},{18,2},{26... | collective-permute-start | bytes 786440 | tf_op jit(solution)/shard_map/ppermute | solution.py:165
  656.8 42.2 %collective-permute-start.57 = (bf16[64,2048]{1,0:T(8,128)(2,1)}, bf16[64,2048]{1,0:T(8,128)(2,1)}, u32[]{:S(2)}, u32[]{:S(2)}) collective-permute-start(bf16[64,2048]{1,0:T(8,128)(2,1)} %get-tuple-element.254), channel_id=1, source_target_pairs={{8,0},{16,8},{24,16},{0,24},{9,1},{17,9},{25,17},{1,25},{10,2},{18... | collective-permute-start | bytes 786440 | tf_op jit(solution)/shard_map/ppermute | solution.py:165
  (121 other events, 1287.8 us)
Sparse Core Ops, SparseCore 0:
  14.0 66.4 all-gather.5
  88.4 61.3 all-gather.7
  151.9 79.3 all-gather.9
  233.3 45.0 all-gather.13
  280.4 78.8 all-gather.11
  362.0 42.5 reduce-scatter.5
  406.9 78.5 reduce-scatter.7
  492.2 76.8 reduce-scatter.9
  571.5 60.4 reduce-scatter.11
  634.2 63.3 reduce-scatter.13
